TPU v7x, 128 devices: a whole 4x4x4 slice. The times are simulated.
128 devices in a mesh: dp: 8 (over z, core), head: 16 (over y, x).
Axes of the slice: x: 4, y: 4, z: 4, core: 2. Of those that a mesh axis runs over, the one named last changes fastest.
Arguments:
- residual_patch_matrix: bfloat16 [16384, 2048], P(('dp', 'head')), may hold values from -6 to 6
- transfer_tallies: int32 [8, 8], P('dp'), may hold values from 1 to 3, as said below
- picture_membership: int32 [8, 16], P('dp'), may hold values from 0 to 3, never falling along the last dimension, each value on 1 to 8 neighbouring positions
- premix_rescale_vector: float32 [2048], replicated, may hold values from 0.1 to 1.9
- triple_projection_matrix: bfloat16 [2048, 6144], P(None, 'head'), may hold values from -0.125 to 0.125
- per_head_sharpness: float32 [16], P('head'), may hold values from 2 to 900
- headmerge_projection_matrix: bfloat16 [2048, 2048], replicated, may hold values from -0.125 to 0.125
- prefeed_rescale_vector: float32 [2048], replicated, may hold values from 0.1 to 1.9
- feedforward_expand_matrix: bfloat16 [2048, 8192], P(None, 'head'), may hold values from -0.125 to 0.125
- feedforward_contract_matrix: bfloat16 [8192, 2048], P('head'), may hold values from -0.0625 to 0.0625
Outputs:
- block_out: bfloat16 [24576, 2048], P(('dp', 'head'))
Inputs may be any that keep to these rules, and one draw needn't show every extreme that they name: transfer_tallies[s, d] is the number of units every device of group s sends to group d; each row sums to 16; every row's largest entry is 3, and some destination group receives 3 units from every source group. `picture_membership`: ids never fall along a row; each id covers 1 to 8 consecutive units, one exactly 8.
All inputs are finite; a program needn't handle non-finite values.
Results may differ from a plain program's by a relative error of at most 0.014.
The roundings to bfloat16 on the way count: a program that leaves them out, or rounds other values in their place, can miss the bound.
Values may be sent and summed in bfloat16 or wider, within the bound.
No kernel may reach another device: no remote copies, remote signals or barrier semaphores. Data moves between devices by JAX's collectives and lax.ppermute only.
A program may use at most 128 MiB of HBM per device.

v0:
```python
import functools

import jax
import jax.numpy as jnp
from jax import lax
from jax.experimental import pallas as pl
from jax.experimental.pallas import tpu as pltpu
from jax.sharding import Mesh
from jax.sharding import PartitionSpec as P

HEAD_DIM = 128
UNIT = 8
N_DP = 8
SIDE = 4
CAP = 24
EPS = 1e-06
DP = ("z", "c")
BF16 = jnp.bfloat16
F32 = jnp.float32
VMEM = pl.BlockSpec(memory_space=pltpu.VMEM)
SMEM = pl.BlockSpec(memory_space=pltpu.SMEM)
ANY = pl.BlockSpec(memory_space=pl.ANY)


def ring(size, step):
    return [(i, (i + step) % size) for i in range(size)]


def twin_ring():
    down = [(y, (y - 1) % SIDE) for y in range(SIDE)]
    up = [(SIDE + y, SIDE + (y + 1) % SIDE) for y in range(SIDE)]
    return down + up


def dot(a, b):
    return jnp.dot(a, b, preferred_element_type=F32)


def shape(dims, dtype=BF16):
    return jax.ShapeDtypeStruct(dims, dtype)


def call(kernel, outs, ins, scratch=(), vmem=100, flops=0, moved=0):
    return pl.pallas_call(
        kernel,
        out_shape=outs,
        in_specs=ins,
        out_specs=[VMEM] * len(outs),
        scratch_shapes=list(scratch),
        compiler_params=pltpu.CompilerParams(vmem_limit_bytes=vmem * 2**20 // 2),
        cost_estimate=pl.CostEstimate(flops=flops, bytes_accessed=moved, transcendentals=0),
    )


def placement(count_ref, y):
    count = [count_ref[0, d] for d in range(N_DP)]
    offset, start, running = [], [], jnp.int32(0)
    for d in range(N_DP):
        offset.append(running)
        running = running + count[d]
        rank = jnp.int32(0)
        for e in range(N_DP):
            if e != d:
                ahead = count[e] >= count[d] if e < d else count[e] > count[d]
                rank = rank + ahead.astype(jnp.int32)
        place = jnp.where(rank < SIDE, 4 * rank, 4 * (7 - rank) + 4 - count[d])
        start.append((place - 4 * y + 16) & 15)
    return count, offset, start


def spread(unit, count, offset, values):
    out = jnp.zeros_like(unit)
    for d in range(N_DP):
        inside = (unit >= offset[d]) & (unit < offset[d] + count[d])
        out = out + jnp.where(inside, values[d], 0)
    return out


def pick_kernel(where_ref, count_ref, tokens_ref, *outs):
    count, offset, start = placement(count_ref, where_ref[2])
    row = lax.broadcasted_iota(jnp.int32, (1, 128), 1)
    unit = row >> 3
    place = unit + spread(unit, count, offset, [s - o for s, o in zip(start, offset)])
    target = place * UNIT + (row & 7)
    pick = (target == lax.broadcasted_iota(jnp.int32, (128, 128), 0)).astype(F32).astype(BF16)
    for n in range(4):
        cols = pl.ds(512 * n, 512)
        picked = dot(pick, tokens_ref[:, cols]).astype(BF16)
        for k in range(SIDE):
            outs[k][:, cols] = picked[32 * k : 32 * k + 32]


def slice_kernel(where_ref, w1_ref, w2_ref, out_ref, sem):
    z = where_ref[0]
    copies = [
        pltpu.make_async_copy(
            w1_ref.at[pl.ds(pl.multiple_of(z * 512, 512), 512)], out_ref.at[pl.ds(0, 512)], sem.at[0]
        )
    ]
    for q in range(4):
        copies.append(
            pltpu.make_async_copy(
                w2_ref.at[pl.ds(pl.multiple_of(z * 128, 128), 128), pl.ds(512 * q, 512)],
                out_ref.at[pl.ds(512 + 128 * q, 128)],
                sem.at[1 + q],
            )
        )
    for copy in copies:
        copy.start()
    for copy in copies:
        copy.wait()


def half_kernel(where_ref, got_ref, out_ref):
    c = where_ref[1]
    out_ref[:256] = got_ref[pl.ds(pl.multiple_of(c * 256, 256), 256)]
    for q in range(4):
        out_ref[256 + 64 * q : 320 + 64 * q] = got_ref[
            pl.ds(pl.multiple_of(512 + 128 * q + 64 * c, 64), 64)
        ]


def pack_kernel(sharp_ref, wqkv_ref, out_ref, sem):
    copy = pltpu.make_async_copy(wqkv_ref, out_ref.at[pl.ds(0, 2048)], sem)
    copy.start()
    value = jnp.full((16, 384), sharp_ref[0], F32)
    high = value.astype(BF16).astype(F32)
    mid = (value - high).astype(BF16).astype(F32)
    low = value - high - mid
    lane = lax.broadcasted_iota(jnp.int32, (16, 384), 1)
    terms = jnp.where(lane == 0, high, jnp.where(lane == 1, mid, jnp.where(lane == 2, low, 0.0)))
    out_ref[2048:] = terms.astype(BF16)
    copy.wait()


def join_kernel(near_ref, far_ref, out_ref):
    out_ref[:1024] = near_ref[...]
    out_ref[1024:] = far_ref[...]


def far_kernel(where_ref, got_ref, out_ref):
    out_ref[:1024] = got_ref[pl.ds(pl.multiple_of(where_ref[1] * 1024, 1024), 1024)]
    out_ref[1024:] = got_ref[2048:]


def unit_norm(values):
    mean_square = jnp.mean(values * values, axis=-1, keepdims=True)
    return (values * lax.rsqrt(mean_square + EPS) * HEAD_DIM ** (-0.5)).astype(BF16)


def key_of_place(count_ref, member_ref, y):
    count, offset, start = placement(count_ref, y)
    row = (lax.broadcasted_iota(jnp.int32, (1, 512), 1) >> 3) & 3
    col = (lax.broadcasted_iota(jnp.int32, (512, 1), 0) >> 3) & 3
    key_row = jnp.zeros((1, 512), jnp.int32)
    key_col = jnp.zeros((512, 1), jnp.int32)
    for p in range(4):
        key = jnp.int32(0)
        for d in range(N_DP):
            inside = (start[d] <= p) & (p < start[d] + count[d])
            member = member_ref[0, jnp.where(inside, offset[d] + p - start[d], 0)]
            key = key + jnp.where(inside, d * 4 + member, 0)
        key_row = key_row + jnp.where(row == p, key, 0)
        key_col = key_col + jnp.where(col == p, key, 0)
    return key_col == key_row


def attend(raw, scale_row, allowed):
    q = unit_norm(raw[:, :128])
    k = unit_norm(raw[:, 128:256])
    v = raw[:, 256:].astype(BF16)
    score = lax.dot_general(q, k, (((1,), (1,)), ((), ())), preferred_element_type=F32)
    scale = jnp.sum(scale_row.astype(F32), axis=-1, keepdims=True)
    score = jnp.where(allowed, score * scale, -1e30)
    weights = jnp.exp(score - jnp.max(score, axis=-1, keepdims=True))
    p = (weights / jnp.sum(weights, axis=-1, keepdims=True)).astype(BF16)
    return dot(p, v).astype(BF16)


def norm_kernel(a0, a1, a2, a3, gain_ref, out_ref):
    for j, ref in enumerate((a0, a1, a2, a3)):
        values = ref[...].astype(F32)
        mean_square = jnp.mean(values * values, axis=-1, keepdims=True)
        out_ref[128 * j : 128 * j + 128] = (
            values * lax.rsqrt(mean_square + EPS) * gain_ref[...]
        ).astype(BF16)


def near_kernel(
    where_ref, count_ref, member_ref, xn, wq0, wq1, wq2, out_ref, w0, w1, w2, sem
):
    copies = [
        pltpu.make_async_copy(src, dst, sem.at[i])
        for i, (src, dst) in enumerate(((wq0, w0), (wq1, w1), (wq2, w2)))
    ]
    for copy in copies:
        copy.start()
    allowed = key_of_place(count_ref, member_ref, where_ref[2])
    for k, w in enumerate((w0, w1, w2)):
        copies[k].wait()
        raw = dot(xn[...], w[:2048])
        out_ref[:, 128 * k : 128 * k + 128] = attend(raw, w[2048:2049], allowed)


def far_attention_kernel(where_ref, count_ref, member_ref, xn, wqa, wqb, out_ref, w3, sem):
    c = where_ref[1]
    copies = [
        pltpu.make_async_copy(wqa, w3.at[c], sem.at[0]),
        pltpu.make_async_copy(wqb, w3.at[1 - c], sem.at[1]),
    ]
    for copy in copies:
        copy.start()
    allowed = key_of_place(count_ref, member_ref, where_ref[2])
    for copy in copies:
        copy.wait()
    raw = dot(xn[:, :1024], w3[0, :1024]) + dot(xn[:, 1024:], w3[1, :1024])
    out_ref[...] = attend(raw, w3[0, 1024:1025], allowed)


def merge_kernel(
    where_ref, a0, a1, a2, a3, o0, o1, o2, o3, f0, f1, f2, f3, gain_ref, wm, fed_ref, kept_ref,
    heads, total,
):
    c, y, x = where_ref[1], where_ref[2], where_ref[3]
    step = 1 - 2 * c
    source = [y, (y + step + 4) & 3, (y - step + 4) & 3, (y + 2) & 3]
    for m, (near, far) in enumerate(((o0, f0), (o1, f1), (o2, f2), (o3, f3))):
        for k in range(SIDE):
            head = source[k] * SIDE + ((x - m + 4) & 3)
            cols = pl.ds(pl.multiple_of(head * HEAD_DIM, HEAD_DIM), HEAD_DIM)
            for j in range(SIDE):
                theirs = slice(128 * ((j - m) % SIDE), 128 * ((j - m) % SIDE) + 128)
                block = far[theirs] if k == 3 else near[theirs, 128 * k : 128 * k + 128]
                heads[128 * j : 128 * j + 128, cols] = block
    squares = jnp.zeros((512, 1), F32)
    for n in range(4):
        cols = slice(512 * n, 512 * n + 512)
        part = dot(heads[...], wm[:, cols])
        arrived = jnp.concatenate([ref[:, cols] for ref in (a0, a1, a2, a3)], 0)
        part = part + arrived.astype(F32)
        squares = squares + jnp.sum(part * part, axis=-1, keepdims=True)
        total[:, cols] = part
    scale = lax.rsqrt(squares * (1.0 / 2048) + EPS)
    for n in range(4):
        cols = slice(512 * n, 512 * n + 512)
        fed_ref[:, cols] = (total[:, cols] * scale * gain_ref[:, cols]).astype(BF16)
    kept_ref[...] = total[:128]


def mlp_kernel(
    fed_ref, kept_ref, w1_ref, w2_ref, all_ref, own_ref, s1, s2, s3, w1, w2, hidden, sem
):
    copies = [
        [pltpu.make_async_copy(w1_ref, w1.at[0], sem.at[0])],
        [pltpu.make_async_copy(w2_ref, w2.at[pl.ds(0, 512)], sem.at[1])],
    ]
    for c in range(2):
        up, down = [], []
        for z in range(4):
            block = all_ref.at[2 * z + c]
            up.append(
                pltpu.make_async_copy(
                    block.at[pl.ds(0, 512)], w1.at[1 + c, pl.ds(512 * z, 512)], sem.at[2 + 2 * c]
                )
            )
            for q in range(4):
                down.append(
                    pltpu.make_async_copy(
                        block.at[pl.ds(512 + 128 * q, 128)],
                        w2.at[pl.ds(512 * (1 + c) + 128 * z, 128), pl.ds(512 * q, 512)],
                        sem.at[3 + 2 * c],
                    )
                )
        copies += [up, down]
    up, down = [], []
    for z in range(4):
        for c in range(2):
            block = all_ref.at[2 * z + c, pl.ds(1024, 512)]
            up.append(
                pltpu.make_async_copy(
                    block.at[pl.ds(0, 256)], w1.at[3, pl.ds(512 * z + 256 * c, 256)], sem.at[6]
                )
            )
            for q in range(4):
                down.append(
                    pltpu.make_async_copy(
                        block.at[pl.ds(256 + 64 * q, 64)],
                        w2.at[pl.ds(1536 + 128 * z + 64 * c, 64), pl.ds(512 * q, 512)],
                        sem.at[7],
                    )
                )
    copies += [up, down]
    for i in (0, 2, 4, 6, 1, 3, 5, 7):
        for copy in copies[i]:
            copy.start()
    for i in range(SIDE):
        for copy in copies[2 * i]:
            copy.wait()
        hidden[:, 512 * i : 512 * i + 512] = jax.nn.gelu(
            dot(fed_ref[...], w1[i]), approximate=True
        ).astype(BF16)
    for i in range(SIDE):
        for copy in copies[2 * i + 1]:
            copy.wait()
    for n in range(4):
        cols = slice(512 * n, 512 * n + 512)
        part = dot(hidden[...], w2[:, cols])
        own_ref[:, cols] = kept_ref[:, cols] + part[:128]
        for j, ref in enumerate((s1, s2, s3)):
            ref[:, cols] = part[128 * (j + 1) : 128 * (j + 2)].astype(BF16)


def sum_kernel(own_ref, r1, r2, r3, *outs):
    total = own_ref[...] + r1[...].astype(F32) + r2[...].astype(F32) + r3[...].astype(F32)
    total = total.astype(BF16)
    for k in range(SIDE):
        outs[k][...] = total[32 * k : 32 * k + 32]


def leave_kernel(where_ref, count_ref, h0, h1, h2, h3, stay_ref, cross_ref):
    z, c, y = where_ref[0], where_ref[1], where_ref[2]
    count, _, start = placement(count_ref, y)
    slot = lax.broadcasted_iota(jnp.int32, (192, 1), 0)
    block = slot // CAP
    inner = slot - block * CAP
    home = jnp.concatenate([h0[...], h1[...], h2[...], h3[...]], 0)
    target = jnp.full((192, 1), -1, jnp.int32)
    for d in range(N_DP):
        turn = ((d >> 1) - z + 4) & 3
        index = jnp.where((d & 1) == c, turn, 4 + turn)
        here = (block == index) & (inner < UNIT * count[d])
        target = jnp.where(here, UNIT * start[d] + inner, target)
    select = (target == lax.broadcasted_iota(jnp.int32, (192, 128), 1)).astype(F32).astype(BF16)
    moved = dot(select, home).astype(BF16).reshape(8, CAP, -1)
    stay_ref[...] = moved[:4]
    cross_ref[...] = moved[4:]


def pair_kernel(where_ref, stay_ref, cross_ref, *outs):
    c = where_ref[1]
    for m in range(SIDE):
        outs[m][c] = stay_ref[m]
        outs[m][1 - c] = cross_ref[m]


def order_kernel(where_ref, g0, g1, g2, g3, out_ref):
    for m, ref in enumerate((g0, g1, g2, g3)):
        out_ref[pl.ds(2 * ((where_ref[0] - m + 4) & 3), 2)] = ref[...]


def body(tokens, tallies, membership, gain1, wqkv, sharp, wmerge, gain2, w1, w2):
    z, c, y, x = (lax.axis_index(name) for name in ("z", "c", "y", "x"))
    where = jnp.stack([z, c, y, x]).astype(jnp.int32)
    gain1 = gain1[None]
    gain2 = gain2[None]
    cy = ("c", "y")

    blocks = call(pick_kernel, [shape((32, 2048))] * 4, [SMEM, SMEM, VMEM])(where, tallies, tokens)
    came = [blocks[0]] + [lax.ppermute(blocks[k], "y", ring(SIDE, k)) for k in (1, 2, 3)]
    w1_later, w2_later, _ = lax.optimization_barrier((w1, w2, blocks[1]))
    [mlp_slice] = call(
        slice_kernel,
        [shape((1024, 512))],
        [SMEM, ANY, ANY],
        [pltpu.SemaphoreType.DMA((5,))],
    )(where, w1_later, w2_later)
    near = lax.ppermute(mlp_slice, cy, twin_ring())
    [near_half] = call(half_kernel, [shape((512, 512))], [SMEM, VMEM])(where, near)
    far = lax.ppermute(near_half, cy, twin_ring())
    [both] = call(join_kernel, [shape((1536, 512))], [VMEM] * 2)(near, far)

    column = jnp.concatenate(came, 0)
    arrived = [column] + [lax.ppermute(column, "x", ring(SIDE, m)) for m in (1, 2, 3)]
    [packed] = call(
        pack_kernel,
        [shape((2064, 384))],
        [SMEM, ANY],
        [pltpu.SemaphoreType.DMA],
    )(sharp, lax.optimization_barrier((wqkv, column))[0])
    qkv_near = lax.ppermute(packed, cy, twin_ring())
    both_all = lax.all_gather(lax.optimization_barrier((both, column))[0], DP, axis=0, tiled=False)

    [normed] = call(norm_kernel, [shape((512, 2048))], [VMEM] * 5)(*arrived, gain1)
    qkv_near, normed = lax.optimization_barrier((qkv_near, normed))
    qkv_near2 = lax.ppermute(qkv_near, "c", ring(2, 1))
    [qkv_half] = call(far_kernel, [shape((1040, 384))], [SMEM, VMEM])(where, qkv_near)
    qkv_far = lax.ppermute(qkv_half, cy, twin_ring())
    qkv_far2 = lax.ppermute(qkv_far, "c", ring(2, 1))

    [mine] = call(
        near_kernel,
        [shape((512, 384))],
        [SMEM] * 3 + [VMEM] + [ANY] * 3,
        [pltpu.VMEM((2064, 384), BF16)] * 3 + [pltpu.SemaphoreType.DMA((3,))],
        flops=3 * 10**9,
        moved=10 * 2**20,
    )(where, tallies, membership, normed, packed, qkv_near, qkv_near2)
    [mine_far] = call(
        far_attention_kernel,
        [shape((512, 128))],
        [SMEM] * 3 + [VMEM] + [ANY] * 2,
        [pltpu.VMEM((2, 1040, 384), BF16), pltpu.SemaphoreType.DMA((2,))],
        flops=10**9,
        moved=4 * 2**20,
    )(where, tallies, membership, normed, qkv_far, qkv_far2)

    attended = [mine] + [lax.ppermute(mine, "x", ring(SIDE, m)) for m in (1, 2, 3)]
    attended += [mine_far] + [lax.ppermute(mine_far, "x", ring(SIDE, m)) for m in (1, 2, 3)]
    fed, kept = call(
        merge_kernel,
        [shape((512, 2048)), shape((128, 2048), F32)],
        [SMEM] + [VMEM] * 14,
        [pltpu.VMEM((512, 2048), BF16), pltpu.VMEM((512, 2048), F32)],
        flops=5 * 10**9,
        moved=14 * 2**20,
    )(where, *arrived, *attended, gain2, wmerge)

    own, s1, s2, s3 = call(
        mlp_kernel,
        [shape((128, 2048), F32)] + [shape((128, 2048))] * 3,
        [VMEM] * 2 + [ANY] * 3,
        [
            pltpu.VMEM((4, 2048, 512), BF16),
            pltpu.VMEM((2048, 2048), BF16),
            pltpu.VMEM((512, 2048), BF16),
            pltpu.SemaphoreType.DMA((8,)),
        ],
        flops=9 * 10**9,
        moved=20 * 2**20,
    )(fed, kept, w1, w2, both_all)
    sums = [lax.ppermute(s, "x", ring(SIDE, -j)) for j, s in ((1, s1), (2, s2), (3, s3))]
    done = call(sum_kernel, [shape((32, 2048))] * 4, [VMEM] * 4)(own, *sums)
    home = [done[0]] + [lax.ppermute(done[k], "y", ring(SIDE, -k)) for k in (1, 2, 3)]

    stay, cross = call(
        leave_kernel, [shape((4, CAP, 2048))] * 2, [SMEM, SMEM] + [VMEM] * 4
    )(where, tallies, *home)
    crossed = lax.ppermute(cross, "c", ring(2, 1))
    pairs = call(pair_kernel, [shape((2, CAP, 2048))] * 4, [SMEM] + [VMEM] * 2)(where, stay, crossed)
    got = [pairs[0]] + [lax.ppermute(pairs[m], "z", ring(SIDE, m)) for m in (1, 2, 3)]
    [out] = call(order_kernel, [shape((N_DP, CAP, 2048))], [SMEM] + [VMEM] * 4)(where, *got)
    return out.reshape(N_DP * CAP, -1)


def solution(mesh):
    grid = Mesh(mesh.devices.reshape(4, 2, 4, 4), ("z", "c", "y", "x"))
    head = ("y", "x")
    in_specs = (
        P(DP + head, None),
        P(DP, None),
        P(DP, None),
        P(),
        P(None, head),
        P(head),
        P(),
        P(),
        P(None, head),
        P(head, None),
    )
    return jax.shard_map(
        body, mesh=grid, in_specs=in_specs, out_specs=P(DP + head, None), check_vma=False
    )
```

profile of v0, /device:TPU:1, one launch (start us, length us, event | category | flops | bytes accessed | tf_op | source)
XLA Modules:
  0.0 216.4 jit_solution(7627158494007148690)
XLA Ops:
  6.6 1.0 copy-done.3
  8.3 0.9 shard_map.100
  9.2 1.6 copy-done.1
  10.8 1.7 shard_map.107
  12.5 2.2 %collective-permute-start.16 = (bf16[1024,512]{1,0:T(8,128)(2,1)S(1)}, bf16[1024,512]{1,0:T(8,128)(2,1)S(1)}, u32[]{:S(2)}, u32[]{:S(2)}) collective-permute-start(bf16[1024,512]{1,0:T(8,128)(2,1)S(1)} %shard_map.107), channel_id=1, source_target_pairs={{0,12},{4,0},{8,4},{12,8},{16,20},{20,24},{24,28},{28,16},{1,13},{... | collective-permute-start | bytes 3145736 | tf_op jit(solution)/shard_map/ppermute | solution.py:367
  14.7 1.3 collective-permute-start
  16.0 1.4 collective-permute-start.1
  17.4 2.0 collective-permute-start.2
  19.4 11.7 %collective-permute-done.16.got_ref.near_ref = bf16[1024,512]{1,0:T(8,128)(2,1)S(1)} collective-permute-done((bf16[1024,512]{1,0:T(8,128)(2,1)S(1)}, bf16[1024,512]{1,0:T(8,128)(2,1)S(1)}, u32[]{:S(2)}, u32[]{:S(2)}) %collective-permute-start.16) | collective-permute-done | bytes 1048608 | tf_op jit(solution)/shard_map/ppermute | solution.py:367
  32.6 2.6 %collective-permute-done.1 = bf16[32,2048]{1,0:T(8,128)(2,1)S(1)} collective-permute-done((bf16[32,2048]{1,0:T(8,128)(2,1)S(1)}, bf16[32,2048]{1,0:T(8,128)(2,1)S(1)}, u32[]{:S(2)}, u32[]{:S(2)}) %collective-permute-start.1) | collective-permute-done | bytes 131104 | tf_op jit(solution)/shard_map/ppermute | solution.py:359
  35.2 5.9 %collective-permute-done.17.far_ref = bf16[512,512]{1,0:T(8,128)(2,1)S(1)} collective-permute-done((bf16[512,512]{1,0:T(8,128)(2,1)S(1)}, bf16[512,512]{1,0:T(8,128)(2,1)S(1)}, u32[]{:S(2)}, u32[]{:S(2)}) %collective-permute-start.17) | collective-permute-done | bytes 524320 | tf_op jit(solution)/shard_map/ppermute | solution.py:369
  41.1 1.3 shard_map.109
  43.2 1.3 collective-permute-start.3
  44.5 2.4 %collective-permute-start.4 = (bf16[128,2048]{1,0:T(8,128)(2,1)S(1)}, bf16[128,2048]{1,0:T(8,128)(2,1)S(1)}, u32[]{:S(2)}, u32[]{:S(2)}) collective-permute-start(bf16[128,2048]{1,0:T(8,128)(2,1)S(1)} %constant_dynamic-update-slice_fusion.a0), channel_id=1, source_target_pairs={{0,2},{1,3},{2,0},{3,1},{4,6},{5,7},{6,4},{7,5},{8,10},{9,11},{10,... | collective-permute-start | bytes 1572872 | tf_op jit(solution)/shard_map/ppermute | solution.py:373
  47.0 1.2 collective-permute-start.5
  48.1 4.4 %collective-permute-done.3.a1 = bf16[128,2048]{1,0:T(8,128)(2,1)S(1)} collective-permute-done((bf16[128,2048]{1,0:T(8,128)(2,1)S(1)}, bf16[128,2048]{1,0:T(8,128)(2,1)S(1)}, u32[]{:S(2)}, u32[]{:S(2)}) %collective-permute-start.3) | collective-permute-done | bytes 524320 | tf_op jit(solution)/shard_map/ppermute | solution.py:373
  52.5 10.1 %collective-permute-done.4.a2 = bf16[128,2048]{1,0:T(8,128)(2,1)S(1)} collective-permute-done((bf16[128,2048]{1,0:T(8,128)(2,1)S(1)}, bf16[128,2048]{1,0:T(8,128)(2,1)S(1)}, u32[]{:S(2)}, u32[]{:S(2)}) %collective-permute-start.4) | collective-permute-done | bytes 524320 | tf_op jit(solution)/shard_map/ppermute | solution.py:373
  62.6 3.1 %collective-permute-done.5.a3 = bf16[128,2048]{1,0:T(8,128)(2,1)S(1)} collective-permute-done((bf16[128,2048]{1,0:T(8,128)(2,1)S(1)}, bf16[128,2048]{1,0:T(8,128)(2,1)S(1)}, u32[]{:S(2)}, u32[]{:S(2)}) %collective-permute-start.5) | collective-permute-done | bytes 524320 | tf_op jit(solution)/shard_map/ppermute | solution.py:373
  65.7 2.1 shard_map.102.xn
  67.8 5.4 %collective-permute-start.7 = (bf16[2064,384]{1,0:T(8,128)(2,1)S(1)}, bf16[2064,384]{1,0:T(8,128)(2,1)}, u32[]{:S(2)}, u32[]{:S(2)}) collective-permute-start(bf16[2064,384]{1,0:T(8,128)(2,1)S(1)} %collective-permute-done.6.wq1.got_ref), channel_id=1, source_target_pairs={{0,16},{16,0},{1,17},{17,1},{2,18},{18,2},{3,19},{19,3},{4,20},{20... | collective-permute-start | bytes 4755464 | tf_op jit(solution)/shard_map/ppermute | solution.py:385
  74.6 12.0 %collective-permute-done.11.wqa = bf16[1040,384]{1,0:T(8,128)(2,1)S(1)} collective-permute-done((bf16[1040,384]{1,0:T(8,128)(2,1)S(1)}, bf16[1040,384]{1,0:T(8,128)(2,1)S(1)}, u32[]{:S(2)}, u32[]{:S(2)}) %collective-permute-start.11) | collective-permute-done | bytes 798752 | tf_op jit(solution)/shard_map/ppermute | solution.py:387
  86.6 8.6 %shard_map.103.o0 = bf16[512,384]{1,0:T(8,128)(2,1)S(1)} custom-call(s32[4]{0:T(128)S(1)} %pad_add_fusion.where_ref, s32[1,8]{1,0:T(1,128)S(1)} %copy-done.7, s32[1,16]{1,0:T(1,128)S(1)} %copy-done.8, bf16[512,2048]{1,0:T(8,128)(2,1)} %shard_map.102.xn, bf16[2064,384]{1,0:T(8,128)(2,1)S(1)} %shard_map.101.wq0, ...), custom_call_target="tpu_custom_call" | custom-call | flops 3000000000 | bytes 10485760 | tf_op jit(solution)/shard_map/pallas_call | solution.py:390
  95.2 2.1 collective-permute-start.10
  97.3 1.9 collective-permute-start.9
  99.2 3.1 %shard_map.105.f0 = bf16[512,128]{1,0:T(8,128)(2,1)S(1)} custom-call(s32[4]{0:T(128)S(1)} %pad_add_fusion.where_ref, s32[1,8]{1,0:T(1,128)S(1)} %copy-done.7, s32[1,16]{1,0:T(1,128)S(1)} %copy-done.8, bf16[512,2048]{1,0:T(8,128)(2,1)S(1)} %copy-done, bf16[1040,384]{1,0:T(8,128)(2,1)S(1)} %collective-permute-done.11.wqa, ...), custom_call_target="tpu_custom_call" | custom-call | flops 1000000000 | bytes 4194304 | tf_op jit(solution)/shard_map/pallas_call | solution.py:398
  102.3 1.4 collective-permute-start.13
  103.7 0.9 collective-permute-start.14
  104.6 15.8 %collective-permute-done.13.f1 = bf16[512,128]{1,0:T(8,128)(2,1)S(1)} collective-permute-done((bf16[512,128]{1,0:T(8,128)(2,1)S(1)}, bf16[512,128]{1,0:T(8,128)(2,1)S(1)}, u32[]{:S(2)}, u32[]{:S(2)}) %collective-permute-start.13) | collective-permute-done | bytes 131104 | tf_op jit(solution)/shard_map/ppermute | solution.py:408
  120.3 1.4 collective-permute-done.14.f2
  121.7 2.4 %collective-permute-done.15.f3 = bf16[512,128]{1,0:T(8,128)(2,1)S(1)} collective-permute-done((bf16[512,128]{1,0:T(8,128)(2,1)S(1)}, bf16[512,128]{1,0:T(8,128)(2,1)S(1)}, u32[]{:S(2)}, u32[]{:S(2)}) %collective-permute-start.15) | collective-permute-done | bytes 131104 | tf_op jit(solution)/shard_map/ppermute | solution.py:408
  124.2 10.5 %shard_map.106 = (bf16[512,2048]{1,0:T(8,128)(2,1)}, f32[128,2048]{1,0:T(8,128)}) custom-call(s32[4]{0:T(128)S(1)} %pad_add_fusion.where_ref, bf16[128,2048]{1,0:T(8,128)(2,1)S(1)} %constant_dynamic-update-slice_fusion.a0, bf16[128,2048]{1,0:T(8,128)(2,1)S(1)} %collective-permute-done.3.a1, bf16[128,2048]{1,0:T(8,128)(2,1)S(1)} %collective-permute-done.4.a2, ...), custom_call_target="tpu_custom_call" | custom-call | flops 5000000000 | bytes 14680064 | tf_op jit(solution)/shard_map/pallas_call | solution.py:409
  134.6 1.2 copy-done.10
  135.9 13.5 %shard_map.110 = (f32[128,2048]{1,0:T(8,128)S(1)}, bf16[128,2048]{1,0:T(8,128)(2,1)S(1)}, bf16[128,2048]{1,0:T(8,128)(2,1)S(1)}, bf16[128,2048]{1,0:T(8,128)(2,1)S(1)}) custom-call(bf16[512,2048]{1,0:T(8,128)(2,1)} %get-tuple-element.38.fed_ref, f32[128,2048]{1,0:T(8,128)S(1)} %copy-done.10, bf16[2048,512]{1,0:T(8,128)(2,1)} %w1_ref.2, ...), custom_call_target="tpu_custom_call" | custom-call | flops 8999999488 | bytes 20971520 | tf_op jit(solution)/shard_map/pallas_call | solution.py:418
  149.3 1.3 collective-permute-start.18
  151.3 6.6 %collective-permute-done.18.r1 = bf16[128,2048]{1,0:T(8,128)(2,1)S(1)} collective-permute-done((bf16[128,2048]{1,0:T(8,128)(2,1)S(1)}, bf16[128,2048]{1,0:T(8,128)(2,1)S(1)}, u32[]{:S(2)}, u32[]{:S(2)}) %collective-permute-start.18) | collective-permute-done | bytes 524320 | tf_op jit(solution)/shard_map/ppermute | solution.py:431
  157.9 2.8 %collective-permute-done.19.r2 = bf16[128,2048]{1,0:T(8,128)(2,1)S(1)} collective-permute-done((bf16[128,2048]{1,0:T(8,128)(2,1)S(1)}, bf16[128,2048]{1,0:T(8,128)(2,1)S(1)}, u32[]{:S(2)}, u32[]{:S(2)}) %collective-permute-start.19) | collective-permute-done | bytes 524320 | tf_op jit(solution)/shard_map/ppermute | solution.py:431
  160.7 16.3 %collective-permute-done.20.r3 = bf16[128,2048]{1,0:T(8,128)(2,1)S(1)} collective-permute-done((bf16[128,2048]{1,0:T(8,128)(2,1)S(1)}, bf16[128,2048]{1,0:T(8,128)(2,1)S(1)}, u32[]{:S(2)}, u32[]{:S(2)}) %collective-permute-start.20) | collective-permute-done | bytes 524320 | tf_op jit(solution)/shard_map/ppermute | solution.py:431
  177.2 3.9 %collective-permute-start.21 = (bf16[32,2048]{1,0:T(8,128)(2,1)S(1)}, bf16[32,2048]{1,0:T(8,128)(2,1)S(1)}, u32[]{:S(2)}, u32[]{:S(2)}) collective-permute-start(bf16[32,2048]{1,0:T(8,128)(2,1)S(1)} %get-tuple-element.48), channel_id=1, source_target_pairs={{0,12},{4,0},{8,4},{12,8},{1,13},{5,1},{9,5},{13,9},{2,14},{6,2},{... | collective-permute-start | bytes 393224 | tf_op jit(solution)/shard_map/ppermute | solution.py:433
  181.8 0.8 collective-permute-start.23
  182.5 3.5 %collective-permute-done.21.h1 = bf16[32,2048]{1,0:T(8,128)(2,1)S(1)} collective-permute-done((bf16[32,2048]{1,0:T(8,128)(2,1)S(1)}, bf16[32,2048]{1,0:T(8,128)(2,1)S(1)}, u32[]{:S(2)}, u32[]{:S(2)}) %collective-permute-start.21) | collective-permute-done | bytes 131104 | tf_op jit(solution)/shard_map/ppermute | solution.py:433
  186.5 4.1 %collective-permute-done.23.h3 = bf16[32,2048]{1,0:T(8,128)(2,1)S(1)} collective-permute-done((bf16[32,2048]{1,0:T(8,128)(2,1)S(1)}, bf16[32,2048]{1,0:T(8,128)(2,1)S(1)}, u32[]{:S(2)}, u32[]{:S(2)}) %collective-permute-start.23) | collective-permute-done | bytes 131104 | tf_op jit(solution)/shard_map/ppermute | solution.py:433
  190.7 1.1 shard_map.112
  192.5 1.3 collective-permute-done.24.cross_ref
  194.4 1.4 collective-permute-start.25
  195.9 3.3 %collective-permute-start.26 = (bf16[2,24,2048]{2,1,0:T(8,128)(2,1)S(1)}, bf16[2,24,2048]{2,1,0:T(8,128)(2,1)S(1)}, u32[]{:S(2)}, u32[]{:S(2)}) collective-permute-start(bf16[2,24,2048]{2,1,0:T(8,128)(2,1)S(1)} %get-tuple-element.55), channel_id=1, source_target_pairs={{0,64},{32,96},{64,0},{96,32},{1,65},{33,97},{65,1},{97,33},{2,66}... | collective-permute-start | bytes 589832 | tf_op jit(solution)/shard_map/ppermute | solution.py:440
  200.0 3.0 %collective-permute-done.25.g1 = bf16[2,24,2048]{2,1,0:T(8,128)(2,1)S(1)} collective-permute-done((bf16[2,24,2048]{2,1,0:T(8,128)(2,1)S(1)}, bf16[2,24,2048]{2,1,0:T(8,128)(2,1)S(1)}, u32[]{:S(2)}, u32[]{:S(2)}) %collective-permute-start.25) | collective-permute-done | bytes 196640 | tf_op jit(solution)/shard_map/ppermute | solution.py:440
  203.0 5.1 %collective-permute-done.26.g2 = bf16[2,24,2048]{2,1,0:T(8,128)(2,1)S(1)} collective-permute-done((bf16[2,24,2048]{2,1,0:T(8,128)(2,1)S(1)}, bf16[2,24,2048]{2,1,0:T(8,128)(2,1)S(1)}, u32[]{:S(2)}, u32[]{:S(2)}) %collective-permute-start.26) | collective-permute-done | bytes 196640 | tf_op jit(solution)/shard_map/ppermute | solution.py:440
  208.1 1.5 shard_map.114
  (53 shorter events, 7.9 us)
Async XLA Ops:
  6.5 128.1 %all-gather.3.cloned.1.call-start = ((), (), s32[]{:S(2)}) async-start(), calls=%async_computation | async-start | bytes 14155776 | tf_op jit(solution)/shard_map/all_gather | solution.py:381
  6.6 1.0 copy-start.3
  7.7 0.7 copy-start.6
  9.2 1.6 copy-start.1
  12.5 18.6 %collective-permute-start.16 = (bf16[1024,512]{1,0:T(8,128)(2,1)S(1)}, bf16[1024,512]{1,0:T(8,128)(2,1)S(1)}, u32[]{:S(2)}, u32[]{:S(2)}) collective-permute-start(bf16[1024,512]{1,0:T(8,128)(2,1)S(1)} %shard_map.107), channel_id=1, source_target_pairs={{0,12},{4,0},{8,4},{12,8},{16,20},{20,24},{24,28},{28,16},{1,13},{... | collective-permute-start | bytes 3145736 | tf_op jit(solution)/shard_map/ppermute | solution.py:367
  14.7 17.8 %collective-permute-start = (bf16[32,2048]{1,0:T(8,128)(2,1)S(1)}, bf16[32,2048]{1,0:T(8,128)(2,1)S(1)}, u32[]{:S(2)}, u32[]{:S(2)}) collective-permute-start(bf16[32,2048]{1,0:T(8,128)(2,1)S(1)} %get-tuple-element.32), channel_id=1, source_target_pairs={{0,4},{4,8},{8,12},{12,0},{1,5},{5,9},{9,13},{13,1},{2,6},{6,10},{... | collective-permute-start | bytes 393224 | tf_op jit(solution)/shard_map/ppermute | solution.py:359
  16.0 19.1 %collective-permute-start.1 = (bf16[32,2048]{1,0:T(8,128)(2,1)S(1)}, bf16[32,2048]{1,0:T(8,128)(2,1)S(1)}, u32[]{:S(2)}, u32[]{:S(2)}) collective-permute-start(bf16[32,2048]{1,0:T(8,128)(2,1)S(1)} %get-tuple-element.33), channel_id=1, source_target_pairs={{0,8},{4,12},{8,0},{12,4},{1,9},{5,13},{9,1},{13,5},{2,10},{6,14},... | collective-permute-start | bytes 393224 | tf_op jit(solution)/shard_map/ppermute | solution.py:359
  17.4 17.7 %collective-permute-start.2 = (bf16[32,2048]{1,0:T(8,128)(2,1)S(1)}, bf16[32,2048]{1,0:T(8,128)(2,1)S(1)}, u32[]{:S(2)}, u32[]{:S(2)}) collective-permute-start(bf16[32,2048]{1,0:T(8,128)(2,1)S(1)} %get-tuple-element.34), channel_id=1, source_target_pairs={{0,12},{4,0},{8,4},{12,8},{1,13},{5,1},{9,5},{13,9},{2,14},{6,2},{... | collective-permute-start | bytes 393224 | tf_op jit(solution)/shard_map/ppermute | solution.py:359
  31.8 9.3 %collective-permute-start.17 = (bf16[512,512]{1,0:T(8,128)(2,1)S(1)}, bf16[512,512]{1,0:T(8,128)(2,1)S(1)}, u32[]{:S(2)}, u32[]{:S(2)}) collective-permute-start(bf16[512,512]{1,0:T(8,128)(2,1)S(1)} %shard_map.108), channel_id=1, source_target_pairs={{0,12},{4,0},{8,4},{12,8},{16,20},{20,24},{24,28},{28,16},{1,13},{... | collective-permute-start | bytes 1572872 | tf_op jit(solution)/shard_map/ppermute | solution.py:369
  35.2 7.8 %copy-start.2 = (bf16[2048,384]{1,0:T(8,128)(2,1)S(1)}, bf16[2048,384]{1,0:T(8,128)(2,1)}, u32[]{:S(2)}) copy-start(bf16[2048,384]{1,0:T(8,128)(2,1)} %wqkv_ref) | copy-start | bytes 4718596
  42.3 23.4 %copy-start.5 = (f32[2048]{0:T(1024)S(1)}, f32[2048]{0:T(1024)}, u32[]{:S(2)}) copy-start(f32[2048]{0:T(1024)} %param.13) | copy-start | bytes 24580
  43.2 24.7 %collective-permute-start.6 = (bf16[2064,384]{1,0:T(8,128)(2,1)S(1)}, bf16[2064,384]{1,0:T(8,128)(2,1)S(1)}, u32[]{:S(2)}, u32[]{:S(2)}) collective-permute-start(bf16[2064,384]{1,0:T(8,128)(2,1)S(1)} %shard_map.101.wq0), channel_id=1, source_target_pairs={{0,12},{4,0},{8,4},{12,8},{16,20},{20,24},{24,28},{28,16},{1,13},{... | collective-permute-start | bytes 4755464 | tf_op jit(solution)/shard_map/ppermute | solution.py:380
  43.2 9.3 %collective-permute-start.3 = (bf16[128,2048]{1,0:T(8,128)(2,1)S(1)}, bf16[128,2048]{1,0:T(8,128)(2,1)S(1)}, u32[]{:S(2)}, u32[]{:S(2)}) collective-permute-start(bf16[128,2048]{1,0:T(8,128)(2,1)S(1)} %constant_dynamic-update-slice_fusion.a0), channel_id=1, source_target_pairs={{0,1},{1,2},{2,3},{3,0},{4,5},{5,6},{6,7},{7,4},{8,9},{9,10},{10,1... | collective-permute-start | bytes 1572872 | tf_op jit(solution)/shard_map/ppermute | solution.py:373
  44.5 18.1 %collective-permute-start.4 = (bf16[128,2048]{1,0:T(8,128)(2,1)S(1)}, bf16[128,2048]{1,0:T(8,128)(2,1)S(1)}, u32[]{:S(2)}, u32[]{:S(2)}) collective-permute-start(bf16[128,2048]{1,0:T(8,128)(2,1)S(1)} %constant_dynamic-update-slice_fusion.a0), channel_id=1, source_target_pairs={{0,2},{1,3},{2,0},{3,1},{4,6},{5,7},{6,4},{7,5},{8,10},{9,11},{10,... | collective-permute-start | bytes 1572872 | tf_op jit(solution)/shard_map/ppermute | solution.py:373
  47.0 18.8 %collective-permute-start.5 = (bf16[128,2048]{1,0:T(8,128)(2,1)S(1)}, bf16[128,2048]{1,0:T(8,128)(2,1)S(1)}, u32[]{:S(2)}, u32[]{:S(2)}) collective-permute-start(bf16[128,2048]{1,0:T(8,128)(2,1)S(1)} %constant_dynamic-update-slice_fusion.a0), channel_id=1, source_target_pairs={{0,3},{1,0},{2,1},{3,2},{4,7},{5,4},{6,5},{7,6},{8,11},{9,8},{10,9... | collective-permute-start | bytes 1572872 | tf_op jit(solution)/shard_map/ppermute | solution.py:373
  65.7 2.1 copy-start.4
  67.8 18.7 %copy-start.7 = (s32[1,8]{1,0:T(1,128)S(1)}, s32[1,8]{1,0:T(1,128)}, u32[]{:S(2)}) copy-start(s32[1,8]{1,0:T(1,128)} %count_ref.7) | copy-start | bytes 100
  67.8 18.7 %copy-start.8 = (s32[1,16]{1,0:T(1,128)S(1)}, s32[1,16]{1,0:T(1,128)}, u32[]{:S(2)}) copy-start(s32[1,16]{1,0:T(1,128)} %member_ref.3) | copy-start | bytes 196
  67.8 18.7 %collective-permute-start.7 = (bf16[2064,384]{1,0:T(8,128)(2,1)S(1)}, bf16[2064,384]{1,0:T(8,128)(2,1)}, u32[]{:S(2)}, u32[]{:S(2)}) collective-permute-start(bf16[2064,384]{1,0:T(8,128)(2,1)S(1)} %collective-permute-done.6.wq1.got_ref), channel_id=1, source_target_pairs={{0,16},{16,0},{1,17},{17,1},{2,18},{18,2},{3,19},{19,3},{4,20},{20... | collective-permute-start | bytes 4755464 | tf_op jit(solution)/shard_map/ppermute | solution.py:385
  73.9 25.3 %copy-start = (bf16[512,2048]{1,0:T(8,128)(2,1)S(1)}, bf16[512,2048]{1,0:T(8,128)(2,1)}, u32[]{:S(2)}) copy-start(bf16[512,2048]{1,0:T(8,128)(2,1)} %shard_map.102.xn) | copy-start | bytes 6291460
  73.9 12.7 %collective-permute-start.11 = (bf16[1040,384]{1,0:T(8,128)(2,1)S(1)}, bf16[1040,384]{1,0:T(8,128)(2,1)S(1)}, u32[]{:S(2)}, u32[]{:S(2)}) collective-permute-start(bf16[1040,384]{1,0:T(8,128)(2,1)S(1)} %shard_map.104), channel_id=1, source_target_pairs={{0,12},{4,0},{8,4},{12,8},{16,20},{20,24},{24,28},{28,16},{1,13},{... | collective-permute-start | bytes 2396168 | tf_op jit(solution)/shard_map/ppermute | solution.py:387
  86.6 12.7 %collective-permute-start.12 = (bf16[1040,384]{1,0:T(8,128)(2,1)S(1)}, bf16[1040,384]{1,0:T(8,128)(2,1)S(1)}, u32[]{:S(2)}, u32[]{:S(2)}) collective-permute-start(bf16[1040,384]{1,0:T(8,128)(2,1)S(1)} %collective-permute-done.11.wqa), channel_id=1, source_target_pairs={{0,16},{16,0},{1,17},{17,1},{2,18},{18,2},{3,19},{19,3},{4,20},{20... | collective-permute-start | bytes 2396168 | tf_op jit(solution)/shard_map/ppermute | solution.py:388
  95.2 28.9 %copy-start.9 = (f32[2048]{0:T(1024)S(1)}, f32[2048]{0:T(1024)}, u32[]{:S(2)}) copy-start(f32[2048]{0:T(1024)} %param.17) | copy-start | bytes 24580
  95.2 28.9 %collective-permute-start.10 = (bf16[512,384]{1,0:T(8,128)(2,1)S(1)}, bf16[512,384]{1,0:T(8,128)(2,1)S(1)}, u32[]{:S(2)}, u32[]{:S(2)}) collective-permute-start(bf16[512,384]{1,0:T(8,128)(2,1)S(1)} %shard_map.103.o0), channel_id=1, source_target_pairs={{0,3},{1,0},{2,1},{3,2},{4,7},{5,4},{6,5},{7,6},{8,11},{9,8},{10,9... | collective-permute-start | bytes 1179656 | tf_op jit(solution)/shard_map/ppermute | solution.py:407
  97.3 26.8 %collective-permute-start.8 = (bf16[512,384]{1,0:T(8,128)(2,1)S(1)}, bf16[512,384]{1,0:T(8,128)(2,1)S(1)}, u32[]{:S(2)}, u32[]{:S(2)}) collective-permute-start(bf16[512,384]{1,0:T(8,128)(2,1)S(1)} %shard_map.103.o0), channel_id=1, source_target_pairs={{0,1},{1,2},{2,3},{3,0},{4,5},{5,6},{6,7},{7,4},{8,9},{9,10},{10,1... | collective-permute-start | bytes 1179656 | tf_op jit(solution)/shard_map/ppermute | solution.py:407
  97.3 26.8 %collective-permute-start.9 = (bf16[512,384]{1,0:T(8,128)(2,1)S(1)}, bf16[512,384]{1,0:T(8,128)(2,1)S(1)}, u32[]{:S(2)}, u32[]{:S(2)}) collective-permute-start(bf16[512,384]{1,0:T(8,128)(2,1)S(1)} %shard_map.103.o0), channel_id=1, source_target_pairs={{0,2},{1,3},{2,0},{3,1},{4,6},{5,7},{6,4},{7,5},{8,10},{9,11},{10,... | collective-permute-start | bytes 1179656 | tf_op jit(solution)/shard_map/ppermute | solution.py:407
  102.3 18.0 %collective-permute-start.13 = (bf16[512,128]{1,0:T(8,128)(2,1)S(1)}, bf16[512,128]{1,0:T(8,128)(2,1)S(1)}, u32[]{:S(2)}, u32[]{:S(2)}) collective-permute-start(bf16[512,128]{1,0:T(8,128)(2,1)S(1)} %shard_map.105.f0), channel_id=1, source_target_pairs={{0,1},{1,2},{2,3},{3,0},{4,5},{5,6},{6,7},{7,4},{8,9},{9,10},{10,1... | collective-permute-start | bytes 393224 | tf_op jit(solution)/shard_map/ppermute | solution.py:408
  103.7 18.0 %collective-permute-start.14 = (bf16[512,128]{1,0:T(8,128)(2,1)S(1)}, bf16[512,128]{1,0:T(8,128)(2,1)S(1)}, u32[]{:S(2)}, u32[]{:S(2)}) collective-permute-start(bf16[512,128]{1,0:T(8,128)(2,1)S(1)} %shard_map.105.f0), channel_id=1, source_target_pairs={{0,2},{1,3},{2,0},{3,1},{4,6},{5,7},{6,4},{7,5},{8,10},{9,11},{10,... | collective-permute-start | bytes 393224 | tf_op jit(solution)/shard_map/ppermute | solution.py:408
  120.3 3.8 %collective-permute-start.15 = (bf16[512,128]{1,0:T(8,128)(2,1)S(1)}, bf16[512,128]{1,0:T(8,128)(2,1)S(1)}, u32[]{:S(2)}, u32[]{:S(2)}) collective-permute-start(bf16[512,128]{1,0:T(8,128)(2,1)S(1)} %shard_map.105.f0), channel_id=1, source_target_pairs={{0,3},{1,0},{2,1},{3,2},{4,7},{5,4},{6,5},{7,6},{8,11},{9,8},{10,9... | collective-permute-start | bytes 393224 | tf_op jit(solution)/shard_map/ppermute | solution.py:408
  134.6 1.2 copy-start.10
  149.3 8.6 %collective-permute-start.18 = (bf16[128,2048]{1,0:T(8,128)(2,1)S(1)}, bf16[128,2048]{1,0:T(8,128)(2,1)S(1)}, u32[]{:S(2)}, u32[]{:S(2)}) collective-permute-start(bf16[128,2048]{1,0:T(8,128)(2,1)S(1)} %get-tuple-element.44), channel_id=1, source_target_pairs={{0,3},{1,0},{2,1},{3,2},{4,7},{5,4},{6,5},{7,6},{8,11},{9,8},{10,9... | collective-permute-start | bytes 1572872 | tf_op jit(solution)/shard_map/ppermute | solution.py:431
  150.6 10.1 %collective-permute-start.19 = (bf16[128,2048]{1,0:T(8,128)(2,1)S(1)}, bf16[128,2048]{1,0:T(8,128)(2,1)S(1)}, u32[]{:S(2)}, u32[]{:S(2)}) collective-permute-start(bf16[128,2048]{1,0:T(8,128)(2,1)S(1)} %get-tuple-element.45), channel_id=1, source_target_pairs={{0,2},{1,3},{2,0},{3,1},{4,6},{5,7},{6,4},{7,5},{8,10},{9,11},{10,... | collective-permute-start | bytes 1572872 | tf_op jit(solution)/shard_map/ppermute | solution.py:431
  150.8 26.2 %collective-permute-start.20 = (bf16[128,2048]{1,0:T(8,128)(2,1)S(1)}, bf16[128,2048]{1,0:T(8,128)(2,1)S(1)}, u32[]{:S(2)}, u32[]{:S(2)}) collective-permute-start(bf16[128,2048]{1,0:T(8,128)(2,1)S(1)} %get-tuple-element.46), channel_id=1, source_target_pairs={{0,1},{1,2},{2,3},{3,0},{4,5},{5,6},{6,7},{7,4},{8,9},{9,10},{10,1... | collective-permute-start | bytes 1572872 | tf_op jit(solution)/shard_map/ppermute | solution.py:431
  177.2 8.8 %collective-permute-start.21 = (bf16[32,2048]{1,0:T(8,128)(2,1)S(1)}, bf16[32,2048]{1,0:T(8,128)(2,1)S(1)}, u32[]{:S(2)}, u32[]{:S(2)}) collective-permute-start(bf16[32,2048]{1,0:T(8,128)(2,1)S(1)} %get-tuple-element.48), channel_id=1, source_target_pairs={{0,12},{4,0},{8,4},{12,8},{1,13},{5,1},{9,5},{13,9},{2,14},{6,2},{... | collective-permute-start | bytes 393224 | tf_op jit(solution)/shard_map/ppermute | solution.py:433
  181.1 5.4 %collective-permute-start.22 = (bf16[32,2048]{1,0:T(8,128)(2,1)S(1)}, bf16[32,2048]{1,0:T(8,128)(2,1)S(1)}, u32[]{:S(2)}, u32[]{:S(2)}) collective-permute-start(bf16[32,2048]{1,0:T(8,128)(2,1)S(1)} %get-tuple-element.49), channel_id=1, source_target_pairs={{0,8},{4,12},{8,0},{12,4},{1,9},{5,13},{9,1},{13,5},{2,10},{6,14},... | collective-permute-start | bytes 393224 | tf_op jit(solution)/shard_map/ppermute | solution.py:433
  181.8 8.9 %collective-permute-start.23 = (bf16[32,2048]{1,0:T(8,128)(2,1)S(1)}, bf16[32,2048]{1,0:T(8,128)(2,1)S(1)}, u32[]{:S(2)}, u32[]{:S(2)}) collective-permute-start(bf16[32,2048]{1,0:T(8,128)(2,1)S(1)} %get-tuple-element.50), channel_id=1, source_target_pairs={{0,4},{4,8},{8,12},{12,0},{1,5},{5,9},{9,13},{13,1},{2,6},{6,10},{... | collective-permute-start | bytes 393224 | tf_op jit(solution)/shard_map/ppermute | solution.py:433
  191.7 2.1 collective-permute-start.24
  194.4 8.6 %collective-permute-start.25 = (bf16[2,24,2048]{2,1,0:T(8,128)(2,1)S(1)}, bf16[2,24,2048]{2,1,0:T(8,128)(2,1)S(1)}, u32[]{:S(2)}, u32[]{:S(2)}) collective-permute-start(bf16[2,24,2048]{2,1,0:T(8,128)(2,1)S(1)} %get-tuple-element.54), channel_id=1, source_target_pairs={{0,32},{32,64},{64,96},{96,0},{1,33},{33,65},{65,97},{97,1},{2,34}... | collective-permute-start | bytes 589832 | tf_op jit(solution)/shard_map/ppermute | solution.py:440
  195.9 12.2 %collective-permute-start.26 = (bf16[2,24,2048]{2,1,0:T(8,128)(2,1)S(1)}, bf16[2,24,2048]{2,1,0:T(8,128)(2,1)S(1)}, u32[]{:S(2)}, u32[]{:S(2)}) collective-permute-start(bf16[2,24,2048]{2,1,0:T(8,128)(2,1)S(1)} %get-tuple-element.55), channel_id=1, source_target_pairs={{0,64},{32,96},{64,0},{96,32},{1,65},{33,97},{65,1},{97,33},{2,66}... | collective-permute-start | bytes 589832 | tf_op jit(solution)/shard_map/ppermute | solution.py:440
  199.2 8.9 %collective-permute-start.27 = (bf16[2,24,2048]{2,1,0:T(8,128)(2,1)S(1)}, bf16[2,24,2048]{2,1,0:T(8,128)(2,1)S(1)}, u32[]{:S(2)}, u32[]{:S(2)}) collective-permute-start(bf16[2,24,2048]{2,1,0:T(8,128)(2,1)S(1)} %get-tuple-element.56), channel_id=1, source_target_pairs={{0,96},{32,0},{64,32},{96,64},{1,97},{33,1},{65,33},{97,65},{2,98}... | collective-permute-start | bytes 589832 | tf_op jit(solution)/shard_map/ppermute | solution.py:440
Sparse Core Ops, SparseCore 0:
  42.5 73.8 all-gather.2
where the time goes:
time: 217 us; the launch traced here: 216 us
  waiting for transfers between devices  113 us (52%)
  Pallas kernels  46.3 us (21%)
  starting transfers between devices  38.2 us (18%)
  between operations  14.3 us (7%)
  local copies, waits for them, and re-layouts  4.58 us (2%)
    ppermute x3, waiting for transfers between devices, body(): lax.ppermute(s, 'x', ring(SIDE, -j))  25.7 us
    ppermute x3, waiting for transfers between devices, body(): lax.ppermute(mine_far, 'x', ring(SIDE, m))  19.6 us
    ppermute x3, waiting for transfers between devices, body(): lax.ppermute(column, 'x', ring(SIDE, m))  17.6 us
    pallas_call x1, Pallas kernels, body(): call(mlp_kernel, [shape((128, 2048), F32)] + [shape((128, 2048))] * 3, [V...  13.5 us
    ppermute x1, waiting for transfers between devices, body(): qkv_far = lax.ppermute(qkv_half, cy, twin_ring())  12 us
    ppermute x1, waiting for transfers between devices, body(): near = lax.ppermute(mlp_slice, cy, twin_ring())  11.7 us
    pallas_call x1, Pallas kernels, body(): call(merge_kernel, [shape((512, 2048)), shape((128, 2048), F32)], [SMEM]...  10.5 us
    pallas_call x1, Pallas kernels, body(): call(near_kernel, [shape((512, 384))], [SMEM] * 3 + [VMEM] + [ANY] * 3, [...  8.63 us
  transfers between devices with their start and end apart: 29, of which 20 were waited for; matrix products, arithmetic and copies ran while one was open for 0% of the time, Pallas kernels for 12%

commit v1 on v0

--- a/solution.py
+++ b/solution.py
@@ -173,7 +173,7 @@
     scale = jnp.sum(scale_row.astype(F32), axis=-1, keepdims=True)
     score = jnp.where(allowed, score * scale, -1e30)
     weights = jnp.exp(score - jnp.max(score, axis=-1, keepdims=True))
-    p = (weights / jnp.sum(weights, axis=-1, keepdims=True)).astype(BF16)
+    p = (weights * (1.0 / jnp.sum(weights, axis=-1, keepdims=True))).astype(BF16)
     return dot(p, v).astype(BF16)
 
 
@@ -186,35 +186,36 @@
         ).astype(BF16)
 
 
-def near_kernel(
-    where_ref, count_ref, member_ref, xn, wq0, wq1, wq2, out_ref, w0, w1, w2, sem
-):
+def near_kernel(where_ref, count_ref, member_ref, xn, wq0, wq1, out_ref, w0, w1, sem):
     copies = [
         pltpu.make_async_copy(src, dst, sem.at[i])
-        for i, (src, dst) in enumerate(((wq0, w0), (wq1, w1), (wq2, w2)))
+        for i, (src, dst) in enumerate(((wq0, w0), (wq1, w1)))
     ]
     for copy in copies:
         copy.start()
     allowed = key_of_place(count_ref, member_ref, where_ref[2])
-    for k, w in enumerate((w0, w1, w2)):
+    for k, w in enumerate((w0, w1)):
         copies[k].wait()
         raw = dot(xn[...], w[:2048])
         out_ref[:, 128 * k : 128 * k + 128] = attend(raw, w[2048:2049], allowed)
 
 
-def far_attention_kernel(where_ref, count_ref, member_ref, xn, wqa, wqb, out_ref, w3, sem):
+def far_attention_kernel(where_ref, count_ref, member_ref, xn, wq2, wqa, wqb, out_ref, w2, w3, sem):
     c = where_ref[1]
     copies = [
-        pltpu.make_async_copy(wqa, w3.at[c], sem.at[0]),
-        pltpu.make_async_copy(wqb, w3.at[1 - c], sem.at[1]),
+        pltpu.make_async_copy(wq2, w2, sem.at[0]),
+        pltpu.make_async_copy(wqa, w3.at[c], sem.at[1]),
+        pltpu.make_async_copy(wqb, w3.at[1 - c], sem.at[2]),
     ]
     for copy in copies:
         copy.start()
     allowed = key_of_place(count_ref, member_ref, where_ref[2])
-    for copy in copies:
-        copy.wait()
+    copies[0].wait()
+    out_ref[:, :128] = attend(dot(xn[...], w2[:2048]), w2[2048:2049], allowed)
+    copies[1].wait()
+    copies[2].wait()
     raw = dot(xn[:, :1024], w3[0, :1024]) + dot(xn[:, 1024:], w3[1, :1024])
-    out_ref[...] = attend(raw, w3[0, 1024:1025], allowed)
+    out_ref[:, 128:] = attend(raw, w3[0, 1024:1025], allowed)
 
 
 def merge_kernel(
@@ -230,7 +231,7 @@
             cols = pl.ds(pl.multiple_of(head * HEAD_DIM, HEAD_DIM), HEAD_DIM)
             for j in range(SIDE):
                 theirs = slice(128 * ((j - m) % SIDE), 128 * ((j - m) % SIDE) + 128)
-                block = far[theirs] if k == 3 else near[theirs, 128 * k : 128 * k + 128]
+                block = (near, far)[k // 2][theirs, 128 * (k % 2) : 128 * (k % 2) + 128]
                 heads[128 * j : 128 * j + 128, cols] = block
     squares = jnp.zeros((512, 1), F32)
     for n in range(4):
@@ -248,7 +249,7 @@
 
 
 def mlp_kernel(
-    fed_ref, kept_ref, w1_ref, w2_ref, all_ref, own_ref, s1, s2, s3, w1, w2, hidden, sem
+    where_ref, fed_ref, kept_ref, w1_ref, w2_ref, all_ref, out_ref, w1, w2, hidden, sem
 ):
     copies = [
         [pltpu.make_async_copy(w1_ref, w1.at[0], sem.at[0])],
@@ -305,25 +306,29 @@
     for n in range(4):
         cols = slice(512 * n, 512 * n + 512)
         part = dot(hidden[...], w2[:, cols])
-        own_ref[:, cols] = kept_ref[:, cols] + part[:128]
-        for j, ref in enumerate((s1, s2, s3)):
-            ref[:, cols] = part[128 * (j + 1) : 128 * (j + 2)].astype(BF16)
-
-
-def sum_kernel(own_ref, r1, r2, r3, *outs):
-    total = own_ref[...] + r1[...].astype(F32) + r2[...].astype(F32) + r3[...].astype(F32)
-    total = total.astype(BF16)
-    for k in range(SIDE):
-        outs[k][...] = total[32 * k : 32 * k + 32]
-
-
-def leave_kernel(where_ref, count_ref, h0, h1, h2, h3, stay_ref, cross_ref):
-    z, c, y = where_ref[0], where_ref[1], where_ref[2]
-    count, _, start = placement(count_ref, y)
+        for j in range(SIDE):
+            for k in range(SIDE):
+                rows = slice(128 * j + 32 * k, 128 * j + 32 * k + 32)
+                home = ((where_ref[2] - k + 4) & 3) * SIDE + ((where_ref[3] - j + 4) & 3)
+                block = part[rows]
+                if j == 0:
+                    block = block + kept_ref[rows, cols]
+                out_ref[home, :, cols] = block.astype(BF16)
+
+
+def leave_kernel(where_ref, count_ref, parts_ref, stay_ref, cross_ref):
+    z, c = where_ref[0], where_ref[1]
+    count, _, start = placement(count_ref, 0)
     slot = lax.broadcasted_iota(jnp.int32, (192, 1), 0)
     block = slot // CAP
     inner = slot - block * CAP
-    home = jnp.concatenate([h0[...], h1[...], h2[...], h3[...]], 0)
+    rows = []
+    for y in range(SIDE):
+        total = parts_ref[4 * y].astype(F32)
+        for x in range(1, SIDE):
+            total = total + parts_ref[4 * y + x].astype(F32)
+        rows.append(total.astype(BF16))
+    home = jnp.concatenate(rows, 0)
     target = jnp.full((192, 1), -1, jnp.int32)
     for d in range(N_DP):
         turn = ((d >> 1) - z + 4) & 3
@@ -355,7 +360,9 @@
     gain2 = gain2[None]
     cy = ("c", "y")
 
-    blocks = call(pick_kernel, [shape((32, 2048))] * 4, [SMEM, SMEM, VMEM])(where, tallies, tokens)
+    blocks = call(
+        pick_kernel, [shape((32, 2048))] * 4, [SMEM, SMEM, VMEM], flops=10 * 10**9
+    )(where, tallies, tokens)
     came = [blocks[0]] + [lax.ppermute(blocks[k], "y", ring(SIDE, k)) for k in (1, 2, 3)]
     w1_later, w2_later, _ = lax.optimization_barrier((w1, w2, blocks[1]))
     [mlp_slice] = call(
@@ -365,11 +372,12 @@
         [pltpu.SemaphoreType.DMA((5,))],
     )(where, w1_later, w2_later)
     near = lax.ppermute(mlp_slice, cy, twin_ring())
+    column = jnp.concatenate(came, 0)
+    near, column = lax.optimization_barrier((near, column))
     [near_half] = call(half_kernel, [shape((512, 512))], [SMEM, VMEM])(where, near)
     far = lax.ppermute(near_half, cy, twin_ring())
     [both] = call(join_kernel, [shape((1536, 512))], [VMEM] * 2)(near, far)
 
-    column = jnp.concatenate(came, 0)
     arrived = [column] + [lax.ppermute(column, "x", ring(SIDE, m)) for m in (1, 2, 3)]
     [packed] = call(
         pack_kernel,
@@ -378,31 +386,38 @@
         [pltpu.SemaphoreType.DMA],
     )(sharp, lax.optimization_barrier((wqkv, column))[0])
     qkv_near = lax.ppermute(packed, cy, twin_ring())
-    both_all = lax.all_gather(lax.optimization_barrier((both, column))[0], DP, axis=0, tiled=False)
-
-    [normed] = call(norm_kernel, [shape((512, 2048))], [VMEM] * 5)(*arrived, gain1)
+    both_all = lax.all_gather(both, DP, axis=0, tiled=False)
+
+    [normed] = call(norm_kernel, [shape((512, 2048))], [VMEM] * 5, flops=25 * 10**9)(
+        *arrived, gain1
+    )
     qkv_near, normed = lax.optimization_barrier((qkv_near, normed))
     qkv_near2 = lax.ppermute(qkv_near, "c", ring(2, 1))
     [qkv_half] = call(far_kernel, [shape((1040, 384))], [SMEM, VMEM])(where, qkv_near)
     qkv_far = lax.ppermute(qkv_half, cy, twin_ring())
-    qkv_far2 = lax.ppermute(qkv_far, "c", ring(2, 1))
 
     [mine] = call(
         near_kernel,
-        [shape((512, 384))],
-        [SMEM] * 3 + [VMEM] + [ANY] * 3,
-        [pltpu.VMEM((2064, 384), BF16)] * 3 + [pltpu.SemaphoreType.DMA((3,))],
-        flops=3 * 10**9,
-        moved=10 * 2**20,
-    )(where, tallies, membership, normed, packed, qkv_near, qkv_near2)
+        [shape((512, 256))],
+        [SMEM] * 3 + [VMEM] + [ANY] * 2,
+        [pltpu.VMEM((2064, 384), BF16)] * 2 + [pltpu.SemaphoreType.DMA((2,))],
+        flops=2 * 10**9,
+        moved=8 * 2**20,
+    )(where, tallies, membership, normed, packed, qkv_near)
+    qkv_far, mine = lax.optimization_barrier((qkv_far, mine))
+    qkv_far2 = lax.ppermute(qkv_far, "c", ring(2, 1))
     [mine_far] = call(
         far_attention_kernel,
-        [shape((512, 128))],
-        [SMEM] * 3 + [VMEM] + [ANY] * 2,
-        [pltpu.VMEM((2, 1040, 384), BF16), pltpu.SemaphoreType.DMA((2,))],
-        flops=10**9,
-        moved=4 * 2**20,
-    )(where, tallies, membership, normed, qkv_far, qkv_far2)
+        [shape((512, 256))],
+        [SMEM] * 3 + [VMEM] + [ANY] * 3,
+        [
+            pltpu.VMEM((2064, 384), BF16),
+            pltpu.VMEM((2, 1040, 384), BF16),
+            pltpu.SemaphoreType.DMA((3,)),
+        ],
+        flops=2 * 10**9,
+        moved=8 * 2**20,
+    )(where, tallies, membership, normed, qkv_near2, qkv_far, qkv_far2)
 
     attended = [mine] + [lax.ppermute(mine, "x", ring(SIDE, m)) for m in (1, 2, 3)]
     attended += [mine_far] + [lax.ppermute(mine_far, "x", ring(SIDE, m)) for m in (1, 2, 3)]
@@ -411,14 +426,14 @@
         [shape((512, 2048)), shape((128, 2048), F32)],
         [SMEM] + [VMEM] * 14,
         [pltpu.VMEM((512, 2048), BF16), pltpu.VMEM((512, 2048), F32)],
-        flops=5 * 10**9,
+        flops=25 * 10**9,
         moved=14 * 2**20,
     )(where, *arrived, *attended, gain2, wmerge)
 
-    own, s1, s2, s3 = call(
+    [parts] = call(
         mlp_kernel,
-        [shape((128, 2048), F32)] + [shape((128, 2048))] * 3,
-        [VMEM] * 2 + [ANY] * 3,
+        [shape((16, 32, 2048))],
+        [SMEM] + [VMEM] * 2 + [ANY] * 3,
         [
             pltpu.VMEM((4, 2048, 512), BF16),
             pltpu.VMEM((2048, 2048), BF16),
@@ -427,14 +442,11 @@
         ],
         flops=9 * 10**9,
         moved=20 * 2**20,
-    )(fed, kept, w1, w2, both_all)
-    sums = [lax.ppermute(s, "x", ring(SIDE, -j)) for j, s in ((1, s1), (2, s2), (3, s3))]
-    done = call(sum_kernel, [shape((32, 2048))] * 4, [VMEM] * 4)(own, *sums)
-    home = [done[0]] + [lax.ppermute(done[k], "y", ring(SIDE, -k)) for k in (1, 2, 3)]
-
-    stay, cross = call(
-        leave_kernel, [shape((4, CAP, 2048))] * 2, [SMEM, SMEM] + [VMEM] * 4
-    )(where, tallies, *home)
+    )(where, fed, kept, w1, w2, both_all)
+    parts = lax.all_to_all(parts, ("y", "x"), 0, 0, tiled=True)
+    stay, cross = call(leave_kernel, [shape((4, CAP, 2048))] * 2, [SMEM, SMEM, VMEM])(
+        where, tallies, parts
+    )
     crossed = lax.ppermute(cross, "c", ring(2, 1))
     pairs = call(pair_kernel, [shape((2, CAP, 2048))] * 4, [SMEM] + [VMEM] * 2)(where, stay, crossed)
     got = [pairs[0]] + [lax.ppermute(pairs[m], "z", ring(SIDE, m)) for m in (1, 2, 3)]

time: 217 us -> 201 us (0.926)
  waiting for transfers between devices: 113 us -> 68.9 us
  blocking collectives: 0 us -> 32.9 us
  starting transfers between devices: 38.2 us -> 33.5 us
    ppermute x6 -> x0, waiting for transfers between devices: 33.8 us -> none  [the longest x3 25.7 us: body(): lax.ppermute(s, 'x', ring(SIDE, -j))]
    all_to_all x0 -> x1, blocking collectives: none -> 32.9 us  [body(): parts = lax.all_to_all(parts, ('y', 'x'), 0, 0, tiled=True)]
    ppermute x3, waiting for transfers between devices: 3 us -> 15.7 us  [body(): lax.ppermute(blocks[k], 'y', ring(SIDE, k))]
    ppermute x1, waiting for transfers between devices: 11.7 us -> 0.01 us  [body(): near = lax.ppermute(mlp_slice, cy, twin_ring())]
    ppermute x1, waiting for transfers between devices: 12 us -> 1.12 us  [body(): qkv_far = lax.ppermute(qkv_half, cy, twin_ring())]
    ppermute x3, waiting for transfers between devices: 19.6 us -> 10.9 us  [body(): lax.ppermute(mine_far, 'x', ring(SIDE, m))]
    ppermute x6 -> x0, starting transfers between devices: 7.3 us -> none  [the longest x3 5.34 us: body(): lax.ppermute(done[k], 'y', ring(SIDE, -k))]
    ppermute x1, waiting for transfers between devices: 5.86 us -> 9.23 us  [body(): far = lax.ppermute(near_half, cy, twin_ring())]
  transfers between devices with their start and end apart: 29 -> 23, of which waited for: 20 -> 14; matrix products, arithmetic and copies ran while one was open for 0% -> 0% of each run, Pallas kernels for 12% -> 13%
where the time goes in v1:
time: 201 us
  waiting for transfers between devices  68.9 us (34%)
  Pallas kernels  47.4 us (24%)
  starting transfers between devices  33.5 us (17%)
  blocking collectives  32.9 us (16%)
  between operations  14.2 us (7%)
  local copies, waits for them, and re-layouts  3.64 us (2%)
    all_to_all x1, blocking collectives, body(): parts = lax.all_to_all(parts, ('y', 'x'), 0, 0, tiled=True)  32.9 us
    ppermute x3, waiting for transfers between devices, body(): lax.ppermute(column, 'x', ring(SIDE, m))  20.2 us
    ppermute x3, waiting for transfers between devices, body(): lax.ppermute(blocks[k], 'y', ring(SIDE, k))  15.7 us
    pallas_call x1, Pallas kernels, body(): call(mlp_kernel, [shape((16, 32, 2048))], [SMEM] + [VMEM] * 2 + [ANY] * 3...  13.5 us
    ppermute x3, waiting for transfers between devices, body(): lax.ppermute(mine_far, 'x', ring(SIDE, m))  10.9 us
    pallas_call x1, Pallas kernels, body(): call(merge_kernel, [shape((512, 2048)), shape((128, 2048), F32)], [SMEM]...  10.5 us
    ppermute x1, waiting for transfers between devices, body(): far = lax.ppermute(near_half, cy, twin_ring())  9.23 us
    ppermute x3, waiting for transfers between devices, body(): lax.ppermute(pairs[m], 'z', ring(SIDE, m))  8.12 us
  transfers between devices with their start and end apart: 23, of which 14 were waited for; matrix products, arithmetic and copies ran while one was open for 0% of the time, Pallas kernels for 13%

profile of v1, /device:TPU:1, one launch (start us, length us, event | category | flops | bytes accessed | tf_op | source)
XLA Modules:
  0.0 200.6 jit_solution(7693429596608753155)
XLA Ops:
  6.6 0.7 copy-done.2
  7.3 1.0 copy-done.4
  8.3 0.9 shard_map.100
  9.2 0.7 copy-done
  9.9 1.7 shard_map.101
  11.6 2.2 %collective-permute-start = (bf16[1024,512]{1,0:T(8,128)(2,1)S(1)}, bf16[1024,512]{1,0:T(8,128)(2,1)S(1)}, u32[]{:S(2)}, u32[]{:S(2)}) collective-permute-start(bf16[1024,512]{1,0:T(8,128)(2,1)S(1)} %shard_map.101), channel_id=1, source_target_pairs={{0,12},{4,0},{8,4},{12,8},{16,20},{20,24},{24,28},{28,16},{1,13},{... | collective-permute-start | bytes 3145736 | tf_op jit(solution)/shard_map/ppermute | solution.py:374
  13.8 1.3 collective-permute-start.1
  15.1 1.4 collective-permute-start.2
  16.5 2.0 collective-permute-start.3
  18.5 13.1 %collective-permute-done.1 = bf16[32,2048]{1,0:T(8,128)(2,1)S(1)} collective-permute-done((bf16[32,2048]{1,0:T(8,128)(2,1)S(1)}, bf16[32,2048]{1,0:T(8,128)(2,1)S(1)}, u32[]{:S(2)}, u32[]{:S(2)}) %collective-permute-start.1) | collective-permute-done | bytes 131104 | tf_op jit(solution)/shard_map/ppermute | solution.py:366
  31.7 2.6 %collective-permute-done.2 = bf16[32,2048]{1,0:T(8,128)(2,1)S(1)} collective-permute-done((bf16[32,2048]{1,0:T(8,128)(2,1)S(1)}, bf16[32,2048]{1,0:T(8,128)(2,1)S(1)}, u32[]{:S(2)}, u32[]{:S(2)}) %collective-permute-start.2) | collective-permute-done | bytes 131104 | tf_op jit(solution)/shard_map/ppermute | solution.py:366
  34.3 0.6 shard_map.108
  35.0 9.2 %collective-permute-done.17.far_ref = bf16[512,512]{1,0:T(8,128)(2,1)S(1)} collective-permute-done((bf16[512,512]{1,0:T(8,128)(2,1)S(1)}, bf16[512,512]{1,0:T(8,128)(2,1)S(1)}, u32[]{:S(2)}, u32[]{:S(2)}) %collective-permute-start.17) | collective-permute-done | bytes 524320 | tf_op jit(solution)/shard_map/ppermute | solution.py:378
  44.2 1.3 shard_map.109
  45.5 1.3 collective-permute-start.4
  46.8 2.5 %collective-permute-start.5 = (bf16[128,2048]{1,0:T(8,128)(2,1)S(1)}, bf16[128,2048]{1,0:T(8,128)(2,1)S(1)}, u32[]{:S(2)}, u32[]{:S(2)}) collective-permute-start(bf16[128,2048]{1,0:T(8,128)(2,1)S(1)} %pad_maximum_fusion.a0), channel_id=1, source_target_pairs={{0,2},{1,3},{2,0},{3,1},{4,6},{5,7},{6,4},{7,5},{8,10},{9,11},{10,... | collective-permute-start | bytes 1572872 | tf_op jit(solution)/shard_map/ppermute | solution.py:381
  49.2 1.2 collective-permute-start.6
  51.3 7.9 %collective-permute-done.4.a1 = bf16[128,2048]{1,0:T(8,128)(2,1)S(1)} collective-permute-done((bf16[128,2048]{1,0:T(8,128)(2,1)S(1)}, bf16[128,2048]{1,0:T(8,128)(2,1)S(1)}, u32[]{:S(2)}, u32[]{:S(2)}) %collective-permute-start.4) | collective-permute-done | bytes 524320 | tf_op jit(solution)/shard_map/ppermute | solution.py:381
  59.2 12.2 %collective-permute-done.5.a2 = bf16[128,2048]{1,0:T(8,128)(2,1)S(1)} collective-permute-done((bf16[128,2048]{1,0:T(8,128)(2,1)S(1)}, bf16[128,2048]{1,0:T(8,128)(2,1)S(1)}, u32[]{:S(2)}, u32[]{:S(2)}) %collective-permute-start.5) | collective-permute-done | bytes 524320 | tf_op jit(solution)/shard_map/ppermute | solution.py:381
  71.4 2.1 %shard_map.103.xn = bf16[512,2048]{1,0:T(8,128)(2,1)} custom-call(bf16[128,2048]{1,0:T(8,128)(2,1)S(1)} %pad_maximum_fusion.a0, bf16[128,2048]{1,0:T(8,128)(2,1)S(1)} %collective-permute-done.4.a1, bf16[128,2048]{1,0:T(8,128)(2,1)S(1)} %collective-permute-done.5.a2, bf16[128,2048]{1,0:T(8,128)(2,1)S(1)} %collective-permute-done.6.a3, f32[1,2048]{1,0:T(1,128)S(1)} %bitcast.8), custom_call_target="tpu_custom_call" | custom-call | flops 24999999488 | tf_op jit(solution)/shard_map/pallas_call | solution.py:391
  73.6 0.6 shard_map.104
  74.3 5.0 %collective-permute-start.12 = (bf16[2064,384]{1,0:T(8,128)(2,1)S(1)}, bf16[2064,384]{1,0:T(8,128)(2,1)S(1)}, u32[]{:S(2)}, u32[]{:S(2)}) collective-permute-start(bf16[2064,384]{1,0:T(8,128)(2,1)S(1)} %collective-permute-done.7.got_ref.wq1), channel_id=1, source_target_pairs={{0,16},{16,0},{1,17},{17,1},{2,18},{18,2},{3,19},{19,3},{4,20},{20... | collective-permute-start | bytes 4755464 | tf_op jit(solution)/shard_map/ppermute | solution.py:395
  79.3 6.4 %shard_map.105.o0 = bf16[512,256]{1,0:T(8,128)(2,1)S(1)} custom-call(s32[4]{0:T(128)S(1)} %pad_add_fusion.where_ref, s32[1,8]{1,0:T(1,128)S(1)} %copy-done.3, s32[1,16]{1,0:T(1,128)S(1)} %copy-done.8, bf16[512,2048]{1,0:T(8,128)(2,1)} %shard_map.103.xn, bf16[2064,384]{1,0:T(8,128)(2,1)S(1)} %shard_map.102.wq0, ...), custom_call_target="tpu_custom_call" | custom-call | flops 2000000000 | bytes 8388608 | tf_op jit(solution)/shard_map/pallas_call | solution.py:399
  85.7 1.1 collective-permute-done.8.wqa
  86.8 2.1 %collective-permute-start.13 = (bf16[1040,384]{1,0:T(8,128)(2,1)S(1)}, bf16[1040,384]{1,0:T(8,128)(2,1)S(1)}, u32[]{:S(2)}, u32[]{:S(2)}) collective-permute-start(bf16[1040,384]{1,0:T(8,128)(2,1)S(1)} %collective-permute-done.8.wqa), channel_id=1, source_target_pairs={{0,16},{16,0},{1,17},{17,1},{2,18},{18,2},{3,19},{19,3},{4,20},{20... | collective-permute-start | bytes 2396168 | tf_op jit(solution)/shard_map/ppermute | solution.py:408
  88.9 1.7 collective-permute-start.10
  90.7 1.1 collective-permute-start.11
  91.8 0.4 collective-permute-start.9
  92.2 6.4 %shard_map.106.f0 = bf16[512,256]{1,0:T(8,128)(2,1)S(1)} custom-call(s32[4]{0:T(128)S(1)} %pad_add_fusion.where_ref, s32[1,8]{1,0:T(1,128)S(1)} %copy-done.3, s32[1,16]{1,0:T(1,128)S(1)} %copy-done.8, bf16[512,2048]{1,0:T(8,128)(2,1)} %shard_map.103.xn, bf16[2064,384]{1,0:T(8,128)(2,1)S(1)} %collective-permute-done.12.wq2, ...), custom_call_target="tpu_custom_call" | custom-call | flops 2000000000 | bytes 8388608 | tf_op jit(solution)/shard_map/pallas_call | solution.py:409
  99.0 3.2 %collective-permute-start.15 = (bf16[512,256]{1,0:T(8,128)(2,1)S(1)}, bf16[512,256]{1,0:T(8,128)(2,1)S(1)}, u32[]{:S(2)}, u32[]{:S(2)}) collective-permute-start(bf16[512,256]{1,0:T(8,128)(2,1)S(1)} %shard_map.106.f0), channel_id=1, source_target_pairs={{0,2},{1,3},{2,0},{3,1},{4,6},{5,7},{6,4},{7,5},{8,10},{9,11},{10,... | collective-permute-start | bytes 786440 | tf_op jit(solution)/shard_map/ppermute | solution.py:423
  102.1 0.5 collective-permute-done.11.o3
  102.6 1.8 collective-permute-done.9.o1
  104.4 5.9 %collective-permute-done.14.f1 = bf16[512,256]{1,0:T(8,128)(2,1)S(1)} collective-permute-done((bf16[512,256]{1,0:T(8,128)(2,1)S(1)}, bf16[512,256]{1,0:T(8,128)(2,1)S(1)}, u32[]{:S(2)}, u32[]{:S(2)}) %collective-permute-start.14) | collective-permute-done | bytes 262176 | tf_op jit(solution)/shard_map/ppermute | solution.py:423
  110.3 5.0 %collective-permute-done.15.f2 = bf16[512,256]{1,0:T(8,128)(2,1)S(1)} collective-permute-done((bf16[512,256]{1,0:T(8,128)(2,1)S(1)}, bf16[512,256]{1,0:T(8,128)(2,1)S(1)}, u32[]{:S(2)}, u32[]{:S(2)}) %collective-permute-start.15) | collective-permute-done | bytes 262176 | tf_op jit(solution)/shard_map/ppermute | solution.py:423
  115.3 10.5 %shard_map.107 = (bf16[512,2048]{1,0:T(8,128)(2,1)}, f32[128,2048]{1,0:T(8,128)}) custom-call(s32[4]{0:T(128)S(1)} %pad_add_fusion.where_ref, bf16[128,2048]{1,0:T(8,128)(2,1)S(1)} %pad_maximum_fusion.a0, bf16[128,2048]{1,0:T(8,128)(2,1)S(1)} %collective-permute-done.4.a1, bf16[128,2048]{1,0:T(8,128)(2,1)S(1)} %collective-permute-done.5.a2, ...), custom_call_target="tpu_custom_call" | custom-call | flops 24999999488 | bytes 14680064 | tf_op jit(solution)/shard_map/pallas_call | solution.py:424
  125.8 1.2 copy-done.9
  127.0 13.5 %shard_map.110 = bf16[16,32,2048]{2,1,0:T(8,128)(2,1)S(1)} custom-call(s32[4]{0:T(128)S(1)} %pad_add_fusion.where_ref, bf16[512,2048]{1,0:T(8,128)(2,1)} %get-tuple-element.38.fed_ref, f32[128,2048]{1,0:T(8,128)S(1)} %copy-done.9, bf16[2048,512]{1,0:T(8,128)(2,1)} %w1_ref.2, bf16[512,2048]{1,0:T(8,128)(2,1)} %w2_ref.2, bf16[8,1536,512]{2,1,0:T(8,128)(2,1)} %bitcast.10), custom_call_target="tpu_custom_call" | custom-call | flops 8999999488 | bytes 20971520 | tf_op jit(solution)/shard_map/pallas_call | solution.py:433
  140.5 32.9 %all_to_all.5.parts_ref = bf16[16,32,2048]{2,1,0:T(8,128)(2,1)S(1)} all-to-all(bf16[16,32,2048]{2,1,0:T(8,128)(2,1)S(1)} %shard_map.110), channel_id=1, replica_groups=mesh['z'=4,'c'=2,'y'=4,'x'=4] {'y','x'}, dimensions={0} | all-to-all | bytes 4194304 | tf_op jit(solution)/shard_map/all_to_all | solution.py:446
  173.3 1.2 shard_map.111
  174.6 2.0 %collective-permute-start.18 = (bf16[4,24,2048]{2,1,0:T(8,128)(2,1)S(1)}, bf16[4,24,2048]{2,1,0:T(8,128)(2,1)S(1)}, u32[]{:S(2)}, u32[]{:S(2)}) collective-permute-start(bf16[4,24,2048]{2,1,0:T(8,128)(2,1)S(1)} %get-tuple-element.42), channel_id=1, source_target_pairs={{0,16},{16,0},{1,17},{17,1},{2,18},{18,2},{3,19},{19,3},{4,20},{20... | collective-permute-start | bytes 1179656 | tf_op jit(solution)/shard_map/ppermute | solution.py:450
  176.6 1.3 collective-permute-done.18.cross_ref
  177.9 0.6 shard_map.112
  178.5 1.6 collective-permute-start.19
  180.1 3.2 %collective-permute-start.20 = (bf16[2,24,2048]{2,1,0:T(8,128)(2,1)S(1)}, bf16[2,24,2048]{2,1,0:T(8,128)(2,1)S(1)}, u32[]{:S(2)}, u32[]{:S(2)}) collective-permute-start(bf16[2,24,2048]{2,1,0:T(8,128)(2,1)S(1)} %get-tuple-element.45), channel_id=1, source_target_pairs={{0,64},{32,96},{64,0},{96,32},{1,65},{33,97},{65,1},{97,33},{2,66}... | collective-permute-start | bytes 589832 | tf_op jit(solution)/shard_map/ppermute | solution.py:452
  183.4 0.7 collective-permute-start.21
  184.1 3.0 %collective-permute-done.19.g1 = bf16[2,24,2048]{2,1,0:T(8,128)(2,1)S(1)} collective-permute-done((bf16[2,24,2048]{2,1,0:T(8,128)(2,1)S(1)}, bf16[2,24,2048]{2,1,0:T(8,128)(2,1)S(1)}, u32[]{:S(2)}, u32[]{:S(2)}) %collective-permute-start.19) | collective-permute-done | bytes 196640 | tf_op jit(solution)/shard_map/ppermute | solution.py:452
  187.2 5.1 %collective-permute-done.20.g2 = bf16[2,24,2048]{2,1,0:T(8,128)(2,1)S(1)} collective-permute-done((bf16[2,24,2048]{2,1,0:T(8,128)(2,1)S(1)}, bf16[2,24,2048]{2,1,0:T(8,128)(2,1)S(1)}, u32[]{:S(2)}, u32[]{:S(2)}) %collective-permute-start.20) | collective-permute-done | bytes 196640 | tf_op jit(solution)/shard_map/ppermute | solution.py:452
  192.2 1.5 shard_map.113
  (36 shorter events, 1.0 us)
Async XLA Ops:
  6.5 119.2 %all-gather.3.cloned.1.call-start = ((), (), s32[]{:S(2)}) async-start(), calls=%async_computation.1 | async-start | bytes 14155776 | tf_op jit(solution)/shard_map/all_gather | solution.py:389
  6.6 0.7 copy-start.2
  7.3 1.0 copy-start.4
  8.3 1.6 copy-start
  11.6 22.7 %collective-permute-start = (bf16[1024,512]{1,0:T(8,128)(2,1)S(1)}, bf16[1024,512]{1,0:T(8,128)(2,1)S(1)}, u32[]{:S(2)}, u32[]{:S(2)}) collective-permute-start(bf16[1024,512]{1,0:T(8,128)(2,1)S(1)} %shard_map.101), channel_id=1, source_target_pairs={{0,12},{4,0},{8,4},{12,8},{16,20},{20,24},{24,28},{28,16},{1,13},{... | collective-permute-start | bytes 3145736 | tf_op jit(solution)/shard_map/ppermute | solution.py:374
  13.8 17.8 %collective-permute-start.1 = (bf16[32,2048]{1,0:T(8,128)(2,1)S(1)}, bf16[32,2048]{1,0:T(8,128)(2,1)S(1)}, u32[]{:S(2)}, u32[]{:S(2)}) collective-permute-start(bf16[32,2048]{1,0:T(8,128)(2,1)S(1)} %get-tuple-element.26), channel_id=1, source_target_pairs={{0,4},{4,8},{8,12},{12,0},{1,5},{5,9},{9,13},{13,1},{2,6},{6,10},{... | collective-permute-start | bytes 393224 | tf_op jit(solution)/shard_map/ppermute | solution.py:366
  15.1 19.1 %collective-permute-start.2 = (bf16[32,2048]{1,0:T(8,128)(2,1)S(1)}, bf16[32,2048]{1,0:T(8,128)(2,1)S(1)}, u32[]{:S(2)}, u32[]{:S(2)}) collective-permute-start(bf16[32,2048]{1,0:T(8,128)(2,1)S(1)} %get-tuple-element.30), channel_id=1, source_target_pairs={{0,8},{4,12},{8,0},{12,4},{1,9},{5,13},{9,1},{13,5},{2,10},{6,14},... | collective-permute-start | bytes 393224 | tf_op jit(solution)/shard_map/ppermute | solution.py:366
  16.5 17.7 %collective-permute-start.3 = (bf16[32,2048]{1,0:T(8,128)(2,1)S(1)}, bf16[32,2048]{1,0:T(8,128)(2,1)S(1)}, u32[]{:S(2)}, u32[]{:S(2)}) collective-permute-start(bf16[32,2048]{1,0:T(8,128)(2,1)S(1)} %get-tuple-element.31), channel_id=1, source_target_pairs={{0,12},{4,0},{8,4},{12,8},{1,13},{5,1},{9,5},{13,9},{2,14},{6,2},{... | collective-permute-start | bytes 393224 | tf_op jit(solution)/shard_map/ppermute | solution.py:366
  34.9 16.2 %copy-start.1 = (bf16[2048,384]{1,0:T(8,128)(2,1)S(1)}, bf16[2048,384]{1,0:T(8,128)(2,1)}, u32[]{:S(2)}) copy-start(bf16[2048,384]{1,0:T(8,128)(2,1)} %wqkv_ref) | copy-start | bytes 4718596
  34.9 9.3 %collective-permute-start.17 = (bf16[512,512]{1,0:T(8,128)(2,1)S(1)}, bf16[512,512]{1,0:T(8,128)(2,1)S(1)}, u32[]{:S(2)}, u32[]{:S(2)}) collective-permute-start(bf16[512,512]{1,0:T(8,128)(2,1)S(1)} %shard_map.108), channel_id=1, source_target_pairs={{0,12},{4,0},{8,4},{12,8},{16,20},{20,24},{24,28},{28,16},{1,13},{... | collective-permute-start | bytes 1572872 | tf_op jit(solution)/shard_map/ppermute | solution.py:378
  45.5 26.0 %copy-start.6 = (f32[2048]{0:T(1024)S(1)}, f32[2048]{0:T(1024)}, u32[]{:S(2)}) copy-start(f32[2048]{0:T(1024)} %param.13) | copy-start | bytes 24580
  45.5 13.6 %collective-permute-start.4 = (bf16[128,2048]{1,0:T(8,128)(2,1)S(1)}, bf16[128,2048]{1,0:T(8,128)(2,1)S(1)}, u32[]{:S(2)}, u32[]{:S(2)}) collective-permute-start(bf16[128,2048]{1,0:T(8,128)(2,1)S(1)} %pad_maximum_fusion.a0), channel_id=1, source_target_pairs={{0,1},{1,2},{2,3},{3,0},{4,5},{5,6},{6,7},{7,4},{8,9},{9,10},{10,1... | collective-permute-start | bytes 1572872 | tf_op jit(solution)/shard_map/ppermute | solution.py:381
  46.8 24.6 %collective-permute-start.5 = (bf16[128,2048]{1,0:T(8,128)(2,1)S(1)}, bf16[128,2048]{1,0:T(8,128)(2,1)S(1)}, u32[]{:S(2)}, u32[]{:S(2)}) collective-permute-start(bf16[128,2048]{1,0:T(8,128)(2,1)S(1)} %pad_maximum_fusion.a0), channel_id=1, source_target_pairs={{0,2},{1,3},{2,0},{3,1},{4,6},{5,7},{6,4},{7,5},{8,10},{9,11},{10,... | collective-permute-start | bytes 1572872 | tf_op jit(solution)/shard_map/ppermute | solution.py:381
  49.2 22.2 %collective-permute-start.6 = (bf16[128,2048]{1,0:T(8,128)(2,1)S(1)}, bf16[128,2048]{1,0:T(8,128)(2,1)S(1)}, u32[]{:S(2)}, u32[]{:S(2)}) collective-permute-start(bf16[128,2048]{1,0:T(8,128)(2,1)S(1)} %pad_maximum_fusion.a0), channel_id=1, source_target_pairs={{0,3},{1,0},{2,1},{3,2},{4,7},{5,4},{6,5},{7,6},{8,11},{9,8},{10,9... | collective-permute-start | bytes 1572872 | tf_op jit(solution)/shard_map/ppermute | solution.py:381
  51.2 22.4 %collective-permute-start.7 = (bf16[2064,384]{1,0:T(8,128)(2,1)S(1)}, bf16[2064,384]{1,0:T(8,128)(2,1)S(1)}, u32[]{:S(2)}, u32[]{:S(2)}) collective-permute-start(bf16[2064,384]{1,0:T(8,128)(2,1)S(1)} %shard_map.102.wq0), channel_id=1, source_target_pairs={{0,12},{4,0},{8,4},{12,8},{16,20},{20,24},{24,28},{28,16},{1,13},{... | collective-permute-start | bytes 4755464 | tf_op jit(solution)/shard_map/ppermute | solution.py:388
  71.4 2.1 %copy-start.5 = (bf16[128,2048]{1,0:T(8,128)(2,1)}, bf16[128,2048]{1,0:T(8,128)(2,1)S(1)}, u32[]{:S(2)}) copy-start(bf16[128,2048]{1,0:T(8,128)(2,1)S(1)} %collective-permute-done.6.a3) | copy-start | bytes 1572868
  73.6 5.7 %copy-start.3 = (s32[1,8]{1,0:T(1,128)S(1)}, s32[1,8]{1,0:T(1,128)}, u32[]{:S(2)}) copy-start(s32[1,8]{1,0:T(1,128)} %count_ref.7) | copy-start | bytes 100
  73.6 5.7 %copy-start.8 = (s32[1,16]{1,0:T(1,128)S(1)}, s32[1,16]{1,0:T(1,128)}, u32[]{:S(2)}) copy-start(s32[1,16]{1,0:T(1,128)} %member_ref.3) | copy-start | bytes 196
  74.2 12.7 %collective-permute-start.8 = (bf16[1040,384]{1,0:T(8,128)(2,1)S(1)}, bf16[1040,384]{1,0:T(8,128)(2,1)S(1)}, u32[]{:S(2)}, u32[]{:S(2)}) collective-permute-start(bf16[1040,384]{1,0:T(8,128)(2,1)S(1)} %shard_map.104), channel_id=1, source_target_pairs={{0,12},{4,0},{8,4},{12,8},{16,20},{20,24},{24,28},{28,16},{1,13},{... | collective-permute-start | bytes 2396168 | tf_op jit(solution)/shard_map/ppermute | solution.py:397
  74.3 17.9 %collective-permute-start.12 = (bf16[2064,384]{1,0:T(8,128)(2,1)S(1)}, bf16[2064,384]{1,0:T(8,128)(2,1)S(1)}, u32[]{:S(2)}, u32[]{:S(2)}) collective-permute-start(bf16[2064,384]{1,0:T(8,128)(2,1)S(1)} %collective-permute-done.7.got_ref.wq1), channel_id=1, source_target_pairs={{0,16},{16,0},{1,17},{17,1},{2,18},{18,2},{3,19},{19,3},{4,20},{20... | collective-permute-start | bytes 4755464 | tf_op jit(solution)/shard_map/ppermute | solution.py:395
  85.7 29.6 %copy-start.7 = (f32[2048]{0:T(1024)S(1)}, f32[2048]{0:T(1024)}, u32[]{:S(2)}) copy-start(f32[2048]{0:T(1024)} %param.17) | copy-start | bytes 24580
  86.8 5.3 %collective-permute-start.13 = (bf16[1040,384]{1,0:T(8,128)(2,1)S(1)}, bf16[1040,384]{1,0:T(8,128)(2,1)S(1)}, u32[]{:S(2)}, u32[]{:S(2)}) collective-permute-start(bf16[1040,384]{1,0:T(8,128)(2,1)S(1)} %collective-permute-done.8.wqa), channel_id=1, source_target_pairs={{0,16},{16,0},{1,17},{17,1},{2,18},{18,2},{3,19},{19,3},{4,20},{20... | collective-permute-start | bytes 2396168 | tf_op jit(solution)/shard_map/ppermute | solution.py:408
  88.9 13.2 %collective-permute-start.10 = (bf16[512,256]{1,0:T(8,128)(2,1)S(1)}, bf16[512,256]{1,0:T(8,128)(2,1)S(1)}, u32[]{:S(2)}, u32[]{:S(2)}) collective-permute-start(bf16[512,256]{1,0:T(8,128)(2,1)S(1)} %shard_map.105.o0), channel_id=1, source_target_pairs={{0,2},{1,3},{2,0},{3,1},{4,6},{5,7},{6,4},{7,5},{8,10},{9,11},{10,... | collective-permute-start | bytes 786440 | tf_op jit(solution)/shard_map/ppermute | solution.py:422
  90.7 11.9 %collective-permute-start.11 = (bf16[512,256]{1,0:T(8,128)(2,1)S(1)}, bf16[512,256]{1,0:T(8,128)(2,1)S(1)}, u32[]{:S(2)}, u32[]{:S(2)}) collective-permute-start(bf16[512,256]{1,0:T(8,128)(2,1)S(1)} %shard_map.105.o0), channel_id=1, source_target_pairs={{0,3},{1,0},{2,1},{3,2},{4,7},{5,4},{6,5},{7,6},{8,11},{9,8},{10,9... | collective-permute-start | bytes 786440 | tf_op jit(solution)/shard_map/ppermute | solution.py:422
  91.8 12.6 %collective-permute-start.9 = (bf16[512,256]{1,0:T(8,128)(2,1)S(1)}, bf16[512,256]{1,0:T(8,128)(2,1)S(1)}, u32[]{:S(2)}, u32[]{:S(2)}) collective-permute-start(bf16[512,256]{1,0:T(8,128)(2,1)S(1)} %shard_map.105.o0), channel_id=1, source_target_pairs={{0,1},{1,2},{2,3},{3,0},{4,5},{5,6},{6,7},{7,4},{8,9},{9,10},{10,1... | collective-permute-start | bytes 786440 | tf_op jit(solution)/shard_map/ppermute | solution.py:422
  98.6 11.7 %collective-permute-start.14 = (bf16[512,256]{1,0:T(8,128)(2,1)S(1)}, bf16[512,256]{1,0:T(8,128)(2,1)S(1)}, u32[]{:S(2)}, u32[]{:S(2)}) collective-permute-start(bf16[512,256]{1,0:T(8,128)(2,1)S(1)} %shard_map.106.f0), channel_id=1, source_target_pairs={{0,1},{1,2},{2,3},{3,0},{4,5},{5,6},{6,7},{7,4},{8,9},{9,10},{10,1... | collective-permute-start | bytes 786440 | tf_op jit(solution)/shard_map/ppermute | solution.py:423
  99.0 16.3 %collective-permute-start.15 = (bf16[512,256]{1,0:T(8,128)(2,1)S(1)}, bf16[512,256]{1,0:T(8,128)(2,1)S(1)}, u32[]{:S(2)}, u32[]{:S(2)}) collective-permute-start(bf16[512,256]{1,0:T(8,128)(2,1)S(1)} %shard_map.106.f0), channel_id=1, source_target_pairs={{0,2},{1,3},{2,0},{3,1},{4,6},{5,7},{6,4},{7,5},{8,10},{9,11},{10,... | collective-permute-start | bytes 786440 | tf_op jit(solution)/shard_map/ppermute | solution.py:423
  102.1 13.1 %collective-permute-start.16 = (bf16[512,256]{1,0:T(8,128)(2,1)S(1)}, bf16[512,256]{1,0:T(8,128)(2,1)S(1)}, u32[]{:S(2)}, u32[]{:S(2)}) collective-permute-start(bf16[512,256]{1,0:T(8,128)(2,1)S(1)} %shard_map.106.f0), channel_id=1, source_target_pairs={{0,3},{1,0},{2,1},{3,2},{4,7},{5,4},{6,5},{7,6},{8,11},{9,8},{10,9... | collective-permute-start | bytes 786440 | tf_op jit(solution)/shard_map/ppermute | solution.py:423
  125.8 1.2 copy-start.9
  174.6 3.4 %collective-permute-start.18 = (bf16[4,24,2048]{2,1,0:T(8,128)(2,1)S(1)}, bf16[4,24,2048]{2,1,0:T(8,128)(2,1)S(1)}, u32[]{:S(2)}, u32[]{:S(2)}) collective-permute-start(bf16[4,24,2048]{2,1,0:T(8,128)(2,1)S(1)} %get-tuple-element.42), channel_id=1, source_target_pairs={{0,16},{16,0},{1,17},{17,1},{2,18},{18,2},{3,19},{19,3},{4,20},{20... | collective-permute-start | bytes 1179656 | tf_op jit(solution)/shard_map/ppermute | solution.py:450
  178.5 8.6 %collective-permute-start.19 = (bf16[2,24,2048]{2,1,0:T(8,128)(2,1)S(1)}, bf16[2,24,2048]{2,1,0:T(8,128)(2,1)S(1)}, u32[]{:S(2)}, u32[]{:S(2)}) collective-permute-start(bf16[2,24,2048]{2,1,0:T(8,128)(2,1)S(1)} %get-tuple-element.44), channel_id=1, source_target_pairs={{0,32},{32,64},{64,96},{96,0},{1,33},{33,65},{65,97},{97,1},{2,34}... | collective-permute-start | bytes 589832 | tf_op jit(solution)/shard_map/ppermute | solution.py:452
  180.1 12.1 %collective-permute-start.20 = (bf16[2,24,2048]{2,1,0:T(8,128)(2,1)S(1)}, bf16[2,24,2048]{2,1,0:T(8,128)(2,1)S(1)}, u32[]{:S(2)}, u32[]{:S(2)}) collective-permute-start(bf16[2,24,2048]{2,1,0:T(8,128)(2,1)S(1)} %get-tuple-element.45), channel_id=1, source_target_pairs={{0,64},{32,96},{64,0},{96,32},{1,65},{33,97},{65,1},{97,33},{2,66}... | collective-permute-start | bytes 589832 | tf_op jit(solution)/shard_map/ppermute | solution.py:452
  183.4 8.9 %collective-permute-start.21 = (bf16[2,24,2048]{2,1,0:T(8,128)(2,1)S(1)}, bf16[2,24,2048]{2,1,0:T(8,128)(2,1)S(1)}, u32[]{:S(2)}, u32[]{:S(2)}) collective-permute-start(bf16[2,24,2048]{2,1,0:T(8,128)(2,1)S(1)} %get-tuple-element.46), channel_id=1, source_target_pairs={{0,96},{32,0},{64,32},{96,64},{1,97},{33,1},{65,33},{97,65},{2,98}... | collective-permute-start | bytes 589832 | tf_op jit(solution)/shard_map/ppermute | solution.py:452
Sparse Core Ops, SparseCore 0:
  45.6 71.2 all-gather.2

commit v2 on v1

--- a/solution.py
+++ b/solution.py
@@ -40,14 +40,14 @@
     return jax.ShapeDtypeStruct(dims, dtype)
 
 
-def call(kernel, outs, ins, scratch=(), vmem=100, flops=0, moved=0):
+def call(kernel, outs, ins, scratch=(), vmem=6, flops=0, moved=0):
     return pl.pallas_call(
         kernel,
         out_shape=outs,
         in_specs=ins,
         out_specs=[VMEM] * len(outs),
         scratch_shapes=list(scratch),
-        compiler_params=pltpu.CompilerParams(vmem_limit_bytes=vmem * 2**20 // 2),
+        compiler_params=pltpu.CompilerParams(vmem_limit_bytes=vmem * 2**20),
         cost_estimate=pl.CostEstimate(flops=flops, bytes_accessed=moved, transcendentals=0),
     )
 
@@ -133,11 +133,6 @@
     copy.wait()
 
 
-def join_kernel(near_ref, far_ref, out_ref):
-    out_ref[:1024] = near_ref[...]
-    out_ref[1024:] = far_ref[...]
-
-
 def far_kernel(where_ref, got_ref, out_ref):
     out_ref[:1024] = got_ref[pl.ds(pl.multiple_of(where_ref[1] * 1024, 1024), 1024)]
     out_ref[1024:] = got_ref[2048:]
@@ -177,13 +172,19 @@
     return dot(p, v).astype(BF16)
 
 
-def norm_kernel(a0, a1, a2, a3, gain_ref, out_ref):
-    for j, ref in enumerate((a0, a1, a2, a3)):
-        values = ref[...].astype(F32)
+def norm_kernel(a0, a1, a2, a3, gain_ref, out_ref, kept_ref, sem):
+    copies = [
+        pltpu.make_async_copy(ref, kept_ref.at[pl.ds(128 * j, 128)], sem.at[j])
+        for j, ref in enumerate((a0, a1, a2, a3))
+    ]
+    for copy in copies:
+        copy.start()
+    for j, copy in enumerate(copies):
+        rows = slice(128 * j, 128 * j + 128)
+        copy.wait()
+        values = kept_ref[rows].astype(F32)
         mean_square = jnp.mean(values * values, axis=-1, keepdims=True)
-        out_ref[128 * j : 128 * j + 128] = (
-            values * lax.rsqrt(mean_square + EPS) * gain_ref[...]
-        ).astype(BF16)
+        out_ref[rows] = (values * lax.rsqrt(mean_square + EPS) * gain_ref[...]).astype(BF16)
 
 
 def near_kernel(where_ref, count_ref, member_ref, xn, wq0, wq1, out_ref, w0, w1, sem):
@@ -218,27 +219,52 @@
     out_ref[:, 128:] = attend(raw, w3[0, 1024:1025], allowed)
 
 
-def merge_kernel(
-    where_ref, a0, a1, a2, a3, o0, o1, o2, o3, f0, f1, f2, f3, gain_ref, wm, fed_ref, kept_ref,
-    heads, total,
-):
+def merge_part(where_ref, pair, refs, wm_ref, wm, heads, sem):
     c, y, x = where_ref[1], where_ref[2], where_ref[3]
     step = 1 - 2 * c
-    source = [y, (y + step + 4) & 3, (y - step + 4) & 3, (y + 2) & 3]
-    for m, (near, far) in enumerate(((o0, f0), (o1, f1), (o2, f2), (o3, f3))):
-        for k in range(SIDE):
+    source = ([y, (y + step + 4) & 3], [(y - step + 4) & 3, (y + 2) & 3])[pair]
+    copies = []
+    for m in range(SIDE):
+        for k in range(2):
             head = source[k] * SIDE + ((x - m + 4) & 3)
-            cols = pl.ds(pl.multiple_of(head * HEAD_DIM, HEAD_DIM), HEAD_DIM)
-            for j in range(SIDE):
-                theirs = slice(128 * ((j - m) % SIDE), 128 * ((j - m) % SIDE) + 128)
-                block = (near, far)[k // 2][theirs, 128 * (k % 2) : 128 * (k % 2) + 128]
-                heads[128 * j : 128 * j + 128, cols] = block
+            copies.append(
+                pltpu.make_async_copy(
+                    wm_ref.at[pl.ds(pl.multiple_of(head * HEAD_DIM, HEAD_DIM), HEAD_DIM)],
+                    wm.at[pl.ds(256 * m + HEAD_DIM * k, HEAD_DIM)],
+                    sem.at[2 * m + k],
+                )
+            )
+    for copy in copies:
+        copy.start()
+    for m, ref in enumerate(refs):
+        for j in range(SIDE):
+            theirs = 128 * ((j - m) % SIDE)
+            heads[128 * j : 128 * j + 128, 256 * m : 256 * m + 256] = ref[theirs : theirs + 128]
+    for copy in copies:
+        copy.wait()
+
+
+def merge_first_kernel(where_ref, o0, o1, o2, o3, rows_ref, wm_ref, out_ref, wm, heads, rows, sem):
+    carried = pltpu.make_async_copy(rows_ref, rows, sem.at[8])
+    carried.start()
+    merge_part(where_ref, 0, (o0, o1, o2, o3), wm_ref, wm, heads, sem)
+    carried.wait()
+    for n in range(4):
+        cols = slice(512 * n, 512 * n + 512)
+        out_ref[:, cols] = dot(heads[...], wm[:, cols]) + rows[:, cols].astype(F32)
+
+
+def merge_kernel(
+    where_ref, f0, f1, f2, f3, gain_ref, part_ref, wm_ref, fed_ref, kept_ref, wm, heads, total, sem
+):
+    carried = pltpu.make_async_copy(part_ref, total, sem.at[8])
+    carried.start()
+    merge_part(where_ref, 1, (f0, f1, f2, f3), wm_ref, wm, heads, sem)
+    carried.wait()
     squares = jnp.zeros((512, 1), F32)
     for n in range(4):
         cols = slice(512 * n, 512 * n + 512)
-        part = dot(heads[...], wm[:, cols])
-        arrived = jnp.concatenate([ref[:, cols] for ref in (a0, a1, a2, a3)], 0)
-        part = part + arrived.astype(F32)
+        part = dot(heads[...], wm[:, cols]) + total[:, cols]
         squares = squares + jnp.sum(part * part, axis=-1, keepdims=True)
         total[:, cols] = part
     scale = lax.rsqrt(squares * (1.0 / 2048) + EPS)
@@ -248,63 +274,79 @@
     kept_ref[...] = total[:128]
 
 
-def mlp_kernel(
-    where_ref, fed_ref, kept_ref, w1_ref, w2_ref, all_ref, out_ref, w1, w2, hidden, sem
+def near_mlp_kernel(fed_ref, w1_ref, all_ref, out_ref, w1, sem):
+    copies = [[pltpu.make_async_copy(w1_ref, w1.at[0], sem.at[0])]]
+    for c in range(2):
+        copies.append(
+            [
+                pltpu.make_async_copy(
+                    all_ref.at[2 * z + c, pl.ds(0, 512)],
+                    w1.at[1 + c, pl.ds(512 * z, 512)],
+                    sem.at[1 + c],
+                )
+                for z in range(4)
+            ]
+        )
+    for group in copies:
+        for copy in group:
+            copy.start()
+    for i in range(3):
+        for copy in copies[i]:
+            copy.wait()
+        out_ref[:, 512 * i : 512 * i + 512] = jax.nn.gelu(
+            dot(fed_ref[...], w1[i]), approximate=True
+        ).astype(BF16)
+
+
+def far_mlp_kernel(
+    where_ref, fed_ref, kept_ref, hidden_ref, w2_ref, near_ref, far_ref, out_ref,
+    w1, w2, hidden, kept, sem,
 ):
-    copies = [
-        [pltpu.make_async_copy(w1_ref, w1.at[0], sem.at[0])],
-        [pltpu.make_async_copy(w2_ref, w2.at[pl.ds(0, 512)], sem.at[1])],
-    ]
-    for c in range(2):
-        up, down = [], []
-        for z in range(4):
-            block = all_ref.at[2 * z + c]
-            up.append(
+    ups, downs = [], []
+    for z in range(4):
+        for c in range(2):
+            block = far_ref.at[2 * z + c]
+            ups.append(
                 pltpu.make_async_copy(
-                    block.at[pl.ds(0, 512)], w1.at[1 + c, pl.ds(512 * z, 512)], sem.at[2 + 2 * c]
+                    block.at[pl.ds(0, 256)], w1.at[pl.ds(512 * z + 256 * c, 256)], sem.at[0]
                 )
             )
-            for q in range(4):
+    carried = [
+        pltpu.make_async_copy(hidden_ref, hidden.at[:, pl.ds(0, 1536)], sem.at[1]),
+        pltpu.make_async_copy(kept_ref, kept, sem.at[1]),
+    ]
+    for n in range(4):
+        cols = pl.ds(512 * n, 512)
+        down = [pltpu.make_async_copy(w2_ref.at[:, cols], w2.at[pl.ds(0, 512), cols], sem.at[2 + n])]
+        for c in range(2):
+            for z in range(4):
                 down.append(
                     pltpu.make_async_copy(
-                        block.at[pl.ds(512 + 128 * q, 128)],
-                        w2.at[pl.ds(512 * (1 + c) + 128 * z, 128), pl.ds(512 * q, 512)],
-                        sem.at[3 + 2 * c],
+                        near_ref.at[2 * z + c, pl.ds(512 + 128 * n, 128)],
+                        w2.at[pl.ds(512 * (1 + c) + 128 * z, 128), cols],
+                        sem.at[2 + n],
                     )
                 )
-        copies += [up, down]
-    up, down = [], []
-    for z in range(4):
-        for c in range(2):
-            block = all_ref.at[2 * z + c, pl.ds(1024, 512)]
-            up.append(
-                pltpu.make_async_copy(
-                    block.at[pl.ds(0, 256)], w1.at[3, pl.ds(512 * z + 256 * c, 256)], sem.at[6]
-                )
-            )
-            for q in range(4):
                 down.append(
                     pltpu.make_async_copy(
-                        block.at[pl.ds(256 + 64 * q, 64)],
-                        w2.at[pl.ds(1536 + 128 * z + 64 * c, 64), pl.ds(512 * q, 512)],
-                        sem.at[7],
+                        far_ref.at[2 * z + c, pl.ds(256 + 64 * n, 64)],
+                        w2.at[pl.ds(1536 + 128 * z + 64 * c, 64), cols],
+                        sem.at[2 + n],
                     )
                 )
-    copies += [up, down]
-    for i in (0, 2, 4, 6, 1, 3, 5, 7):
-        for copy in copies[i]:
+        downs.append(down)
+    for copies in [ups, carried, *downs]:
+        for copy in copies:
             copy.start()
-    for i in range(SIDE):
-        for copy in copies[2 * i]:
-            copy.wait()
-        hidden[:, 512 * i : 512 * i + 512] = jax.nn.gelu(
-            dot(fed_ref[...], w1[i]), approximate=True
-        ).astype(BF16)
-    for i in range(SIDE):
-        for copy in copies[2 * i + 1]:
-            copy.wait()
+    for copy in ups:
+        copy.wait()
+    hidden[:, 1536:] = jax.nn.gelu(dot(fed_ref[...], w1[...]), approximate=True).astype(BF16)
+    for copy in carried:
+        copy.wait()
     for n in range(4):
         cols = slice(512 * n, 512 * n + 512)
+        for copy in downs[n]:
+            copy.wait()
         part = dot(hidden[...], w2[:, cols])
         for j in range(SIDE):
             for k in range(SIDE):
@@ -312,12 +354,12 @@
                 home = ((where_ref[2] - k + 4) & 3) * SIDE + ((where_ref[3] - j + 4) & 3)
                 block = part[rows]
                 if j == 0:
-                    block = block + kept_ref[rows, cols]
+                    block = block + kept[rows, cols]
                 out_ref[home, :, cols] = block.astype(BF16)
 
 
-def leave_kernel(where_ref, count_ref, parts_ref, stay_ref, cross_ref):
-    z, c = where_ref[0], where_ref[1]
+def leave_kernel(where_ref, count_ref, parts_ref, *outs):
+    group = 2 * where_ref[0] + where_ref[1]
     count, _, start = placement(count_ref, 0)
     slot = lax.broadcasted_iota(jnp.int32, (192, 1), 0)
     block = slot // CAP
@@ -331,26 +373,18 @@
     home = jnp.concatenate(rows, 0)
     target = jnp.full((192, 1), -1, jnp.int32)
     for d in range(N_DP):
-        turn = ((d >> 1) - z + 4) & 3
-        index = jnp.where((d & 1) == c, turn, 4 + turn)
-        here = (block == index) & (inner < UNIT * count[d])
+        here = (block == ((d - group + N_DP) & 7)) & (inner < UNIT * count[d])
         target = jnp.where(here, UNIT * start[d] + inner, target)
     select = (target == lax.broadcasted_iota(jnp.int32, (192, 128), 1)).astype(F32).astype(BF16)
     moved = dot(select, home).astype(BF16).reshape(8, CAP, -1)
-    stay_ref[...] = moved[:4]
-    cross_ref[...] = moved[4:]
-
-
-def pair_kernel(where_ref, stay_ref, cross_ref, *outs):
-    c = where_ref[1]
-    for m in range(SIDE):
-        outs[m][c] = stay_ref[m]
-        outs[m][1 - c] = cross_ref[m]
-
-
-def order_kernel(where_ref, g0, g1, g2, g3, out_ref):
-    for m, ref in enumerate((g0, g1, g2, g3)):
-        out_ref[pl.ds(2 * ((where_ref[0] - m + 4) & 3), 2)] = ref[...]
+    for m, out in enumerate(outs):
+        out[...] = moved[m]
+
+
+def order_kernel(where_ref, *refs):
+    group = 2 * where_ref[0] + where_ref[1]
+    for m, ref in enumerate(refs[:-1]):
+        refs[-1][(group - m + N_DP) & 7] = ref[...]
 
 
 def body(tokens, tallies, membership, gain1, wqkv, sharp, wmerge, gain2, w1, w2):
@@ -373,12 +407,11 @@
     )(where, w1_later, w2_later)
     near = lax.ppermute(mlp_slice, cy, twin_ring())
     column = jnp.concatenate(came, 0)
-    near, column = lax.optimization_barrier((near, column))
+    arrived = [column] + [lax.ppermute(column, "x", ring(SIDE, m)) for m in (1, 2, 3)]
+    near, _ = lax.optimization_barrier((near, column))
+    near_all = lax.all_gather(near, DP, axis=0, tiled=False)
     [near_half] = call(half_kernel, [shape((512, 512))], [SMEM, VMEM])(where, near)
     far = lax.ppermute(near_half, cy, twin_ring())
-    [both] = call(join_kernel, [shape((1536, 512))], [VMEM] * 2)(near, far)
-
-    arrived = [column] + [lax.ppermute(column, "x", ring(SIDE, m)) for m in (1, 2, 3)]
     [packed] = call(
         pack_kernel,
         [shape((2064, 384))],
@@ -386,12 +419,15 @@
         [pltpu.SemaphoreType.DMA],
     )(sharp, lax.optimization_barrier((wqkv, column))[0])
     qkv_near = lax.ppermute(packed, cy, twin_ring())
-    both_all = lax.all_gather(both, DP, axis=0, tiled=False)
-
-    [normed] = call(norm_kernel, [shape((512, 2048))], [VMEM] * 5, flops=25 * 10**9)(
-        *arrived, gain1
-    )
-    qkv_near, normed = lax.optimization_barrier((qkv_near, normed))
+    gain1, qkv_near, far = lax.optimization_barrier((gain1, qkv_near, far))
+    normed, kept_rows = call(
+        norm_kernel,
+        [shape((512, 2048))] * 2,
+        [ANY] * 4 + [VMEM],
+        [pltpu.SemaphoreType.DMA((4,))],
+        vmem=12,
+        flops=25 * 10**9,
+    )(*arrived, gain1)
     qkv_near2 = lax.ppermute(qkv_near, "c", ring(2, 1))
     [qkv_half] = call(far_kernel, [shape((1040, 384))], [SMEM, VMEM])(where, qkv_near)
     qkv_far = lax.ppermute(qkv_half, cy, twin_ring())
@@ -401,10 +437,13 @@
         [shape((512, 256))],
         [SMEM] * 3 + [VMEM] + [ANY] * 2,
         [pltpu.VMEM((2064, 384), BF16)] * 2 + [pltpu.SemaphoreType.DMA((2,))],
+        vmem=20,
         flops=2 * 10**9,
         moved=8 * 2**20,
     )(where, tallies, membership, normed, packed, qkv_near)
     qkv_far, mine = lax.optimization_barrier((qkv_far, mine))
+    far, _ = lax.optimization_barrier((far, mine))
+    far_all = lax.all_gather(far, DP, axis=0, tiled=False)
     qkv_far2 = lax.ppermute(qkv_far, "c", ring(2, 1))
     [mine_far] = call(
         far_attention_kernel,
@@ -415,42 +454,65 @@
             pltpu.VMEM((2, 1040, 384), BF16),
             pltpu.SemaphoreType.DMA((3,)),
         ],
+        vmem=20,
         flops=2 * 10**9,
         moved=8 * 2**20,
     )(where, tallies, membership, normed, qkv_near2, qkv_far, qkv_far2)
 
-    attended = [mine] + [lax.ppermute(mine, "x", ring(SIDE, m)) for m in (1, 2, 3)]
-    attended += [mine_far] + [lax.ppermute(mine_far, "x", ring(SIDE, m)) for m in (1, 2, 3)]
+    first = [mine] + [lax.ppermute(mine, "x", ring(SIDE, m)) for m in (1, 2, 3)]
+    second = [mine_far] + [lax.ppermute(mine_far, "x", ring(SIDE, m)) for m in (1, 2, 3)]
+    scratch = [pltpu.VMEM((1024, 2048), BF16), pltpu.VMEM((512, 1024), BF16)]
+    [merged] = call(
+        merge_first_kernel,
+        [shape((512, 2048), F32)],
+        [SMEM] + [VMEM] * 4 + [ANY] * 2,
+        scratch + [pltpu.VMEM((512, 2048), BF16), pltpu.SemaphoreType.DMA((9,))],
+        vmem=60,
+        flops=2 * 10**9,
+        moved=12 * 2**20,
+    )(where, *first, kept_rows, wmerge)
+    second[0], near_all = lax.optimization_barrier((second[0], near_all))
     fed, kept = call(
         merge_kernel,
         [shape((512, 2048)), shape((128, 2048), F32)],
-        [SMEM] + [VMEM] * 14,
-        [pltpu.VMEM((512, 2048), BF16), pltpu.VMEM((512, 2048), F32)],
+        [SMEM] + [VMEM] * 5 + [ANY] * 2,
+        scratch + [pltpu.VMEM((512, 2048), F32), pltpu.SemaphoreType.DMA((9,))],
+        vmem=60,
         flops=25 * 10**9,
         moved=14 * 2**20,
-    )(where, *arrived, *attended, gain2, wmerge)
-
+    )(where, *second, gain2, merged, wmerge)
+
+    [near_hidden] = call(
+        near_mlp_kernel,
+        [shape((512, 1536))],
+        [VMEM] + [ANY] * 2,
+        [pltpu.VMEM((3, 2048, 512), BF16), pltpu.SemaphoreType.DMA((3,))],
+        vmem=60,
+        flops=4 * 10**9,
+        moved=10 * 2**20,
+    )(fed, w1, near_all)
     [parts] = call(
-        mlp_kernel,
+        far_mlp_kernel,
         [shape((16, 32, 2048))],
-        [SMEM] + [VMEM] * 2 + [ANY] * 3,
+        [SMEM, VMEM] + [ANY] * 5,
         [
-            pltpu.VMEM((4, 2048, 512), BF16),
+            pltpu.VMEM((2048, 512), BF16),
             pltpu.VMEM((2048, 2048), BF16),
             pltpu.VMEM((512, 2048), BF16),
-            pltpu.SemaphoreType.DMA((8,)),
+            pltpu.VMEM((128, 2048), F32),
+            pltpu.SemaphoreType.DMA((6,)),
         ],
-        flops=9 * 10**9,
-        moved=20 * 2**20,
-    )(where, fed, kept, w1, w2, both_all)
+        vmem=60,
+        flops=6 * 10**9,
+        moved=14 * 2**20,
+    )(where, fed, kept, near_hidden, w2, near_all, far_all)
     parts = lax.all_to_all(parts, ("y", "x"), 0, 0, tiled=True)
-    stay, cross = call(leave_kernel, [shape((4, CAP, 2048))] * 2, [SMEM, SMEM, VMEM])(
+    leaving = call(leave_kernel, [shape((CAP, 2048))] * 8, [SMEM, SMEM, VMEM], vmem=14)(
         where, tallies, parts
     )
-    crossed = lax.ppermute(cross, "c", ring(2, 1))
-    pairs = call(pair_kernel, [shape((2, CAP, 2048))] * 4, [SMEM] + [VMEM] * 2)(where, stay, crossed)
-    got = [pairs[0]] + [lax.ppermute(pairs[m], "z", ring(SIDE, m)) for m in (1, 2, 3)]
-    [out] = call(order_kernel, [shape((N_DP, CAP, 2048))], [SMEM] + [VMEM] * 4)(where, *got)
+    got = [leaving[0]]
+    got += [lax.ppermute(leaving[m], DP, ring(N_DP, m)) for m in range(1, N_DP)]
+    [out] = call(order_kernel, [shape((N_DP, CAP, 2048))], [SMEM] + [VMEM] * 8)(where, *got)
     return out.reshape(N_DP * CAP, -1)
 
 

time: 201 us -> 197 us (0.980)
  waiting for transfers between devices: 68.9 us -> 45.9 us
  Pallas kernels: 47.4 us -> 57.6 us
  local copies, waits for them, and re-layouts: 3.64 us -> 8.57 us
    ppermute x3, waiting for transfers between devices: 20.2 us -> 0.01 us  [body(): lax.ppermute(column, 'x', ring(SIDE, m))]
    pallas_call x6, Pallas kernels: 20.1 us -> 32.8 us  [the longest x1 10.9 us: body(): call(far_mlp_kernel, [shape((16, 32, 2048))], [SMEM, VMEM] + [ANY] * 5, [...]
    ppermute x1, waiting for transfers between devices: 9.23 us -> 20.9 us  [body(): far = lax.ppermute(near_half, cy, twin_ring())]
    ppermute x3, waiting for transfers between devices: 10.9 us -> 0.92 us  [body(): lax.ppermute(mine_far, 'x', ring(SIDE, m))]
    ppermute x7 -> x10, waiting for transfers between devices: 11.7 us -> 5.26 us  [the longest x7 5.25 us: body(): got += [lax.ppermute(leaving[m], DP, ring(N_DP, m)) for m in range(1, N_DP)]]
    ppermute x7 -> x10, starting transfers between devices: 10.8 us -> 16.3 us  [the longest x7 11.5 us: body(): got += [lax.ppermute(leaving[m], DP, ring(N_DP, m)) for m in range(1, N_DP)]]
    unnamed x20 -> x51, local copies, waits for them, and re-layouts: 3.64 us -> 8.56 us
    ppermute x1, starting transfers between devices: 5.02 us -> 1.46 us  [body(): qkv_near2 = lax.ppermute(qkv_near, 'c', ring(2, 1))]
  transfers between devices with their start and end apart: 23 -> 27, of which waited for: 14 -> 8; matrix products, arithmetic and copies ran while one was open for 0% -> 0% of each run, Pallas kernels for 13% -> 22%
where the time goes in v2:
time: 197 us; the launch traced here: 196 us
  Pallas kernels  57.6 us (29%)
  waiting for transfers between devices  45.9 us (23%)
  starting transfers between devices  34.8 us (18%)
  blocking collectives  34.8 us (18%)
  between operations  14.5 us (7%)
  local copies, waits for them, and re-layouts  8.57 us (4%)
    all_to_all x1, blocking collectives, body(): parts = lax.all_to_all(parts, ('y', 'x'), 0, 0, tiled=True)  34.8 us
    ppermute x1, waiting for transfers between devices, body(): far = lax.ppermute(near_half, cy, twin_ring())  20.9 us
    ppermute x3, waiting for transfers between devices, body(): lax.ppermute(blocks[k], 'y', ring(SIDE, k))  15.7 us
    ppermute x7, starting transfers between devices, body(): got += [lax.ppermute(leaving[m], DP, ring(N_DP, m)) for m in range(1, N_DP)]  11.5 us
    pallas_call x1, Pallas kernels, body(): call(far_mlp_kernel, [shape((16, 32, 2048))], [SMEM, VMEM] + [ANY] * 5, [...  10.9 us
    pallas_call x1, Pallas kernels, body(): call(merge_kernel, [shape((512, 2048)), shape((128, 2048), F32)], [SMEM]...  8.89 us
    pallas_call x1, Pallas kernels, body(): call(merge_first_kernel, [shape((512, 2048), F32)], [SMEM] + [VMEM] * 4 +...  8.88 us
    pallas_call x1, Pallas kernels, body(): call(near_mlp_kernel, [shape((512, 1536))], [VMEM] + [ANY] * 2, [pltpu.VM...  8.74 us
  transfers between devices with their start and end apart: 27, of which 8 were waited for; matrix products, arithmetic and copies ran while one was open for 0% of the time, Pallas kernels for 22%

profile of v2, /device:TPU:1, one launch (start us, length us, event | category | flops | bytes accessed | tf_op | source)
XLA Modules:
  0.0 196.3 jit_solution(16822202423616591866)
XLA Ops:
  6.6 0.7 copy-done.9
  7.3 1.0 copy-done.11
  8.3 0.9 shard_map.100
  9.2 0.7 copy-done.3
  9.9 0.6 copy-done.4
  10.5 0.7 shard_map.102
  11.3 2.2 %collective-permute-start.7 = (bf16[1024,512]{1,0:T(8,128)(2,1)S(1)}, bf16[1024,512]{1,0:T(8,128)(2,1)S(1)}, u32[]{:S(2)}, u32[]{:S(2)}) collective-permute-start(bf16[1024,512]{1,0:T(8,128)(2,1)S(1)} %shard_map.102), channel_id=1, source_target_pairs={{0,12},{4,0},{8,4},{12,8},{16,20},{20,24},{24,28},{28,16},{1,13},{... | collective-permute-start | bytes 3145736 | tf_op jit(solution)/shard_map/ppermute | solution.py:408
  13.5 1.3 collective-permute-start
  14.8 1.4 collective-permute-start.1
  16.2 2.0 %collective-permute-start.2 = (bf16[32,2048]{1,0:T(8,128)(2,1)S(1)}, bf16[32,2048]{1,0:T(8,128)(2,1)S(1)}, u32[]{:S(2)}, u32[]{:S(2)}) collective-permute-start(bf16[32,2048]{1,0:T(8,128)(2,1)S(1)} %get-tuple-element.36), channel_id=1, source_target_pairs={{0,12},{4,0},{8,4},{12,8},{1,13},{5,1},{9,5},{13,9},{2,14},{6,2},{... | collective-permute-start | bytes 393224 | tf_op jit(solution)/shard_map/ppermute | solution.py:400
  18.2 13.1 %collective-permute-done = bf16[32,2048]{1,0:T(8,128)(2,1)S(1)} collective-permute-done((bf16[32,2048]{1,0:T(8,128)(2,1)S(1)}, bf16[32,2048]{1,0:T(8,128)(2,1)S(1)}, u32[]{:S(2)}, u32[]{:S(2)}) %collective-permute-start) | collective-permute-done | bytes 131104 | tf_op jit(solution)/shard_map/ppermute | solution.py:400
  31.3 2.6 %collective-permute-done.1 = bf16[32,2048]{1,0:T(8,128)(2,1)S(1)} collective-permute-done((bf16[32,2048]{1,0:T(8,128)(2,1)S(1)}, bf16[32,2048]{1,0:T(8,128)(2,1)S(1)}, u32[]{:S(2)}, u32[]{:S(2)}) %collective-permute-start.1) | collective-permute-done | bytes 131104 | tf_op jit(solution)/shard_map/ppermute | solution.py:400
  33.9 1.0 copy-done
  35.7 1.3 shard_map.101.wq0
  38.2 1.2 collective-permute-start.3
  39.5 2.5 %collective-permute-start.4 = (bf16[128,2048]{1,0:T(8,128)(2,1)S(1)}, bf16[128,2048]{1,0:T(8,128)(2,1)}, u32[]{:S(2)}, u32[]{:S(2)}) collective-permute-start(bf16[128,2048]{1,0:T(8,128)(2,1)S(1)} %constant_dynamic-update-slice_fusion.a0), channel_id=1, source_target_pairs={{0,2},{1,3},{2,0},{3,1},{4,6},{5,7},{6,4},{7,5},{8,10},{9,11},{10,... | collective-permute-start | bytes 1572872 | tf_op jit(solution)/shard_map/ppermute | solution.py:410
  41.9 1.2 collective-permute-start.5
  43.1 20.9 %collective-permute-done.8 = bf16[512,512]{1,0:T(8,128)(2,1)S(1)} collective-permute-done((bf16[512,512]{1,0:T(8,128)(2,1)S(1)}, bf16[512,512]{1,0:T(8,128)(2,1)S(1)}, u32[]{:S(2)}, u32[]{:S(2)}) %collective-permute-start.8) | collective-permute-done | bytes 524320 | tf_op jit(solution)/shard_map/ppermute | solution.py:414
  64.7 1.6 shard_map.104
  66.4 1.3 copy-done.2
  67.7 6.5 %shard_map.106.o0 = bf16[512,256]{1,0:T(8,128)(2,1)S(1)} custom-call(s32[4]{0:T(128)S(1)} %pad_add_fusion.where_ref, s32[1,8]{1,0:T(1,128)S(1)} %copy-done.10, s32[1,16]{1,0:T(1,128)S(1)} %copy-done.14, bf16[512,2048]{1,0:T(8,128)(2,1)S(1)} %get-tuple-element.42.xn, bf16[2064,384]{1,0:T(8,128)(2,1)} %shard_map.101.wq0, ...), custom_call_target="tpu_custom_call" | custom-call | flops 2000000000 | bytes 8388608 | tf_op jit(solution)/shard_map/pallas_call | solution.py:435
  74.2 3.1 %collective-permute-done.10.wqa = bf16[1040,384]{1,0:T(8,128)(2,1)} collective-permute-done((bf16[1040,384]{1,0:T(8,128)(2,1)S(1)}, bf16[1040,384]{1,0:T(8,128)(2,1)}, u32[]{:S(2)}, u32[]{:S(2)}) %collective-permute-start.10) | collective-permute-done | bytes 798752 | tf_op jit(solution)/shard_map/ppermute | solution.py:433
  77.3 1.5 collective-permute-start.9
  78.8 1.2 collective-permute-start.15
  80.1 2.5 %collective-permute-start.16 = (bf16[512,256]{1,0:T(8,128)(2,1)S(1)}, bf16[512,256]{1,0:T(8,128)(2,1)S(1)}, u32[]{:S(2)}, u32[]{:S(2)}) collective-permute-start(bf16[512,256]{1,0:T(8,128)(2,1)S(1)} %shard_map.106.o0), channel_id=1, source_target_pairs={{0,2},{1,3},{2,0},{3,1},{4,6},{5,7},{6,4},{7,5},{8,10},{9,11},{10,... | collective-permute-start | bytes 786440 | tf_op jit(solution)/shard_map/ppermute | solution.py:462
  82.5 1.2 collective-permute-start.17
  83.7 1.6 copy-done.16
  85.3 5.3 %shard_map.107.f0 = bf16[512,256]{1,0:T(8,128)(2,1)S(1)} custom-call(s32[4]{0:T(128)S(1)} %pad_add_fusion.where_ref, s32[1,8]{1,0:T(1,128)S(1)} %copy-done.10, s32[1,16]{1,0:T(1,128)S(1)} %copy-done.14, bf16[512,2048]{1,0:T(8,128)(2,1)S(1)} %copy-done.16, bf16[2064,384]{1,0:T(8,128)(2,1)S(1)} %collective-permute-done.9.wq2, ...), custom_call_target="tpu_custom_call" | custom-call | flops 2000000000 | bytes 8388608 | tf_op jit(solution)/shard_map/pallas_call | solution.py:448
  90.6 1.0 collective-permute-start.12
  91.6 2.5 %collective-permute-start.13 = (bf16[512,256]{1,0:T(8,128)(2,1)S(1)}, bf16[512,256]{1,0:T(8,128)(2,1)S(1)}, u32[]{:S(2)}, u32[]{:S(2)}) collective-permute-start(bf16[512,256]{1,0:T(8,128)(2,1)S(1)} %shard_map.107.f0), channel_id=1, source_target_pairs={{0,2},{1,3},{2,0},{3,1},{4,6},{5,7},{6,4},{7,5},{8,10},{9,11},{10,... | collective-permute-start | bytes 786440 | tf_op jit(solution)/shard_map/ppermute | solution.py:463
  94.1 1.2 collective-permute-start.14
  95.3 0.7 copy-done.19
  96.0 8.9 %shard_map.108.part_ref = f32[512,2048]{1,0:T(8,128)} custom-call(s32[4]{0:T(128)} %copy-done.7, bf16[512,256]{1,0:T(8,128)(2,1)} %copy-done.6, bf16[512,256]{1,0:T(8,128)(2,1)} %copy-done.18, bf16[512,256]{1,0:T(8,128)(2,1)} %copy-done.19, bf16[512,256]{1,0:T(8,128)(2,1)} %copy-done.20, bf16[512,2048]{1,0:T(8,128)(2,1)} %copy-done.2, bf16[2048,2048]{1,0:T(8,128)(2,1)} %wm_ref.3), custom_call_target="tpu_custom_call" | custom-call | flops 2000000000 | bytes 12582912 | tf_op jit(solution)/shard_map/pallas_call | solution.py:465
  105.0 0.9 collective-permute-done.13.f2
  105.9 0.7 copy-done.22
  106.7 8.9 %shard_map.109 = (bf16[512,2048]{1,0:T(8,128)(2,1)}, f32[128,2048]{1,0:T(8,128)}) custom-call(s32[4]{0:T(128)} %copy-done.7, bf16[512,256]{1,0:T(8,128)(2,1)} %copy-done.12, bf16[512,256]{1,0:T(8,128)(2,1)} %copy-done.21, bf16[512,256]{1,0:T(8,128)(2,1)} %copy-done.22, bf16[512,256]{1,0:T(8,128)(2,1)} %copy-done.23, f32[1,2048]{1,0:T(1,128)} %bitcast.13, ...), custom_call_target="tpu_custom_call" | custom-call | flops 24999999488 | bytes 14680064 | tf_op jit(solution)/shard_map/pallas_call | solution.py:475
  115.6 8.7 %shard_map.110.hidden_ref = bf16[512,1536]{1,0:T(8,128)(2,1)} custom-call(bf16[512,2048]{1,0:T(8,128)(2,1)} %get-tuple-element.48.fed_ref, bf16[2048,512]{1,0:T(8,128)(2,1)} %w1_ref.2, bf16[8,1024,512]{2,1,0:T(8,128)(2,1)} %bitcast.10), custom_call_target="tpu_custom_call" | custom-call | flops 4000000000 | bytes 10485760 | tf_op jit(solution)/shard_map/pallas_call | solution.py:485
  124.4 10.9 %shard_map.111 = bf16[16,32,2048]{2,1,0:T(8,128)(2,1)} custom-call(s32[4]{0:T(128)} %copy-done.7, bf16[512,2048]{1,0:T(8,128)(2,1)} %get-tuple-element.48.fed_ref, f32[128,2048]{1,0:T(8,128)} %get-tuple-element.49.kept_ref, bf16[512,1536]{1,0:T(8,128)(2,1)} %shard_map.110.hidden_ref, bf16[512,2048]{1,0:T(8,128)(2,1)} %w2_ref.2, ...), custom_call_target="tpu_custom_call" | custom-call | flops 6000000000 | bytes 14680064 | tf_op jit(solution)/shard_map/pallas_call | solution.py:494
  135.3 34.8 %all_to_all.5.parts_ref = bf16[16,32,2048]{2,1,0:T(8,128)(2,1)S(1)} all-to-all(bf16[16,32,2048]{2,1,0:T(8,128)(2,1)} %shard_map.111), channel_id=1, replica_groups=mesh['z'=4,'c'=2,'y'=4,'x'=4] {'y','x'}, dimensions={0} | all-to-all | bytes 4194304 | tf_op jit(solution)/shard_map/all_to_all | solution.py:509
  170.1 1.2 shard_map.112
  171.3 3.4 %collective-permute-start.18 = (bf16[24,2048]{1,0:T(8,128)(2,1)S(1)}, bf16[24,2048]{1,0:T(8,128)(2,1)S(1)}, u32[]{:S(2)}, u32[]{:S(2)}) collective-permute-start(bf16[24,2048]{1,0:T(8,128)(2,1)S(1)} %get-tuple-element.54), channel_id=1, source_target_pairs={{0,16},{16,32},{32,48},{48,64},{64,80},{80,96},{96,112},{112,0},{1... | collective-permute-start | bytes 294920 | tf_op jit(solution)/shard_map/ppermute | solution.py:514
  174.7 1.6 collective-permute-start.19
  176.4 2.1 %collective-permute-start.20 = (bf16[24,2048]{1,0:T(8,128)(2,1)S(1)}, bf16[24,2048]{1,0:T(8,128)(2,1)S(1)}, u32[]{:S(2)}, u32[]{:S(2)}) collective-permute-start(bf16[24,2048]{1,0:T(8,128)(2,1)S(1)} %get-tuple-element.56), channel_id=1, source_target_pairs={{0,48},{16,64},{32,80},{48,96},{64,112},{80,0},{96,16},{112,32},{1... | collective-permute-start | bytes 294920 | tf_op jit(solution)/shard_map/ppermute | solution.py:514
  178.5 2.3 %collective-permute-start.22 = (bf16[24,2048]{1,0:T(8,128)(2,1)S(1)}, bf16[24,2048]{1,0:T(8,128)(2,1)S(1)}, u32[]{:S(2)}, u32[]{:S(2)}) collective-permute-start(bf16[24,2048]{1,0:T(8,128)(2,1)S(1)} %get-tuple-element.58), channel_id=1, source_target_pairs={{0,80},{16,96},{32,112},{48,0},{64,16},{80,32},{96,48},{112,64},{1... | collective-permute-start | bytes 294920 | tf_op jit(solution)/shard_map/ppermute | solution.py:514
  180.8 0.8 collective-permute-start.23
  181.6 1.1 collective-permute-start.24
  182.8 4.1 %collective-permute-done.21.refs_4_ = bf16[24,2048]{1,0:T(8,128)(2,1)S(1)} collective-permute-done((bf16[24,2048]{1,0:T(8,128)(2,1)S(1)}, bf16[24,2048]{1,0:T(8,128)(2,1)S(1)}, u32[]{:S(2)}, u32[]{:S(2)}) %collective-permute-start.21) | collective-permute-done | bytes 98336 | tf_op jit(solution)/shard_map/ppermute | solution.py:514
  188.0 1.5 shard_map.113
  (76 shorter events, 3.6 us)
Async XLA Ops:
  6.5 98.4 %all-gather.5.cloned.1.call-start = ((), (), s32[]{:S(2)}) async-start(), calls=%async_computation.1 | async-start | bytes 9437184 | tf_op jit(solution)/shard_map/all_gather | solution.py:412
  7.3 1.0 copy-start.11
  8.3 75.4 %copy-start.7 = (s32[4]{0:T(128)}, s32[4]{0:T(128)S(1)}, u32[]{:S(2)}) copy-start(s32[4]{0:T(128)S(1)} %pad_add_fusion.where_ref) | copy-start | bytes 52
  8.3 1.6 copy-start.3
  8.3 2.2 %copy-start.4 = (bf16[512,2048]{1,0:T(8,128)(2,1)S(1)}, bf16[512,2048]{1,0:T(8,128)(2,1)}, u32[]{:S(2)}) copy-start(bf16[512,2048]{1,0:T(8,128)(2,1)} %w2_ref.2) | copy-start | bytes 6291460
  11.3 24.5 %copy-start.5 = (bf16[2048,384]{1,0:T(8,128)(2,1)S(1)}, bf16[2048,384]{1,0:T(8,128)(2,1)}, u32[]{:S(2)}) copy-start(bf16[2048,384]{1,0:T(8,128)(2,1)} %wqkv_ref) | copy-start | bytes 4718596
  11.3 22.7 %collective-permute-start.7 = (bf16[1024,512]{1,0:T(8,128)(2,1)S(1)}, bf16[1024,512]{1,0:T(8,128)(2,1)S(1)}, u32[]{:S(2)}, u32[]{:S(2)}) collective-permute-start(bf16[1024,512]{1,0:T(8,128)(2,1)S(1)} %shard_map.102), channel_id=1, source_target_pairs={{0,12},{4,0},{8,4},{12,8},{16,20},{20,24},{24,28},{28,16},{1,13},{... | collective-permute-start | bytes 3145736 | tf_op jit(solution)/shard_map/ppermute | solution.py:408
  13.5 17.8 %collective-permute-start = (bf16[32,2048]{1,0:T(8,128)(2,1)S(1)}, bf16[32,2048]{1,0:T(8,128)(2,1)S(1)}, u32[]{:S(2)}, u32[]{:S(2)}) collective-permute-start(bf16[32,2048]{1,0:T(8,128)(2,1)S(1)} %get-tuple-element.34), channel_id=1, source_target_pairs={{0,4},{4,8},{8,12},{12,0},{1,5},{5,9},{9,13},{13,1},{2,6},{6,10},{... | collective-permute-start | bytes 393224 | tf_op jit(solution)/shard_map/ppermute | solution.py:400
  14.8 19.1 %collective-permute-start.1 = (bf16[32,2048]{1,0:T(8,128)(2,1)S(1)}, bf16[32,2048]{1,0:T(8,128)(2,1)S(1)}, u32[]{:S(2)}, u32[]{:S(2)}) collective-permute-start(bf16[32,2048]{1,0:T(8,128)(2,1)S(1)} %get-tuple-element.35), channel_id=1, source_target_pairs={{0,8},{4,12},{8,0},{12,4},{1,9},{5,13},{9,1},{13,5},{2,10},{6,14},... | collective-permute-start | bytes 393224 | tf_op jit(solution)/shard_map/ppermute | solution.py:400
  16.2 17.7 %collective-permute-start.2 = (bf16[32,2048]{1,0:T(8,128)(2,1)S(1)}, bf16[32,2048]{1,0:T(8,128)(2,1)S(1)}, u32[]{:S(2)}, u32[]{:S(2)}) collective-permute-start(bf16[32,2048]{1,0:T(8,128)(2,1)S(1)} %get-tuple-element.36), channel_id=1, source_target_pairs={{0,12},{4,0},{8,4},{12,8},{1,13},{5,1},{9,5},{13,9},{2,14},{6,2},{... | collective-permute-start | bytes 393224 | tf_op jit(solution)/shard_map/ppermute | solution.py:400
  33.9 1.0 copy-start
  34.9 2.2 %copy-start.1 = (bf16[1024,512]{1,0:T(8,128)(2,1)S(1)}, bf16[1024,512]{1,0:T(8,128)(2,1)}, u32[]{:S(2)}) copy-start(bf16[1024,512]{1,0:T(8,128)(2,1)} %copy-done) | copy-start | bytes 3145732
  35.0 89.4 %all-gather.7.cloned.1.call-start = ((), (), s32[]{:S(2)}) async-start(), calls=%async_computation.2 | async-start | bytes 4718592 | tf_op jit(solution)/shard_map/all_gather | solution.py:446
  37.0 27.7 %copy-start.13 = (f32[2048]{0:T(1024)S(1)}, f32[2048]{0:T(1024)}, u32[]{:S(2)}) copy-start(f32[2048]{0:T(1024)} %param.13) | copy-start | bytes 24580
  37.1 26.9 %collective-permute-start.6 = (bf16[2064,384]{1,0:T(8,128)(2,1)}, bf16[2064,384]{1,0:T(8,128)(2,1)S(1)}, u32[]{:S(2)}, u32[]{:S(2)}) collective-permute-start(bf16[2064,384]{1,0:T(8,128)(2,1)} %shard_map.101.wq0), channel_id=1, source_target_pairs={{0,12},{4,0},{8,4},{12,8},{16,20},{20,24},{24,28},{28,16},{1,13},{... | collective-permute-start | bytes 4755464 | tf_op jit(solution)/shard_map/ppermute | solution.py:421
  37.7 26.2 %collective-permute-start.8 = (bf16[512,512]{1,0:T(8,128)(2,1)S(1)}, bf16[512,512]{1,0:T(8,128)(2,1)S(1)}, u32[]{:S(2)}, u32[]{:S(2)}) collective-permute-start(bf16[512,512]{1,0:T(8,128)(2,1)S(1)} %shard_map.103), channel_id=1, source_target_pairs={{0,12},{4,0},{8,4},{12,8},{16,20},{20,24},{24,28},{28,16},{1,13},{... | collective-permute-start | bytes 1572872 | tf_op jit(solution)/shard_map/ppermute | solution.py:414
  38.2 26.5 %collective-permute-start.3 = (bf16[128,2048]{1,0:T(8,128)(2,1)S(1)}, bf16[128,2048]{1,0:T(8,128)(2,1)S(1)}, u32[]{:S(2)}, u32[]{:S(2)}) collective-permute-start(bf16[128,2048]{1,0:T(8,128)(2,1)S(1)} %constant_dynamic-update-slice_fusion.a0), channel_id=1, source_target_pairs={{0,1},{1,2},{2,3},{3,0},{4,5},{5,6},{6,7},{7,4},{8,9},{9,10},{10,1... | collective-permute-start | bytes 1572872 | tf_op jit(solution)/shard_map/ppermute | solution.py:410
  39.5 25.2 %collective-permute-start.4 = (bf16[128,2048]{1,0:T(8,128)(2,1)S(1)}, bf16[128,2048]{1,0:T(8,128)(2,1)}, u32[]{:S(2)}, u32[]{:S(2)}) collective-permute-start(bf16[128,2048]{1,0:T(8,128)(2,1)S(1)} %constant_dynamic-update-slice_fusion.a0), channel_id=1, source_target_pairs={{0,2},{1,3},{2,0},{3,1},{4,6},{5,7},{6,4},{7,5},{8,10},{9,11},{10,... | collective-permute-start | bytes 1572872 | tf_op jit(solution)/shard_map/ppermute | solution.py:410
  41.9 22.8 %collective-permute-start.5 = (bf16[128,2048]{1,0:T(8,128)(2,1)S(1)}, bf16[128,2048]{1,0:T(8,128)(2,1)}, u32[]{:S(2)}, u32[]{:S(2)}) collective-permute-start(bf16[128,2048]{1,0:T(8,128)(2,1)S(1)} %constant_dynamic-update-slice_fusion.a0), channel_id=1, source_target_pairs={{0,3},{1,0},{2,1},{3,2},{4,7},{5,4},{6,5},{7,6},{8,11},{9,8},{10,9... | collective-permute-start | bytes 1572872 | tf_op jit(solution)/shard_map/ppermute | solution.py:410
  64.0 2.4 %copy-start.17 = (bf16[512,512]{1,0:T(8,128)(2,1)}, bf16[512,512]{1,0:T(8,128)(2,1)S(1)}, u32[]{:S(2)}) copy-start(bf16[512,512]{1,0:T(8,128)(2,1)S(1)} %collective-permute-done.8) | copy-start | bytes 1572868
  64.6 3.1 %copy-start.10 = (s32[1,8]{1,0:T(1,128)S(1)}, s32[1,8]{1,0:T(1,128)}, u32[]{:S(2)}) copy-start(s32[1,8]{1,0:T(1,128)} %count_ref.7) | copy-start | bytes 100
  64.6 3.1 %copy-start.14 = (s32[1,16]{1,0:T(1,128)S(1)}, s32[1,16]{1,0:T(1,128)}, u32[]{:S(2)}) copy-start(s32[1,16]{1,0:T(1,128)} %member_ref.3) | copy-start | bytes 196
  64.6 12.7 %collective-permute-start.10 = (bf16[1040,384]{1,0:T(8,128)(2,1)S(1)}, bf16[1040,384]{1,0:T(8,128)(2,1)}, u32[]{:S(2)}, u32[]{:S(2)}) collective-permute-start(bf16[1040,384]{1,0:T(8,128)(2,1)S(1)} %shard_map.105), channel_id=1, source_target_pairs={{0,12},{4,0},{8,4},{12,8},{16,20},{20,24},{24,28},{28,16},{1,13},{... | collective-permute-start | bytes 2396168 | tf_op jit(solution)/shard_map/ppermute | solution.py:433
  66.4 1.3 copy-start.2
  67.7 6.5 %copy-start.15 = (bf16[512,2048]{1,0:T(8,128)(2,1)}, bf16[512,2048]{1,0:T(8,128)(2,1)S(1)}, u32[]{:S(2)}) copy-start(bf16[512,2048]{1,0:T(8,128)(2,1)S(1)} %get-tuple-element.42.xn) | copy-start | bytes 6291460
  74.2 16.4 %copy-start.6 = (bf16[512,256]{1,0:T(8,128)(2,1)}, bf16[512,256]{1,0:T(8,128)(2,1)S(1)}, u32[]{:S(2)}) copy-start(bf16[512,256]{1,0:T(8,128)(2,1)S(1)} %shard_map.106.o0) | copy-start | bytes 786436
  77.3 6.4 %collective-permute-start.9 = (bf16[2064,384]{1,0:T(8,128)(2,1)S(1)}, bf16[2064,384]{1,0:T(8,128)(2,1)S(1)}, u32[]{:S(2)}, u32[]{:S(2)}) collective-permute-start(bf16[2064,384]{1,0:T(8,128)(2,1)S(1)} %collective-permute-done.6.got_ref.wq1), channel_id=1, source_target_pairs={{0,16},{16,0},{1,17},{17,1},{2,18},{18,2},{3,19},{19,3},{4,20},{20... | collective-permute-start | bytes 4755464 | tf_op jit(solution)/shard_map/ppermute | solution.py:431
  78.7 4.9 %collective-permute-start.11 = (bf16[1040,384]{1,0:T(8,128)(2,1)}, bf16[1040,384]{1,0:T(8,128)(2,1)S(1)}, u32[]{:S(2)}, u32[]{:S(2)}) collective-permute-start(bf16[1040,384]{1,0:T(8,128)(2,1)} %collective-permute-done.10.wqa), channel_id=1, source_target_pairs={{0,16},{16,0},{1,17},{17,1},{2,18},{18,2},{3,19},{19,3},{4,20},{20... | collective-permute-start | bytes 2396168 | tf_op jit(solution)/shard_map/ppermute | solution.py:447
  78.8 15.2 %collective-permute-start.15 = (bf16[512,256]{1,0:T(8,128)(2,1)S(1)}, bf16[512,256]{1,0:T(8,128)(2,1)S(1)}, u32[]{:S(2)}, u32[]{:S(2)}) collective-permute-start(bf16[512,256]{1,0:T(8,128)(2,1)S(1)} %shard_map.106.o0), channel_id=1, source_target_pairs={{0,1},{1,2},{2,3},{3,0},{4,5},{5,6},{6,7},{7,4},{8,9},{9,10},{10,1... | collective-permute-start | bytes 786440 | tf_op jit(solution)/shard_map/ppermute | solution.py:462
  80.1 15.2 %collective-permute-start.16 = (bf16[512,256]{1,0:T(8,128)(2,1)S(1)}, bf16[512,256]{1,0:T(8,128)(2,1)S(1)}, u32[]{:S(2)}, u32[]{:S(2)}) collective-permute-start(bf16[512,256]{1,0:T(8,128)(2,1)S(1)} %shard_map.106.o0), channel_id=1, source_target_pairs={{0,2},{1,3},{2,0},{3,1},{4,6},{5,7},{6,4},{7,5},{8,10},{9,11},{10,... | collective-permute-start | bytes 786440 | tf_op jit(solution)/shard_map/ppermute | solution.py:462
  82.5 12.7 %collective-permute-start.17 = (bf16[512,256]{1,0:T(8,128)(2,1)S(1)}, bf16[512,256]{1,0:T(8,128)(2,1)S(1)}, u32[]{:S(2)}, u32[]{:S(2)}) collective-permute-start(bf16[512,256]{1,0:T(8,128)(2,1)S(1)} %shard_map.106.o0), channel_id=1, source_target_pairs={{0,3},{1,0},{2,1},{3,2},{4,7},{5,4},{6,5},{7,6},{8,11},{9,8},{10,9... | collective-permute-start | bytes 786440 | tf_op jit(solution)/shard_map/ppermute | solution.py:462
  83.7 1.6 copy-start.16
  90.6 14.3 %copy-start.12 = (bf16[512,256]{1,0:T(8,128)(2,1)}, bf16[512,256]{1,0:T(8,128)(2,1)S(1)}, u32[]{:S(2)}) copy-start(bf16[512,256]{1,0:T(8,128)(2,1)S(1)} %shard_map.107.f0) | copy-start | bytes 786436
  90.6 14.4 %collective-permute-start.12 = (bf16[512,256]{1,0:T(8,128)(2,1)S(1)}, bf16[512,256]{1,0:T(8,128)(2,1)S(1)}, u32[]{:S(2)}, u32[]{:S(2)}) collective-permute-start(bf16[512,256]{1,0:T(8,128)(2,1)S(1)} %shard_map.107.f0), channel_id=1, source_target_pairs={{0,1},{1,2},{2,3},{3,0},{4,5},{5,6},{6,7},{7,4},{8,9},{9,10},{10,1... | collective-permute-start | bytes 786440 | tf_op jit(solution)/shard_map/ppermute | solution.py:463
  91.6 14.3 %collective-permute-start.13 = (bf16[512,256]{1,0:T(8,128)(2,1)S(1)}, bf16[512,256]{1,0:T(8,128)(2,1)S(1)}, u32[]{:S(2)}, u32[]{:S(2)}) collective-permute-start(bf16[512,256]{1,0:T(8,128)(2,1)S(1)} %shard_map.107.f0), channel_id=1, source_target_pairs={{0,2},{1,3},{2,0},{3,1},{4,6},{5,7},{6,4},{7,5},{8,10},{9,11},{10,... | collective-permute-start | bytes 786440 | tf_op jit(solution)/shard_map/ppermute | solution.py:463
  94.1 1.2 copy-start.18
  94.1 11.8 %collective-permute-start.14 = (bf16[512,256]{1,0:T(8,128)(2,1)S(1)}, bf16[512,256]{1,0:T(8,128)(2,1)S(1)}, u32[]{:S(2)}, u32[]{:S(2)}) collective-permute-start(bf16[512,256]{1,0:T(8,128)(2,1)S(1)} %shard_map.107.f0), channel_id=1, source_target_pairs={{0,3},{1,0},{2,1},{3,2},{4,7},{5,4},{6,5},{7,6},{8,11},{9,8},{10,9... | collective-permute-start | bytes 786440 | tf_op jit(solution)/shard_map/ppermute | solution.py:463
  95.2 0.8 copy-start.20
  105.0 0.9 copy-start.21
  105.9 0.8 copy-start.23
  135.3 34.8 %copy-start.8 = (s32[4]{0:T(128)S(1)}, s32[4]{0:T(128)}, u32[]{:S(2)}) copy-start(s32[4]{0:T(128)} %copy-done.7) | copy-start | bytes 52
  171.3 9.5 %collective-permute-start.18 = (bf16[24,2048]{1,0:T(8,128)(2,1)S(1)}, bf16[24,2048]{1,0:T(8,128)(2,1)S(1)}, u32[]{:S(2)}, u32[]{:S(2)}) collective-permute-start(bf16[24,2048]{1,0:T(8,128)(2,1)S(1)} %get-tuple-element.54), channel_id=1, source_target_pairs={{0,16},{16,32},{32,48},{48,64},{64,80},{80,96},{96,112},{112,0},{1... | collective-permute-start | bytes 294920 | tf_op jit(solution)/shard_map/ppermute | solution.py:514
  174.7 6.9 %collective-permute-start.19 = (bf16[24,2048]{1,0:T(8,128)(2,1)S(1)}, bf16[24,2048]{1,0:T(8,128)(2,1)S(1)}, u32[]{:S(2)}, u32[]{:S(2)}) collective-permute-start(bf16[24,2048]{1,0:T(8,128)(2,1)S(1)} %get-tuple-element.55), channel_id=1, source_target_pairs={{0,32},{16,48},{32,64},{48,80},{64,96},{80,112},{96,0},{112,16},{1... | collective-permute-start | bytes 294920 | tf_op jit(solution)/shard_map/ppermute | solution.py:514
  176.4 6.4 %collective-permute-start.20 = (bf16[24,2048]{1,0:T(8,128)(2,1)S(1)}, bf16[24,2048]{1,0:T(8,128)(2,1)S(1)}, u32[]{:S(2)}, u32[]{:S(2)}) collective-permute-start(bf16[24,2048]{1,0:T(8,128)(2,1)S(1)} %get-tuple-element.56), channel_id=1, source_target_pairs={{0,48},{16,64},{32,80},{48,96},{64,112},{80,0},{96,16},{112,32},{1... | collective-permute-start | bytes 294920 | tf_op jit(solution)/shard_map/ppermute | solution.py:514
  178.5 8.4 %collective-permute-start.21 = (bf16[24,2048]{1,0:T(8,128)(2,1)S(1)}, bf16[24,2048]{1,0:T(8,128)(2,1)S(1)}, u32[]{:S(2)}, u32[]{:S(2)}) collective-permute-start(bf16[24,2048]{1,0:T(8,128)(2,1)S(1)} %get-tuple-element.57), channel_id=1, source_target_pairs={{0,64},{16,80},{32,96},{48,112},{64,0},{80,16},{96,32},{112,48},{1... | collective-permute-start | bytes 294920 | tf_op jit(solution)/shard_map/ppermute | solution.py:514
  178.5 9.0 %collective-permute-start.22 = (bf16[24,2048]{1,0:T(8,128)(2,1)S(1)}, bf16[24,2048]{1,0:T(8,128)(2,1)S(1)}, u32[]{:S(2)}, u32[]{:S(2)}) collective-permute-start(bf16[24,2048]{1,0:T(8,128)(2,1)S(1)} %get-tuple-element.58), channel_id=1, source_target_pairs={{0,80},{16,96},{32,112},{48,0},{64,16},{80,32},{96,48},{112,64},{1... | collective-permute-start | bytes 294920 | tf_op jit(solution)/shard_map/ppermute | solution.py:514
  180.8 6.7 %collective-permute-start.23 = (bf16[24,2048]{1,0:T(8,128)(2,1)S(1)}, bf16[24,2048]{1,0:T(8,128)(2,1)S(1)}, u32[]{:S(2)}, u32[]{:S(2)}) collective-permute-start(bf16[24,2048]{1,0:T(8,128)(2,1)S(1)} %get-tuple-element.59), channel_id=1, source_target_pairs={{0,96},{16,112},{32,0},{48,16},{64,32},{80,48},{96,64},{112,80},{1... | collective-permute-start | bytes 294920 | tf_op jit(solution)/shard_map/ppermute | solution.py:514
  181.6 6.4 %collective-permute-start.24 = (bf16[24,2048]{1,0:T(8,128)(2,1)S(1)}, bf16[24,2048]{1,0:T(8,128)(2,1)S(1)}, u32[]{:S(2)}, u32[]{:S(2)}) collective-permute-start(bf16[24,2048]{1,0:T(8,128)(2,1)S(1)} %get-tuple-element.60), channel_id=1, source_target_pairs={{0,112},{16,0},{32,16},{48,32},{64,48},{80,64},{96,80},{112,96},{1... | collective-permute-start | bytes 294920 | tf_op jit(solution)/shard_map/ppermute | solution.py:514
  (3 other events, 2.1 us)
Sparse Core Ops, SparseCore 0:
  35.1 52.4 all-gather.4
  89.3 32.3 all-gather.6

commit v3 on v2

--- a/solution.py
+++ b/solution.py
@@ -219,10 +219,10 @@
     out_ref[:, 128:] = attend(raw, w3[0, 1024:1025], allowed)
 
 
-def merge_part(where_ref, pair, refs, wm_ref, wm, heads, sem):
+def merge_part(where_ref, refs, wm_ref, wm, heads, sem):
     c, y, x = where_ref[1], where_ref[2], where_ref[3]
     step = 1 - 2 * c
-    source = ([y, (y + step + 4) & 3], [(y - step + 4) & 3, (y + 2) & 3])[pair]
+    source = [y, (y + step + 4) & 3]
     copies = []
     for m in range(SIDE):
         for k in range(2):
@@ -247,7 +247,7 @@
 def merge_first_kernel(where_ref, o0, o1, o2, o3, rows_ref, wm_ref, out_ref, wm, heads, rows, sem):
     carried = pltpu.make_async_copy(rows_ref, rows, sem.at[8])
     carried.start()
-    merge_part(where_ref, 0, (o0, o1, o2, o3), wm_ref, wm, heads, sem)
+    merge_part(where_ref, (o0, o1, o2, o3), wm_ref, wm, heads, sem)
     carried.wait()
     for n in range(4):
         cols = slice(512 * n, 512 * n + 512)
@@ -255,15 +255,49 @@
 
 
 def merge_kernel(
-    where_ref, f0, f1, f2, f3, gain_ref, part_ref, wm_ref, fed_ref, kept_ref, wm, heads, total, sem
+    where_ref, f0, f1, f2, f3, gain_ref, part_ref, wm_ref, w1_ref, all_ref,
+    fed_ref, kept_ref, out_ref, wm, heads, total, w1, sem,
 ):
-    carried = pltpu.make_async_copy(part_ref, total, sem.at[8])
-    carried.start()
-    merge_part(where_ref, 1, (f0, f1, f2, f3), wm_ref, wm, heads, sem)
-    carried.wait()
+    c, y, x = where_ref[1], where_ref[2], where_ref[3]
+    step = 1 - 2 * c
+    source = [(y - step + 4) & 3, (y + 2) & 3]
+    merges = []
+    for n in range(4):
+        cols = pl.ds(512 * n, 512)
+        group = [pltpu.make_async_copy(part_ref.at[:, cols], total.at[:, cols], sem.at[n])]
+        for m in range(SIDE):
+            for k in range(2):
+                head = source[k] * SIDE + ((x - m + 4) & 3)
+                rows = pl.ds(pl.multiple_of(head * HEAD_DIM, HEAD_DIM), HEAD_DIM)
+                here = pl.ds(256 * m + HEAD_DIM * k, HEAD_DIM)
+                group.append(
+                    pltpu.make_async_copy(wm_ref.at[rows, cols], wm.at[here, cols], sem.at[n])
+                )
+        merges.append(group)
+    ups = [[pltpu.make_async_copy(w1_ref, w1.at[0], sem.at[4])]]
+    for half in range(2):
+        ups.append(
+            [
+                pltpu.make_async_copy(
+                    all_ref.at[2 * z + half, pl.ds(0, 512)],
+                    w1.at[1 + half, pl.ds(512 * z, 512)],
+                    sem.at[5 + half],
+                )
+                for z in range(4)
+            ]
+        )
+    for group in merges + ups:
+        for copy in group:
+            copy.start()
+    for m, ref in enumerate((f0, f1, f2, f3)):
+        for j in range(SIDE):
+            theirs = 128 * ((j - m) % SIDE)
+            heads[128 * j : 128 * j + 128, 256 * m : 256 * m + 256] = ref[theirs : theirs + 128]
     squares = jnp.zeros((512, 1), F32)
     for n in range(4):
         cols = slice(512 * n, 512 * n + 512)
+        for copy in merges[n]:
+            copy.wait()
         part = dot(heads[...], wm[:, cols]) + total[:, cols]
         squares = squares + jnp.sum(part * part, axis=-1, keepdims=True)
         total[:, cols] = part
@@ -272,26 +306,8 @@
         cols = slice(512 * n, 512 * n + 512)
         fed_ref[:, cols] = (total[:, cols] * scale * gain_ref[:, cols]).astype(BF16)
     kept_ref[...] = total[:128]
-
-
-def near_mlp_kernel(fed_ref, w1_ref, all_ref, out_ref, w1, sem):
-    copies = [[pltpu.make_async_copy(w1_ref, w1.at[0], sem.at[0])]]
-    for c in range(2):
-        copies.append(
-            [
-                pltpu.make_async_copy(
-                    all_ref.at[2 * z + c, pl.ds(0, 512)],
-                    w1.at[1 + c, pl.ds(512 * z, 512)],
-                    sem.at[1 + c],
-                )
-                for z in range(4)
-            ]
-        )
-    for group in copies:
-        for copy in group:
-            copy.start()
     for i in range(3):
-        for copy in copies[i]:
+        for copy in ups[i]:
             copy.wait()
         out_ref[:, 512 * i : 512 * i + 512] = jax.nn.gelu(
             dot(fed_ref[...], w1[i]), approximate=True
@@ -472,25 +488,21 @@
         moved=12 * 2**20,
     )(where, *first, kept_rows, wmerge)
     second[0], near_all = lax.optimization_barrier((second[0], near_all))
-    fed, kept = call(
+    fed, kept, near_hidden = call(
         merge_kernel,
-        [shape((512, 2048)), shape((128, 2048), F32)],
-        [SMEM] + [VMEM] * 5 + [ANY] * 2,
-        scratch + [pltpu.VMEM((512, 2048), F32), pltpu.SemaphoreType.DMA((9,))],
+        [shape((512, 2048)), shape((128, 2048), F32), shape((512, 1536))],
+        [SMEM] + [VMEM] * 5 + [ANY] * 4,
+        scratch
+        + [
+            pltpu.VMEM((512, 2048), F32),
+            pltpu.VMEM((3, 2048, 512), BF16),
+            pltpu.SemaphoreType.DMA((7,)),
+        ],
         vmem=60,
         flops=25 * 10**9,
-        moved=14 * 2**20,
-    )(where, *second, gain2, merged, wmerge)
-
-    [near_hidden] = call(
-        near_mlp_kernel,
-        [shape((512, 1536))],
-        [VMEM] + [ANY] * 2,
-        [pltpu.VMEM((3, 2048, 512), BF16), pltpu.SemaphoreType.DMA((3,))],
-        vmem=60,
-        flops=4 * 10**9,
-        moved=10 * 2**20,
-    )(fed, w1, near_all)
+        moved=24 * 2**20,
+    )(where, *second, gain2, merged, wmerge, w1, near_all)
+
     [parts] = call(
         far_mlp_kernel,
         [shape((16, 32, 2048))],

time: 197 us -> 191 us (0.970)
  Pallas kernels: 57.6 us -> 51.7 us
  waiting for transfers between devices: 45.9 us -> 50.1 us
  starting transfers between devices: 34.8 us -> 31.7 us
    pallas_call x2 -> x1, Pallas kernels: 17.6 us -> 11.7 us  [body(): call(merge_kernel, [shape((512, 2048)), shape((128, 2048), F32), shape((5...]
    ppermute x7, starting transfers between devices: 11.5 us -> 8.29 us  [body(): got += [lax.ppermute(leaving[m], DP, ring(N_DP, m)) for m in range(1, N_DP)]]
    all_gather x1, waiting for transfers between devices: 0.02 us -> 3.17 us  [body(): far_all = lax.all_gather(far, DP, axis=0, tiled=False)]
  transfers between devices with their start and end apart: 27 -> 27, of which waited for: 8 -> 11; matrix products, arithmetic and copies ran while one was open for 0% -> 0% of each run, Pallas kernels for 22% -> 19%
where the time goes in v3:
time: 191 us
  Pallas kernels  51.7 us (27%)
  waiting for transfers between devices  50.1 us (26%)
  blocking collectives  34.2 us (18%)
  starting transfers between devices  31.7 us (17%)
  between operations  14.5 us (8%)
  local copies, waits for them, and re-layouts  8.55 us (4%)
    all_to_all x1, blocking collectives, body(): parts = lax.all_to_all(parts, ('y', 'x'), 0, 0, tiled=True)  34.2 us
    ppermute x1, waiting for transfers between devices, body(): far = lax.ppermute(near_half, cy, twin_ring())  20.9 us
    ppermute x3, waiting for transfers between devices, body(): lax.ppermute(blocks[k], 'y', ring(SIDE, k))  15.7 us
    pallas_call x1, Pallas kernels, body(): call(merge_kernel, [shape((512, 2048)), shape((128, 2048), F32), shape((5...  11.7 us
    pallas_call x1, Pallas kernels, body(): call(far_mlp_kernel, [shape((16, 32, 2048))], [SMEM, VMEM] + [ANY] * 5, [...  10.9 us
    pallas_call x1, Pallas kernels, body(): call(merge_first_kernel, [shape((512, 2048), F32)], [SMEM] + [VMEM] * 4 +...  8.86 us
    unnamed x51, local copies, waits for them, and re-layouts  8.54 us
    ppermute x7, starting transfers between devices, body(): got += [lax.ppermute(leaving[m], DP, ring(N_DP, m)) for m in range(1, N_DP)]  8.29 us
  transfers between devices with their start and end apart: 27, of which 11 were waited for; matrix products, arithmetic and copies ran while one was open for 0% of the time, Pallas kernels for 19%

profile of v3, /device:TPU:1, one launch (start us, length us, event | category | flops | bytes accessed | tf_op | source)
XLA Modules:
  0.0 190.9 jit_solution(1818668322051313184)
XLA Ops:
  7.3 1.0 copy-done.11
  8.3 0.9 shard_map.100
  9.2 0.7 copy-done.3
  10.5 0.7 shard_map.102
  11.3 2.2 %collective-permute-start.7 = (bf16[1024,512]{1,0:T(8,128)(2,1)S(1)}, bf16[1024,512]{1,0:T(8,128)(2,1)S(1)}, u32[]{:S(2)}, u32[]{:S(2)}) collective-permute-start(bf16[1024,512]{1,0:T(8,128)(2,1)S(1)} %shard_map.102), channel_id=1, source_target_pairs={{0,12},{4,0},{8,4},{12,8},{16,20},{20,24},{24,28},{28,16},{1,13},{... | collective-permute-start | bytes 3145736 | tf_op jit(solution)/shard_map/ppermute | solution.py:424
  13.5 1.3 collective-permute-start
  14.8 1.4 collective-permute-start.1
  16.2 2.0 %collective-permute-start.2 = (bf16[32,2048]{1,0:T(8,128)(2,1)S(1)}, bf16[32,2048]{1,0:T(8,128)(2,1)S(1)}, u32[]{:S(2)}, u32[]{:S(2)}) collective-permute-start(bf16[32,2048]{1,0:T(8,128)(2,1)S(1)} %get-tuple-element.37), channel_id=1, source_target_pairs={{0,12},{4,0},{8,4},{12,8},{1,13},{5,1},{9,5},{13,9},{2,14},{6,2},{... | collective-permute-start | bytes 393224 | tf_op jit(solution)/shard_map/ppermute | solution.py:416
  18.2 13.1 %collective-permute-done = bf16[32,2048]{1,0:T(8,128)(2,1)S(1)} collective-permute-done((bf16[32,2048]{1,0:T(8,128)(2,1)S(1)}, bf16[32,2048]{1,0:T(8,128)(2,1)S(1)}, u32[]{:S(2)}, u32[]{:S(2)}) %collective-permute-start) | collective-permute-done | bytes 131104 | tf_op jit(solution)/shard_map/ppermute | solution.py:416
  31.3 2.6 %collective-permute-done.1 = bf16[32,2048]{1,0:T(8,128)(2,1)S(1)} collective-permute-done((bf16[32,2048]{1,0:T(8,128)(2,1)S(1)}, bf16[32,2048]{1,0:T(8,128)(2,1)S(1)}, u32[]{:S(2)}, u32[]{:S(2)}) %collective-permute-start.1) | collective-permute-done | bytes 131104 | tf_op jit(solution)/shard_map/ppermute | solution.py:416
  33.9 1.0 copy-done
  35.7 1.3 shard_map.101.wq0
  38.2 1.2 collective-permute-start.3
  39.5 2.5 %collective-permute-start.4 = (bf16[128,2048]{1,0:T(8,128)(2,1)S(1)}, bf16[128,2048]{1,0:T(8,128)(2,1)}, u32[]{:S(2)}, u32[]{:S(2)}) collective-permute-start(bf16[128,2048]{1,0:T(8,128)(2,1)S(1)} %constant_dynamic-update-slice_fusion.a0), channel_id=1, source_target_pairs={{0,2},{1,3},{2,0},{3,1},{4,6},{5,7},{6,4},{7,5},{8,10},{9,11},{10,... | collective-permute-start | bytes 1572872 | tf_op jit(solution)/shard_map/ppermute | solution.py:426
  41.9 1.2 collective-permute-start.5
  43.1 20.9 %collective-permute-done.8 = bf16[512,512]{1,0:T(8,128)(2,1)S(1)} collective-permute-done((bf16[512,512]{1,0:T(8,128)(2,1)S(1)}, bf16[512,512]{1,0:T(8,128)(2,1)S(1)}, u32[]{:S(2)}, u32[]{:S(2)}) %collective-permute-start.8) | collective-permute-done | bytes 524320 | tf_op jit(solution)/shard_map/ppermute | solution.py:430
  64.7 1.6 shard_map.104
  66.4 1.3 copy-done.2
  67.7 6.5 %shard_map.106.o0 = bf16[512,256]{1,0:T(8,128)(2,1)S(1)} custom-call(s32[4]{0:T(128)S(1)} %pad_add_fusion.where_ref, s32[1,8]{1,0:T(1,128)S(1)} %copy-done.10, s32[1,16]{1,0:T(1,128)S(1)} %copy-done.14, bf16[512,2048]{1,0:T(8,128)(2,1)S(1)} %get-tuple-element.43.xn, bf16[2064,384]{1,0:T(8,128)(2,1)} %shard_map.101.wq0, ...), custom_call_target="tpu_custom_call" | custom-call | flops 2000000000 | bytes 8388608 | tf_op jit(solution)/shard_map/pallas_call | solution.py:451
  74.2 3.1 %collective-permute-done.10.wqa = bf16[1040,384]{1,0:T(8,128)(2,1)} collective-permute-done((bf16[1040,384]{1,0:T(8,128)(2,1)S(1)}, bf16[1040,384]{1,0:T(8,128)(2,1)}, u32[]{:S(2)}, u32[]{:S(2)}) %collective-permute-start.10) | collective-permute-done | bytes 798752 | tf_op jit(solution)/shard_map/ppermute | solution.py:449
  77.3 1.5 collective-permute-start.9
  78.8 1.2 collective-permute-start.15
  80.1 2.5 %collective-permute-start.16 = (bf16[512,256]{1,0:T(8,128)(2,1)S(1)}, bf16[512,256]{1,0:T(8,128)(2,1)S(1)}, u32[]{:S(2)}, u32[]{:S(2)}) collective-permute-start(bf16[512,256]{1,0:T(8,128)(2,1)S(1)} %shard_map.106.o0), channel_id=1, source_target_pairs={{0,2},{1,3},{2,0},{3,1},{4,6},{5,7},{6,4},{7,5},{8,10},{9,11},{10,... | collective-permute-start | bytes 786440 | tf_op jit(solution)/shard_map/ppermute | solution.py:478
  82.5 1.2 collective-permute-start.17
  83.7 1.6 copy-done.16
  85.3 5.3 %shard_map.107.f0 = bf16[512,256]{1,0:T(8,128)(2,1)S(1)} custom-call(s32[4]{0:T(128)S(1)} %pad_add_fusion.where_ref, s32[1,8]{1,0:T(1,128)S(1)} %copy-done.10, s32[1,16]{1,0:T(1,128)S(1)} %copy-done.14, bf16[512,2048]{1,0:T(8,128)(2,1)S(1)} %copy-done.16, bf16[2064,384]{1,0:T(8,128)(2,1)S(1)} %collective-permute-done.9.wq2, ...), custom_call_target="tpu_custom_call" | custom-call | flops 2000000000 | bytes 8388608 | tf_op jit(solution)/shard_map/pallas_call | solution.py:464
  90.6 1.0 collective-permute-start.12
  91.6 2.5 %collective-permute-start.13 = (bf16[512,256]{1,0:T(8,128)(2,1)S(1)}, bf16[512,256]{1,0:T(8,128)(2,1)S(1)}, u32[]{:S(2)}, u32[]{:S(2)}) collective-permute-start(bf16[512,256]{1,0:T(8,128)(2,1)S(1)} %shard_map.107.f0), channel_id=1, source_target_pairs={{0,2},{1,3},{2,0},{3,1},{4,6},{5,7},{6,4},{7,5},{8,10},{9,11},{10,... | collective-permute-start | bytes 786440 | tf_op jit(solution)/shard_map/ppermute | solution.py:479
  94.1 1.2 collective-permute-start.14
  95.3 0.7 copy-done.19
  96.0 8.9 %shard_map.108.part_ref = f32[512,2048]{1,0:T(8,128)} custom-call(s32[4]{0:T(128)} %copy-done.7, bf16[512,256]{1,0:T(8,128)(2,1)} %copy-done.6, bf16[512,256]{1,0:T(8,128)(2,1)} %copy-done.18, bf16[512,256]{1,0:T(8,128)(2,1)} %copy-done.19, bf16[512,256]{1,0:T(8,128)(2,1)} %copy-done.20, bf16[512,2048]{1,0:T(8,128)(2,1)} %copy-done.2, bf16[2048,2048]{1,0:T(8,128)(2,1)} %wm_ref.3), custom_call_target="tpu_custom_call" | custom-call | flops 2000000000 | bytes 12582912 | tf_op jit(solution)/shard_map/pallas_call | solution.py:481
  104.9 1.0 collective-permute-done.13.f2
  105.9 0.7 copy-done.22
  106.7 11.7 %shard_map.109 = (bf16[512,2048]{1,0:T(8,128)(2,1)}, f32[128,2048]{1,0:T(8,128)}, bf16[512,1536]{1,0:T(8,128)(2,1)}) custom-call(s32[4]{0:T(128)} %copy-done.7, bf16[512,256]{1,0:T(8,128)(2,1)} %copy-done.12, bf16[512,256]{1,0:T(8,128)(2,1)} %copy-done.21, bf16[512,256]{1,0:T(8,128)(2,1)} %copy-done.22, bf16[512,256]{1,0:T(8,128)(2,1)} %copy-done.23, ...), custom_call_target="tpu_custom_call" | custom-call | flops 24999999488 | bytes 25165824 | tf_op jit(solution)/shard_map/pallas_call | solution.py:491
  118.5 3.2 %all-gather.7.cloned.1.call-done = bf16[4096,512]{1,0:T(8,128)(2,1)} async-done(((bf16[512,512]{1,0:T(8,128)(2,1)}), bf16[4096,512]{1,0:T(8,128)(2,1)}) %all-gather.7.cloned.1.call-update) | async-done | bytes 4194320 | tf_op jit(solution)/shard_map/all_gather | solution.py:462
  121.6 10.9 %shard_map.110 = bf16[16,32,2048]{2,1,0:T(8,128)(2,1)} custom-call(s32[4]{0:T(128)} %copy-done.7, bf16[512,2048]{1,0:T(8,128)(2,1)} %get-tuple-element.50.fed_ref, f32[128,2048]{1,0:T(8,128)} %get-tuple-element.51.kept_ref, bf16[512,1536]{1,0:T(8,128)(2,1)} %get-tuple-element.52.hidden_ref, bf16[512,2048]{1,0:T(8,128)(2,1)} %w2_ref.2, ...), custom_call_target="tpu_custom_call" | custom-call | flops 6000000000 | bytes 14680064 | tf_op jit(solution)/shard_map/pallas_call | solution.py:506
  132.6 34.2 %all_to_all.5.parts_ref = bf16[16,32,2048]{2,1,0:T(8,128)(2,1)S(1)} all-to-all(bf16[16,32,2048]{2,1,0:T(8,128)(2,1)} %shard_map.110), channel_id=1, replica_groups=mesh['z'=4,'c'=2,'y'=4,'x'=4] {'y','x'}, dimensions={0} | all-to-all | bytes 4194304 | tf_op jit(solution)/shard_map/all_to_all | solution.py:521
  166.8 1.2 shard_map.111
  168.0 1.6 collective-permute-start.18
  169.6 1.0 collective-permute-start.19
  170.6 2.1 %collective-permute-start.20 = (bf16[24,2048]{1,0:T(8,128)(2,1)S(1)}, bf16[24,2048]{1,0:T(8,128)(2,1)S(1)}, u32[]{:S(2)}, u32[]{:S(2)}) collective-permute-start(bf16[24,2048]{1,0:T(8,128)(2,1)S(1)} %get-tuple-element.58), channel_id=1, source_target_pairs={{0,48},{16,64},{32,80},{48,96},{64,112},{80,0},{96,16},{112,32},{1... | collective-permute-start | bytes 294920 | tf_op jit(solution)/shard_map/ppermute | solution.py:526
  172.7 0.7 collective-permute-start.21
  173.4 2.6 %collective-permute-start.22 = (bf16[24,2048]{1,0:T(8,128)(2,1)S(1)}, bf16[24,2048]{1,0:T(8,128)(2,1)S(1)}, u32[]{:S(2)}, u32[]{:S(2)}) collective-permute-start(bf16[24,2048]{1,0:T(8,128)(2,1)S(1)} %get-tuple-element.60), channel_id=1, source_target_pairs={{0,80},{16,96},{32,112},{48,0},{64,16},{80,32},{96,48},{112,64},{1... | collective-permute-start | bytes 294920 | tf_op jit(solution)/shard_map/ppermute | solution.py:526
  176.0 0.7 collective-permute-done.19.refs_2_
  177.0 1.1 collective-permute-done.20.refs_3_
  178.2 3.0 %collective-permute-done.21.refs_4_ = bf16[24,2048]{1,0:T(8,128)(2,1)S(1)} collective-permute-done((bf16[24,2048]{1,0:T(8,128)(2,1)S(1)}, bf16[24,2048]{1,0:T(8,128)(2,1)S(1)}, u32[]{:S(2)}, u32[]{:S(2)}) %collective-permute-start.21) | collective-permute-done | bytes 98336 | tf_op jit(solution)/shard_map/ppermute | solution.py:526
  181.7 0.8 collective-permute-done.24.refs_7_
  182.5 1.5 shard_map.112
  (75 shorter events, 4.6 us)
Async XLA Ops:
  6.5 98.4 %all-gather.5.cloned.1.call-start = ((), (), s32[]{:S(2)}) async-start(), calls=%async_computation.1 | async-start | bytes 9437184 | tf_op jit(solution)/shard_map/all_gather | solution.py:428
  7.3 1.0 copy-start.11
  8.3 75.4 %copy-start.7 = (s32[4]{0:T(128)}, s32[4]{0:T(128)S(1)}, u32[]{:S(2)}) copy-start(s32[4]{0:T(128)S(1)} %pad_add_fusion.where_ref) | copy-start | bytes 52
  8.3 1.6 copy-start.3
  8.3 2.2 %copy-start.4 = (bf16[512,2048]{1,0:T(8,128)(2,1)S(1)}, bf16[512,2048]{1,0:T(8,128)(2,1)}, u32[]{:S(2)}) copy-start(bf16[512,2048]{1,0:T(8,128)(2,1)} %w2_ref.2) | copy-start | bytes 6291460
  11.3 24.5 %copy-start.5 = (bf16[2048,384]{1,0:T(8,128)(2,1)S(1)}, bf16[2048,384]{1,0:T(8,128)(2,1)}, u32[]{:S(2)}) copy-start(bf16[2048,384]{1,0:T(8,128)(2,1)} %wqkv_ref) | copy-start | bytes 4718596
  11.3 22.7 %collective-permute-start.7 = (bf16[1024,512]{1,0:T(8,128)(2,1)S(1)}, bf16[1024,512]{1,0:T(8,128)(2,1)S(1)}, u32[]{:S(2)}, u32[]{:S(2)}) collective-permute-start(bf16[1024,512]{1,0:T(8,128)(2,1)S(1)} %shard_map.102), channel_id=1, source_target_pairs={{0,12},{4,0},{8,4},{12,8},{16,20},{20,24},{24,28},{28,16},{1,13},{... | collective-permute-start | bytes 3145736 | tf_op jit(solution)/shard_map/ppermute | solution.py:424
  13.5 17.8 %collective-permute-start = (bf16[32,2048]{1,0:T(8,128)(2,1)S(1)}, bf16[32,2048]{1,0:T(8,128)(2,1)S(1)}, u32[]{:S(2)}, u32[]{:S(2)}) collective-permute-start(bf16[32,2048]{1,0:T(8,128)(2,1)S(1)} %get-tuple-element.35), channel_id=1, source_target_pairs={{0,4},{4,8},{8,12},{12,0},{1,5},{5,9},{9,13},{13,1},{2,6},{6,10},{... | collective-permute-start | bytes 393224 | tf_op jit(solution)/shard_map/ppermute | solution.py:416
  14.8 19.1 %collective-permute-start.1 = (bf16[32,2048]{1,0:T(8,128)(2,1)S(1)}, bf16[32,2048]{1,0:T(8,128)(2,1)S(1)}, u32[]{:S(2)}, u32[]{:S(2)}) collective-permute-start(bf16[32,2048]{1,0:T(8,128)(2,1)S(1)} %get-tuple-element.36), channel_id=1, source_target_pairs={{0,8},{4,12},{8,0},{12,4},{1,9},{5,13},{9,1},{13,5},{2,10},{6,14},... | collective-permute-start | bytes 393224 | tf_op jit(solution)/shard_map/ppermute | solution.py:416
  16.2 17.7 %collective-permute-start.2 = (bf16[32,2048]{1,0:T(8,128)(2,1)S(1)}, bf16[32,2048]{1,0:T(8,128)(2,1)S(1)}, u32[]{:S(2)}, u32[]{:S(2)}) collective-permute-start(bf16[32,2048]{1,0:T(8,128)(2,1)S(1)} %get-tuple-element.37), channel_id=1, source_target_pairs={{0,12},{4,0},{8,4},{12,8},{1,13},{5,1},{9,5},{13,9},{2,14},{6,2},{... | collective-permute-start | bytes 393224 | tf_op jit(solution)/shard_map/ppermute | solution.py:416
  33.9 1.0 copy-start
  34.9 2.2 %copy-start.1 = (bf16[1024,512]{1,0:T(8,128)(2,1)S(1)}, bf16[1024,512]{1,0:T(8,128)(2,1)}, u32[]{:S(2)}) copy-start(bf16[1024,512]{1,0:T(8,128)(2,1)} %copy-done) | copy-start | bytes 3145732
  35.0 86.7 %all-gather.7.cloned.1.call-start = ((), (), s32[]{:S(2)}) async-start(), calls=%async_computation.2 | async-start | bytes 4718592 | tf_op jit(solution)/shard_map/all_gather | solution.py:462
  37.0 27.7 %copy-start.13 = (f32[2048]{0:T(1024)S(1)}, f32[2048]{0:T(1024)}, u32[]{:S(2)}) copy-start(f32[2048]{0:T(1024)} %param.13) | copy-start | bytes 24580
  37.1 26.9 %collective-permute-start.6 = (bf16[2064,384]{1,0:T(8,128)(2,1)}, bf16[2064,384]{1,0:T(8,128)(2,1)S(1)}, u32[]{:S(2)}, u32[]{:S(2)}) collective-permute-start(bf16[2064,384]{1,0:T(8,128)(2,1)} %shard_map.101.wq0), channel_id=1, source_target_pairs={{0,12},{4,0},{8,4},{12,8},{16,20},{20,24},{24,28},{28,16},{1,13},{... | collective-permute-start | bytes 4755464 | tf_op jit(solution)/shard_map/ppermute | solution.py:437
  37.7 26.2 %collective-permute-start.8 = (bf16[512,512]{1,0:T(8,128)(2,1)S(1)}, bf16[512,512]{1,0:T(8,128)(2,1)S(1)}, u32[]{:S(2)}, u32[]{:S(2)}) collective-permute-start(bf16[512,512]{1,0:T(8,128)(2,1)S(1)} %shard_map.103), channel_id=1, source_target_pairs={{0,12},{4,0},{8,4},{12,8},{16,20},{20,24},{24,28},{28,16},{1,13},{... | collective-permute-start | bytes 1572872 | tf_op jit(solution)/shard_map/ppermute | solution.py:430
  38.2 26.5 %collective-permute-start.3 = (bf16[128,2048]{1,0:T(8,128)(2,1)S(1)}, bf16[128,2048]{1,0:T(8,128)(2,1)S(1)}, u32[]{:S(2)}, u32[]{:S(2)}) collective-permute-start(bf16[128,2048]{1,0:T(8,128)(2,1)S(1)} %constant_dynamic-update-slice_fusion.a0), channel_id=1, source_target_pairs={{0,1},{1,2},{2,3},{3,0},{4,5},{5,6},{6,7},{7,4},{8,9},{9,10},{10,1... | collective-permute-start | bytes 1572872 | tf_op jit(solution)/shard_map/ppermute | solution.py:426
  39.5 25.2 %collective-permute-start.4 = (bf16[128,2048]{1,0:T(8,128)(2,1)S(1)}, bf16[128,2048]{1,0:T(8,128)(2,1)}, u32[]{:S(2)}, u32[]{:S(2)}) collective-permute-start(bf16[128,2048]{1,0:T(8,128)(2,1)S(1)} %constant_dynamic-update-slice_fusion.a0), channel_id=1, source_target_pairs={{0,2},{1,3},{2,0},{3,1},{4,6},{5,7},{6,4},{7,5},{8,10},{9,11},{10,... | collective-permute-start | bytes 1572872 | tf_op jit(solution)/shard_map/ppermute | solution.py:426
  41.9 22.8 %collective-permute-start.5 = (bf16[128,2048]{1,0:T(8,128)(2,1)S(1)}, bf16[128,2048]{1,0:T(8,128)(2,1)}, u32[]{:S(2)}, u32[]{:S(2)}) collective-permute-start(bf16[128,2048]{1,0:T(8,128)(2,1)S(1)} %constant_dynamic-update-slice_fusion.a0), channel_id=1, source_target_pairs={{0,3},{1,0},{2,1},{3,2},{4,7},{5,4},{6,5},{7,6},{8,11},{9,8},{10,9... | collective-permute-start | bytes 1572872 | tf_op jit(solution)/shard_map/ppermute | solution.py:426
  64.0 2.4 %copy-start.17 = (bf16[512,512]{1,0:T(8,128)(2,1)}, bf16[512,512]{1,0:T(8,128)(2,1)S(1)}, u32[]{:S(2)}) copy-start(bf16[512,512]{1,0:T(8,128)(2,1)S(1)} %collective-permute-done.8) | copy-start | bytes 1572868
  64.6 3.1 %copy-start.10 = (s32[1,8]{1,0:T(1,128)S(1)}, s32[1,8]{1,0:T(1,128)}, u32[]{:S(2)}) copy-start(s32[1,8]{1,0:T(1,128)} %count_ref.7) | copy-start | bytes 100
  64.6 3.1 %copy-start.14 = (s32[1,16]{1,0:T(1,128)S(1)}, s32[1,16]{1,0:T(1,128)}, u32[]{:S(2)}) copy-start(s32[1,16]{1,0:T(1,128)} %member_ref.3) | copy-start | bytes 196
  64.6 12.7 %collective-permute-start.10 = (bf16[1040,384]{1,0:T(8,128)(2,1)S(1)}, bf16[1040,384]{1,0:T(8,128)(2,1)}, u32[]{:S(2)}, u32[]{:S(2)}) collective-permute-start(bf16[1040,384]{1,0:T(8,128)(2,1)S(1)} %shard_map.105), channel_id=1, source_target_pairs={{0,12},{4,0},{8,4},{12,8},{16,20},{20,24},{24,28},{28,16},{1,13},{... | collective-permute-start | bytes 2396168 | tf_op jit(solution)/shard_map/ppermute | solution.py:449
  66.4 1.3 copy-start.2
  67.7 6.5 %copy-start.15 = (bf16[512,2048]{1,0:T(8,128)(2,1)}, bf16[512,2048]{1,0:T(8,128)(2,1)S(1)}, u32[]{:S(2)}) copy-start(bf16[512,2048]{1,0:T(8,128)(2,1)S(1)} %get-tuple-element.43.xn) | copy-start | bytes 6291460
  74.2 16.4 %copy-start.6 = (bf16[512,256]{1,0:T(8,128)(2,1)}, bf16[512,256]{1,0:T(8,128)(2,1)S(1)}, u32[]{:S(2)}) copy-start(bf16[512,256]{1,0:T(8,128)(2,1)S(1)} %shard_map.106.o0) | copy-start | bytes 786436
  77.3 6.4 %collective-permute-start.9 = (bf16[2064,384]{1,0:T(8,128)(2,1)S(1)}, bf16[2064,384]{1,0:T(8,128)(2,1)S(1)}, u32[]{:S(2)}, u32[]{:S(2)}) collective-permute-start(bf16[2064,384]{1,0:T(8,128)(2,1)S(1)} %collective-permute-done.6.got_ref.wq1), channel_id=1, source_target_pairs={{0,16},{16,0},{1,17},{17,1},{2,18},{18,2},{3,19},{19,3},{4,20},{20... | collective-permute-start | bytes 4755464 | tf_op jit(solution)/shard_map/ppermute | solution.py:447
  78.7 4.9 %collective-permute-start.11 = (bf16[1040,384]{1,0:T(8,128)(2,1)}, bf16[1040,384]{1,0:T(8,128)(2,1)S(1)}, u32[]{:S(2)}, u32[]{:S(2)}) collective-permute-start(bf16[1040,384]{1,0:T(8,128)(2,1)} %collective-permute-done.10.wqa), channel_id=1, source_target_pairs={{0,16},{16,0},{1,17},{17,1},{2,18},{18,2},{3,19},{19,3},{4,20},{20... | collective-permute-start | bytes 2396168 | tf_op jit(solution)/shard_map/ppermute | solution.py:463
  78.8 15.2 %collective-permute-start.15 = (bf16[512,256]{1,0:T(8,128)(2,1)S(1)}, bf16[512,256]{1,0:T(8,128)(2,1)S(1)}, u32[]{:S(2)}, u32[]{:S(2)}) collective-permute-start(bf16[512,256]{1,0:T(8,128)(2,1)S(1)} %shard_map.106.o0), channel_id=1, source_target_pairs={{0,1},{1,2},{2,3},{3,0},{4,5},{5,6},{6,7},{7,4},{8,9},{9,10},{10,1... | collective-permute-start | bytes 786440 | tf_op jit(solution)/shard_map/ppermute | solution.py:478
  80.1 15.2 %collective-permute-start.16 = (bf16[512,256]{1,0:T(8,128)(2,1)S(1)}, bf16[512,256]{1,0:T(8,128)(2,1)S(1)}, u32[]{:S(2)}, u32[]{:S(2)}) collective-permute-start(bf16[512,256]{1,0:T(8,128)(2,1)S(1)} %shard_map.106.o0), channel_id=1, source_target_pairs={{0,2},{1,3},{2,0},{3,1},{4,6},{5,7},{6,4},{7,5},{8,10},{9,11},{10,... | collective-permute-start | bytes 786440 | tf_op jit(solution)/shard_map/ppermute | solution.py:478
  82.5 12.7 %collective-permute-start.17 = (bf16[512,256]{1,0:T(8,128)(2,1)S(1)}, bf16[512,256]{1,0:T(8,128)(2,1)S(1)}, u32[]{:S(2)}, u32[]{:S(2)}) collective-permute-start(bf16[512,256]{1,0:T(8,128)(2,1)S(1)} %shard_map.106.o0), channel_id=1, source_target_pairs={{0,3},{1,0},{2,1},{3,2},{4,7},{5,4},{6,5},{7,6},{8,11},{9,8},{10,9... | collective-permute-start | bytes 786440 | tf_op jit(solution)/shard_map/ppermute | solution.py:478
  83.7 1.6 copy-start.16
  90.6 14.3 %copy-start.12 = (bf16[512,256]{1,0:T(8,128)(2,1)}, bf16[512,256]{1,0:T(8,128)(2,1)S(1)}, u32[]{:S(2)}) copy-start(bf16[512,256]{1,0:T(8,128)(2,1)S(1)} %shard_map.107.f0) | copy-start | bytes 786436
  90.6 14.3 %collective-permute-start.12 = (bf16[512,256]{1,0:T(8,128)(2,1)S(1)}, bf16[512,256]{1,0:T(8,128)(2,1)S(1)}, u32[]{:S(2)}, u32[]{:S(2)}) collective-permute-start(bf16[512,256]{1,0:T(8,128)(2,1)S(1)} %shard_map.107.f0), channel_id=1, source_target_pairs={{0,1},{1,2},{2,3},{3,0},{4,5},{5,6},{6,7},{7,4},{8,9},{9,10},{10,1... | collective-permute-start | bytes 786440 | tf_op jit(solution)/shard_map/ppermute | solution.py:479
  91.6 14.3 %collective-permute-start.13 = (bf16[512,256]{1,0:T(8,128)(2,1)S(1)}, bf16[512,256]{1,0:T(8,128)(2,1)S(1)}, u32[]{:S(2)}, u32[]{:S(2)}) collective-permute-start(bf16[512,256]{1,0:T(8,128)(2,1)S(1)} %shard_map.107.f0), channel_id=1, source_target_pairs={{0,2},{1,3},{2,0},{3,1},{4,6},{5,7},{6,4},{7,5},{8,10},{9,11},{10,... | collective-permute-start | bytes 786440 | tf_op jit(solution)/shard_map/ppermute | solution.py:479
  94.1 1.2 copy-start.18
  94.1 11.8 %collective-permute-start.14 = (bf16[512,256]{1,0:T(8,128)(2,1)S(1)}, bf16[512,256]{1,0:T(8,128)(2,1)S(1)}, u32[]{:S(2)}, u32[]{:S(2)}) collective-permute-start(bf16[512,256]{1,0:T(8,128)(2,1)S(1)} %shard_map.107.f0), channel_id=1, source_target_pairs={{0,3},{1,0},{2,1},{3,2},{4,7},{5,4},{6,5},{7,6},{8,11},{9,8},{10,9... | collective-permute-start | bytes 786440 | tf_op jit(solution)/shard_map/ppermute | solution.py:479
  95.2 0.8 copy-start.20
  104.9 1.0 copy-start.21
  105.9 0.8 copy-start.23
  132.5 34.2 %copy-start.8 = (s32[4]{0:T(128)S(1)}, s32[4]{0:T(128)}, u32[]{:S(2)}) copy-start(s32[4]{0:T(128)} %copy-done.7) | copy-start | bytes 52
  168.0 8.0 %collective-permute-start.18 = (bf16[24,2048]{1,0:T(8,128)(2,1)S(1)}, bf16[24,2048]{1,0:T(8,128)(2,1)S(1)}, u32[]{:S(2)}, u32[]{:S(2)}) collective-permute-start(bf16[24,2048]{1,0:T(8,128)(2,1)S(1)} %get-tuple-element.56), channel_id=1, source_target_pairs={{0,16},{16,32},{32,48},{48,64},{64,80},{80,96},{96,112},{112,0},{1... | collective-permute-start | bytes 294920 | tf_op jit(solution)/shard_map/ppermute | solution.py:526
  169.6 7.1 %collective-permute-start.19 = (bf16[24,2048]{1,0:T(8,128)(2,1)S(1)}, bf16[24,2048]{1,0:T(8,128)(2,1)S(1)}, u32[]{:S(2)}, u32[]{:S(2)}) collective-permute-start(bf16[24,2048]{1,0:T(8,128)(2,1)S(1)} %get-tuple-element.57), channel_id=1, source_target_pairs={{0,32},{16,48},{32,64},{48,80},{64,96},{80,112},{96,0},{112,16},{1... | collective-permute-start | bytes 294920 | tf_op jit(solution)/shard_map/ppermute | solution.py:526
  170.6 7.5 %collective-permute-start.20 = (bf16[24,2048]{1,0:T(8,128)(2,1)S(1)}, bf16[24,2048]{1,0:T(8,128)(2,1)S(1)}, u32[]{:S(2)}, u32[]{:S(2)}) collective-permute-start(bf16[24,2048]{1,0:T(8,128)(2,1)S(1)} %get-tuple-element.58), channel_id=1, source_target_pairs={{0,48},{16,64},{32,80},{48,96},{64,112},{80,0},{96,16},{112,32},{1... | collective-permute-start | bytes 294920 | tf_op jit(solution)/shard_map/ppermute | solution.py:526
  172.7 8.4 %collective-permute-start.21 = (bf16[24,2048]{1,0:T(8,128)(2,1)S(1)}, bf16[24,2048]{1,0:T(8,128)(2,1)S(1)}, u32[]{:S(2)}, u32[]{:S(2)}) collective-permute-start(bf16[24,2048]{1,0:T(8,128)(2,1)S(1)} %get-tuple-element.59), channel_id=1, source_target_pairs={{0,64},{16,80},{32,96},{48,112},{64,0},{80,16},{96,32},{112,48},{1... | collective-permute-start | bytes 294920 | tf_op jit(solution)/shard_map/ppermute | solution.py:526
  173.4 8.3 %collective-permute-start.22 = (bf16[24,2048]{1,0:T(8,128)(2,1)S(1)}, bf16[24,2048]{1,0:T(8,128)(2,1)S(1)}, u32[]{:S(2)}, u32[]{:S(2)}) collective-permute-start(bf16[24,2048]{1,0:T(8,128)(2,1)S(1)} %get-tuple-element.60), channel_id=1, source_target_pairs={{0,80},{16,96},{32,112},{48,0},{64,16},{80,32},{96,48},{112,64},{1... | collective-permute-start | bytes 294920 | tf_op jit(solution)/shard_map/ppermute | solution.py:526
  176.0 5.7 %collective-permute-start.23 = (bf16[24,2048]{1,0:T(8,128)(2,1)S(1)}, bf16[24,2048]{1,0:T(8,128)(2,1)S(1)}, u32[]{:S(2)}, u32[]{:S(2)}) collective-permute-start(bf16[24,2048]{1,0:T(8,128)(2,1)S(1)} %get-tuple-element.61), channel_id=1, source_target_pairs={{0,96},{16,112},{32,0},{48,16},{64,32},{80,48},{96,64},{112,80},{1... | collective-permute-start | bytes 294920 | tf_op jit(solution)/shard_map/ppermute | solution.py:526
  176.8 5.8 %collective-permute-start.24 = (bf16[24,2048]{1,0:T(8,128)(2,1)S(1)}, bf16[24,2048]{1,0:T(8,128)(2,1)S(1)}, u32[]{:S(2)}, u32[]{:S(2)}) collective-permute-start(bf16[24,2048]{1,0:T(8,128)(2,1)S(1)} %get-tuple-element.62), channel_id=1, source_target_pairs={{0,112},{16,0},{32,16},{48,32},{64,48},{80,64},{96,80},{112,96},{1... | collective-permute-start | bytes 294920 | tf_op jit(solution)/shard_map/ppermute | solution.py:526
  (3 other events, 2.1 us)
Sparse Core Ops, SparseCore 0:
  35.1 52.4 all-gather.4
  89.3 32.3 all-gather.6

commit v4 on v3

--- a/solution.py
+++ b/solution.py
@@ -255,8 +255,8 @@
 
 
 def merge_kernel(
-    where_ref, f0, f1, f2, f3, gain_ref, part_ref, wm_ref, w1_ref, all_ref,
-    fed_ref, kept_ref, out_ref, wm, heads, total, w1, sem,
+    where_ref, f0, f1, f2, f3, gain_ref, part_ref, wm_ref, w1_ref, w2_ref, all_ref,
+    fed_ref, sums_ref, wm, heads, total, w1, w2, hidden, sem,
 ):
     c, y, x = where_ref[1], where_ref[2], where_ref[3]
     step = 1 - 2 * c
@@ -286,7 +286,21 @@
                 for z in range(4)
             ]
         )
-    for group in merges + ups:
+    downs = []
+    for n in range(4):
+        cols = pl.ds(512 * n, 512)
+        down = [pltpu.make_async_copy(w2_ref.at[:, cols], w2.at[pl.ds(0, 512), cols], sem.at[7 + n])]
+        for half in range(2):
+            for z in range(4):
+                down.append(
+                    pltpu.make_async_copy(
+                        all_ref.at[2 * z + half, pl.ds(512 + 128 * n, 128)],
+                        w2.at[pl.ds(512 * (1 + half) + 128 * z, 128), cols],
+                        sem.at[7 + n],
+                    )
+                )
+        downs.append(down)
+    for group in merges + ups + downs:
         for copy in group:
             copy.start()
     for m, ref in enumerate((f0, f1, f2, f3)):
@@ -305,73 +319,55 @@
     for n in range(4):
         cols = slice(512 * n, 512 * n + 512)
         fed_ref[:, cols] = (total[:, cols] * scale * gain_ref[:, cols]).astype(BF16)
-    kept_ref[...] = total[:128]
     for i in range(3):
         for copy in ups[i]:
             copy.wait()
-        out_ref[:, 512 * i : 512 * i + 512] = jax.nn.gelu(
+        hidden[:, 512 * i : 512 * i + 512] = jax.nn.gelu(
             dot(fed_ref[...], w1[i]), approximate=True
         ).astype(BF16)
-
-
-def far_mlp_kernel(
-    where_ref, fed_ref, kept_ref, hidden_ref, w2_ref, near_ref, far_ref, out_ref,
-    w1, w2, hidden, kept, sem,
-):
+    for n in range(4):
+        cols = slice(512 * n, 512 * n + 512)
+        for copy in downs[n]:
+            copy.wait()
+        part = dot(hidden[...], w2[:, cols])
+        sums_ref[:128, cols] = total[:128, cols] + part[:128]
+        sums_ref[128:, cols] = part[128:]
+
+
+def far_mlp_kernel(where_ref, fed_ref, part_ref, all_ref, out_ref, w1, w2, sums, sem):
     ups, downs = [], []
     for z in range(4):
         for c in range(2):
-            block = far_ref.at[2 * z + c]
+            block = all_ref.at[2 * z + c]
             ups.append(
                 pltpu.make_async_copy(
                     block.at[pl.ds(0, 256)], w1.at[pl.ds(512 * z + 256 * c, 256)], sem.at[0]
                 )
             )
-    carried = [
-        pltpu.make_async_copy(hidden_ref, hidden.at[:, pl.ds(0, 1536)], sem.at[1]),
-        pltpu.make_async_copy(kept_ref, kept, sem.at[1]),
-    ]
-    for n in range(4):
-        cols = pl.ds(512 * n, 512)
-        down = [pltpu.make_async_copy(w2_ref.at[:, cols], w2.at[pl.ds(0, 512), cols], sem.at[2 + n])]
-        for c in range(2):
-            for z in range(4):
-                down.append(
+            for n in range(4):
+                downs.append(
                     pltpu.make_async_copy(
-                        near_ref.at[2 * z + c, pl.ds(512 + 128 * n, 128)],
-                        w2.at[pl.ds(512 * (1 + c) + 128 * z, 128), cols],
-                        sem.at[2 + n],
+                        block.at[pl.ds(256 + 64 * n, 64)],
+                        w2.at[pl.ds(128 * z + 64 * c, 64), pl.ds(512 * n, 512)],
+                        sem.at[1],
                     )
                 )
-                down.append(
-                    pltpu.make_async_copy(
-                        far_ref.at[2 * z + c, pl.ds(256 + 64 * n, 64)],
-                        w2.at[pl.ds(1536 + 128 * z + 64 * c, 64), cols],
-                        sem.at[2 + n],
-                    )
-                )
-        downs.append(down)
-    for copies in [ups, carried, *downs]:
-        for copy in copies:
-            copy.start()
+    carried = pltpu.make_async_copy(part_ref, sums, sem.at[2])
+    for copy in [*ups, *downs, carried]:
+        copy.start()
     for copy in ups:
         copy.wait()
-    hidden[:, 1536:] = jax.nn.gelu(dot(fed_ref[...], w1[...]), approximate=True).astype(BF16)
-    for copy in carried:
+    hidden = jax.nn.gelu(dot(fed_ref[...], w1[...]), approximate=True).astype(BF16)
+    for copy in [*downs, carried]:
         copy.wait()
     for n in range(4):
         cols = slice(512 * n, 512 * n + 512)
-        for copy in downs[n]:
-            copy.wait()
-        part = dot(hidden[...], w2[:, cols])
+        part = sums[:, cols] + dot(hidden, w2[:, cols])
         for j in range(SIDE):
             for k in range(SIDE):
                 rows = slice(128 * j + 32 * k, 128 * j + 32 * k + 32)
                 home = ((where_ref[2] - k + 4) & 3) * SIDE + ((where_ref[3] - j + 4) & 3)
-                block = part[rows]
-                if j == 0:
-                    block = block + kept[rows, cols]
-                out_ref[home, :, cols] = block.astype(BF16)
+                out_ref[home, :, cols] = part[rows].astype(BF16)
 
 
 def leave_kernel(where_ref, count_ref, parts_ref, *outs):
@@ -488,36 +484,37 @@
         moved=12 * 2**20,
     )(where, *first, kept_rows, wmerge)
     second[0], near_all = lax.optimization_barrier((second[0], near_all))
-    fed, kept, near_hidden = call(
+    fed, near_part = call(
         merge_kernel,
-        [shape((512, 2048)), shape((128, 2048), F32), shape((512, 1536))],
-        [SMEM] + [VMEM] * 5 + [ANY] * 4,
+        [shape((512, 2048)), shape((512, 2048), F32)],
+        [SMEM] + [VMEM] * 5 + [ANY] * 5,
         scratch
         + [
             pltpu.VMEM((512, 2048), F32),
             pltpu.VMEM((3, 2048, 512), BF16),
-            pltpu.SemaphoreType.DMA((7,)),
+            pltpu.VMEM((1536, 2048), BF16),
+            pltpu.VMEM((512, 1536), BF16),
+            pltpu.SemaphoreType.DMA((11,)),
         ],
         vmem=60,
         flops=25 * 10**9,
-        moved=24 * 2**20,
-    )(where, *second, gain2, merged, wmerge, w1, near_all)
+        moved=34 * 2**20,
+    )(where, *second, gain2, merged, wmerge, w1, w2, near_all)
 
     [parts] = call(
         far_mlp_kernel,
         [shape((16, 32, 2048))],
-        [SMEM, VMEM] + [ANY] * 5,
+        [SMEM, VMEM] + [ANY] * 2,
         [
             pltpu.VMEM((2048, 512), BF16),
-            pltpu.VMEM((2048, 2048), BF16),
             pltpu.VMEM((512, 2048), BF16),
-            pltpu.VMEM((128, 2048), F32),
-            pltpu.SemaphoreType.DMA((6,)),
+            pltpu.VMEM((512, 2048), F32),
+            pltpu.SemaphoreType.DMA((3,)),
         ],
         vmem=60,
-        flops=6 * 10**9,
-        moved=14 * 2**20,
-    )(where, fed, kept, near_hidden, w2, near_all, far_all)
+        flops=2 * 10**9,
+        moved=10 * 2**20,
+    )(where, fed, near_part, far_all)
     parts = lax.all_to_all(parts, ("y", "x"), 0, 0, tiled=True)
     leaving = call(leave_kernel, [shape((CAP, 2048))] * 8, [SMEM, SMEM, VMEM], vmem=14)(
         where, tallies, parts

time: 191 us -> 192 us (level)
  waiting for transfers between devices: 50.1 us -> 46 us
  starting transfers between devices: 31.7 us -> 35 us
    ppermute x7, starting transfers between devices: 8.29 us -> 11.6 us  [body(): got += [lax.ppermute(leaving[m], DP, ring(N_DP, m)) for m in range(1, N_DP)]]
    all_gather x1, waiting for transfers between devices: 3.17 us -> 0.02 us  [body(): far_all = lax.all_gather(far, DP, axis=0, tiled=False)]
  transfers between devices with their start and end apart: 27 -> 27, of which waited for: 11 -> 8; matrix products, arithmetic and copies ran while one was open for 0% -> 0% of each run, Pallas kernels for 19% -> 21%
where the time goes in v4:
time: 192 us
  Pallas kernels  53.2 us (28%)
  waiting for transfers between devices  46 us (24%)
  starting transfers between devices  35 us (18%)
  blocking collectives  34.7 us (18%)
  between operations  14.5 us (8%)
  local copies, waits for them, and re-layouts  8.56 us (4%)
    all_to_all x1, blocking collectives, body(): parts = lax.all_to_all(parts, ('y', 'x'), 0, 0, tiled=True)  34.7 us
    ppermute x1, waiting for transfers between devices, body(): far = lax.ppermute(near_half, cy, twin_ring())  20.9 us
    pallas_call x1, Pallas kernels, body(): call(merge_kernel, [shape((512, 2048)), shape((512, 2048), F32)], [SMEM]...  16.5 us
    ppermute x3, waiting for transfers between devices, body(): lax.ppermute(blocks[k], 'y', ring(SIDE, k))  15.7 us
    ppermute x7, starting transfers between devices, body(): got += [lax.ppermute(leaving[m], DP, ring(N_DP, m)) for m in range(1, N_DP)]  11.6 us
    pallas_call x1, Pallas kernels, body(): call(merge_first_kernel, [shape((512, 2048), F32)], [SMEM] + [VMEM] * 4 +...  8.87 us
    unnamed x51, local copies, waits for them, and re-layouts  8.55 us
    pallas_call x1, Pallas kernels, body(): call(far_mlp_kernel, [shape((16, 32, 2048))], [SMEM, VMEM] + [ANY] * 2, [...  7.67 us
  transfers between devices with their start and end apart: 27, of which 8 were waited for; matrix products, arithmetic and copies ran while one was open for 0% of the time, Pallas kernels for 21%

profile of v4, /device:TPU:1, one launch (start us, length us, event | category | flops | bytes accessed | tf_op | source)
XLA Modules:
  0.0 192.0 jit_solution(16168788860084890298)
XLA Ops:
  6.6 0.7 copy-done.9
  7.3 1.0 copy-done.11
  8.3 0.9 shard_map.100
  9.2 0.7 copy-done.3
  9.9 0.6 copy-done.4
  10.5 0.7 shard_map.102
  11.3 2.2 %collective-permute-start.7 = (bf16[1024,512]{1,0:T(8,128)(2,1)S(1)}, bf16[1024,512]{1,0:T(8,128)(2,1)S(1)}, u32[]{:S(2)}, u32[]{:S(2)}) collective-permute-start(bf16[1024,512]{1,0:T(8,128)(2,1)S(1)} %shard_map.102), channel_id=1, source_target_pairs={{0,12},{4,0},{8,4},{12,8},{16,20},{20,24},{24,28},{28,16},{1,13},{... | collective-permute-start | bytes 3145736 | tf_op jit(solution)/shard_map/ppermute | solution.py:420
  13.5 1.3 collective-permute-start
  14.8 1.4 collective-permute-start.1
  16.2 2.0 %collective-permute-start.2 = (bf16[32,2048]{1,0:T(8,128)(2,1)S(1)}, bf16[32,2048]{1,0:T(8,128)(2,1)S(1)}, u32[]{:S(2)}, u32[]{:S(2)}) collective-permute-start(bf16[32,2048]{1,0:T(8,128)(2,1)S(1)} %get-tuple-element.36), channel_id=1, source_target_pairs={{0,12},{4,0},{8,4},{12,8},{1,13},{5,1},{9,5},{13,9},{2,14},{6,2},{... | collective-permute-start | bytes 393224 | tf_op jit(solution)/shard_map/ppermute | solution.py:412
  18.2 13.1 %collective-permute-done = bf16[32,2048]{1,0:T(8,128)(2,1)S(1)} collective-permute-done((bf16[32,2048]{1,0:T(8,128)(2,1)S(1)}, bf16[32,2048]{1,0:T(8,128)(2,1)S(1)}, u32[]{:S(2)}, u32[]{:S(2)}) %collective-permute-start) | collective-permute-done | bytes 131104 | tf_op jit(solution)/shard_map/ppermute | solution.py:412
  31.3 2.6 %collective-permute-done.1 = bf16[32,2048]{1,0:T(8,128)(2,1)S(1)} collective-permute-done((bf16[32,2048]{1,0:T(8,128)(2,1)S(1)}, bf16[32,2048]{1,0:T(8,128)(2,1)S(1)}, u32[]{:S(2)}, u32[]{:S(2)}) %collective-permute-start.1) | collective-permute-done | bytes 131104 | tf_op jit(solution)/shard_map/ppermute | solution.py:412
  33.9 1.0 copy-done
  35.7 1.3 shard_map.101.wq0
  38.2 1.2 collective-permute-start.3
  39.5 2.5 %collective-permute-start.4 = (bf16[128,2048]{1,0:T(8,128)(2,1)S(1)}, bf16[128,2048]{1,0:T(8,128)(2,1)}, u32[]{:S(2)}, u32[]{:S(2)}) collective-permute-start(bf16[128,2048]{1,0:T(8,128)(2,1)S(1)} %constant_dynamic-update-slice_fusion.a0), channel_id=1, source_target_pairs={{0,2},{1,3},{2,0},{3,1},{4,6},{5,7},{6,4},{7,5},{8,10},{9,11},{10,... | collective-permute-start | bytes 1572872 | tf_op jit(solution)/shard_map/ppermute | solution.py:422
  41.9 1.2 collective-permute-start.5
  43.1 20.9 %collective-permute-done.8 = bf16[512,512]{1,0:T(8,128)(2,1)S(1)} collective-permute-done((bf16[512,512]{1,0:T(8,128)(2,1)S(1)}, bf16[512,512]{1,0:T(8,128)(2,1)S(1)}, u32[]{:S(2)}, u32[]{:S(2)}) %collective-permute-start.8) | collective-permute-done | bytes 524320 | tf_op jit(solution)/shard_map/ppermute | solution.py:426
  64.0 0.6 shard_map.105
  64.7 1.6 shard_map.104
  66.4 1.3 copy-done.2
  67.7 6.5 %shard_map.106.o0 = bf16[512,256]{1,0:T(8,128)(2,1)S(1)} custom-call(s32[4]{0:T(128)S(1)} %pad_add_fusion.where_ref, s32[1,8]{1,0:T(1,128)S(1)} %copy-done.10, s32[1,16]{1,0:T(1,128)S(1)} %copy-done.14, bf16[512,2048]{1,0:T(8,128)(2,1)S(1)} %get-tuple-element.42.xn, bf16[2064,384]{1,0:T(8,128)(2,1)} %shard_map.101.wq0, ...), custom_call_target="tpu_custom_call" | custom-call | flops 2000000000 | bytes 8388608 | tf_op jit(solution)/shard_map/pallas_call | solution.py:447
  74.2 3.1 %collective-permute-done.10.wqa = bf16[1040,384]{1,0:T(8,128)(2,1)} collective-permute-done((bf16[1040,384]{1,0:T(8,128)(2,1)S(1)}, bf16[1040,384]{1,0:T(8,128)(2,1)}, u32[]{:S(2)}, u32[]{:S(2)}) %collective-permute-start.10) | collective-permute-done | bytes 798752 | tf_op jit(solution)/shard_map/ppermute | solution.py:445
  77.3 1.5 collective-permute-start.9
  78.8 1.2 collective-permute-start.15
  80.1 2.5 %collective-permute-start.16 = (bf16[512,256]{1,0:T(8,128)(2,1)S(1)}, bf16[512,256]{1,0:T(8,128)(2,1)S(1)}, u32[]{:S(2)}, u32[]{:S(2)}) collective-permute-start(bf16[512,256]{1,0:T(8,128)(2,1)S(1)} %shard_map.106.o0), channel_id=1, source_target_pairs={{0,2},{1,3},{2,0},{3,1},{4,6},{5,7},{6,4},{7,5},{8,10},{9,11},{10,... | collective-permute-start | bytes 786440 | tf_op jit(solution)/shard_map/ppermute | solution.py:474
  82.5 1.2 collective-permute-start.17
  83.7 1.6 copy-done.16
  85.3 5.3 %shard_map.107.f0 = bf16[512,256]{1,0:T(8,128)(2,1)S(1)} custom-call(s32[4]{0:T(128)S(1)} %pad_add_fusion.where_ref, s32[1,8]{1,0:T(1,128)S(1)} %copy-done.10, s32[1,16]{1,0:T(1,128)S(1)} %copy-done.14, bf16[512,2048]{1,0:T(8,128)(2,1)S(1)} %copy-done.16, bf16[2064,384]{1,0:T(8,128)(2,1)S(1)} %collective-permute-done.9.wq2, ...), custom_call_target="tpu_custom_call" | custom-call | flops 2000000000 | bytes 8388608 | tf_op jit(solution)/shard_map/pallas_call | solution.py:460
  90.6 1.0 collective-permute-start.12
  91.6 2.5 %collective-permute-start.13 = (bf16[512,256]{1,0:T(8,128)(2,1)S(1)}, bf16[512,256]{1,0:T(8,128)(2,1)S(1)}, u32[]{:S(2)}, u32[]{:S(2)}) collective-permute-start(bf16[512,256]{1,0:T(8,128)(2,1)S(1)} %shard_map.107.f0), channel_id=1, source_target_pairs={{0,2},{1,3},{2,0},{3,1},{4,6},{5,7},{6,4},{7,5},{8,10},{9,11},{10,... | collective-permute-start | bytes 786440 | tf_op jit(solution)/shard_map/ppermute | solution.py:475
  94.1 1.2 collective-permute-start.14
  95.3 0.7 copy-done.19
  96.0 8.9 %shard_map.108.part_ref = f32[512,2048]{1,0:T(8,128)} custom-call(s32[4]{0:T(128)} %copy-done.7, bf16[512,256]{1,0:T(8,128)(2,1)} %copy-done.6, bf16[512,256]{1,0:T(8,128)(2,1)} %copy-done.18, bf16[512,256]{1,0:T(8,128)(2,1)} %copy-done.19, bf16[512,256]{1,0:T(8,128)(2,1)} %copy-done.20, bf16[512,2048]{1,0:T(8,128)(2,1)} %copy-done.2, bf16[2048,2048]{1,0:T(8,128)(2,1)} %wm_ref.3), custom_call_target="tpu_custom_call" | custom-call | flops 2000000000 | bytes 12582912 | tf_op jit(solution)/shard_map/pallas_call | solution.py:477
  105.0 0.9 collective-permute-done.13.f2
  105.9 0.7 copy-done.22
  106.7 16.5 %shard_map.109 = (bf16[512,2048]{1,0:T(8,128)(2,1)}, f32[512,2048]{1,0:T(8,128)}) custom-call(s32[4]{0:T(128)} %copy-done.7, bf16[512,256]{1,0:T(8,128)(2,1)} %copy-done.12, bf16[512,256]{1,0:T(8,128)(2,1)} %copy-done.21, bf16[512,256]{1,0:T(8,128)(2,1)} %copy-done.22, bf16[512,256]{1,0:T(8,128)(2,1)} %copy-done.23, f32[1,2048]{1,0:T(1,128)} %bitcast.12, ...), custom_call_target="tpu_custom_call" | custom-call | flops 24999999488 | bytes 35651584 | tf_op jit(solution)/shard_map/pallas_call | solution.py:487
  123.2 7.7 %shard_map.110 = bf16[16,32,2048]{2,1,0:T(8,128)(2,1)} custom-call(s32[4]{0:T(128)} %copy-done.7, bf16[512,2048]{1,0:T(8,128)(2,1)} %get-tuple-element.49.fed_ref, f32[512,2048]{1,0:T(8,128)} %get-tuple-element.50.part_ref, bf16[8,512,512]{2,1,0:T(8,128)(2,1)} %bitcast.10), custom_call_target="tpu_custom_call" | custom-call | flops 2000000000 | bytes 10485760 | tf_op jit(solution)/shard_map/pallas_call | solution.py:504
  130.9 34.7 %all_to_all.5.parts_ref = bf16[16,32,2048]{2,1,0:T(8,128)(2,1)S(1)} all-to-all(bf16[16,32,2048]{2,1,0:T(8,128)(2,1)} %shard_map.110), channel_id=1, replica_groups=mesh['z'=4,'c'=2,'y'=4,'x'=4] {'y','x'}, dimensions={0} | all-to-all | bytes 4194304 | tf_op jit(solution)/shard_map/all_to_all | solution.py:518
  165.6 1.2 shard_map.111
  166.8 3.5 %collective-permute-start.18 = (bf16[24,2048]{1,0:T(8,128)(2,1)S(1)}, bf16[24,2048]{1,0:T(8,128)(2,1)S(1)}, u32[]{:S(2)}, u32[]{:S(2)}) collective-permute-start(bf16[24,2048]{1,0:T(8,128)(2,1)S(1)} %get-tuple-element.54), channel_id=1, source_target_pairs={{0,16},{16,32},{32,48},{48,64},{64,80},{80,96},{96,112},{112,0},{1... | collective-permute-start | bytes 294920 | tf_op jit(solution)/shard_map/ppermute | solution.py:523
  170.3 1.7 collective-permute-start.19
  172.1 2.1 %collective-permute-start.20 = (bf16[24,2048]{1,0:T(8,128)(2,1)S(1)}, bf16[24,2048]{1,0:T(8,128)(2,1)S(1)}, u32[]{:S(2)}, u32[]{:S(2)}) collective-permute-start(bf16[24,2048]{1,0:T(8,128)(2,1)S(1)} %get-tuple-element.56), channel_id=1, source_target_pairs={{0,48},{16,64},{32,80},{48,96},{64,112},{80,0},{96,16},{112,32},{1... | collective-permute-start | bytes 294920 | tf_op jit(solution)/shard_map/ppermute | solution.py:523
  174.2 2.3 %collective-permute-start.22 = (bf16[24,2048]{1,0:T(8,128)(2,1)S(1)}, bf16[24,2048]{1,0:T(8,128)(2,1)S(1)}, u32[]{:S(2)}, u32[]{:S(2)}) collective-permute-start(bf16[24,2048]{1,0:T(8,128)(2,1)S(1)} %get-tuple-element.58), channel_id=1, source_target_pairs={{0,80},{16,96},{32,112},{48,0},{64,16},{80,32},{96,48},{112,64},{1... | collective-permute-start | bytes 294920 | tf_op jit(solution)/shard_map/ppermute | solution.py:523
  176.5 0.8 collective-permute-start.23
  177.3 1.1 collective-permute-start.24
  178.5 4.1 %collective-permute-done.21.refs_4_ = bf16[24,2048]{1,0:T(8,128)(2,1)S(1)} collective-permute-done((bf16[24,2048]{1,0:T(8,128)(2,1)S(1)}, bf16[24,2048]{1,0:T(8,128)(2,1)S(1)}, u32[]{:S(2)}, u32[]{:S(2)}) %collective-permute-start.21) | collective-permute-done | bytes 98336 | tf_op jit(solution)/shard_map/ppermute | solution.py:523
  183.7 1.5 shard_map.112
  (75 shorter events, 3.0 us)
Async XLA Ops:
  6.5 98.4 %all-gather.5.cloned.1.call-start = ((), (), s32[]{:S(2)}) async-start(), calls=%async_computation.1 | async-start | bytes 9437184 | tf_op jit(solution)/shard_map/all_gather | solution.py:424
  7.3 1.0 copy-start.11
  8.3 75.4 %copy-start.7 = (s32[4]{0:T(128)}, s32[4]{0:T(128)S(1)}, u32[]{:S(2)}) copy-start(s32[4]{0:T(128)S(1)} %pad_add_fusion.where_ref) | copy-start | bytes 52
  8.3 1.6 copy-start.3
  8.3 2.2 %copy-start.4 = (bf16[512,2048]{1,0:T(8,128)(2,1)S(1)}, bf16[512,2048]{1,0:T(8,128)(2,1)}, u32[]{:S(2)}) copy-start(bf16[512,2048]{1,0:T(8,128)(2,1)} %w2_ref.2) | copy-start | bytes 6291460
  11.3 24.5 %copy-start.5 = (bf16[2048,384]{1,0:T(8,128)(2,1)S(1)}, bf16[2048,384]{1,0:T(8,128)(2,1)}, u32[]{:S(2)}) copy-start(bf16[2048,384]{1,0:T(8,128)(2,1)} %wqkv_ref) | copy-start | bytes 4718596
  11.3 22.7 %collective-permute-start.7 = (bf16[1024,512]{1,0:T(8,128)(2,1)S(1)}, bf16[1024,512]{1,0:T(8,128)(2,1)S(1)}, u32[]{:S(2)}, u32[]{:S(2)}) collective-permute-start(bf16[1024,512]{1,0:T(8,128)(2,1)S(1)} %shard_map.102), channel_id=1, source_target_pairs={{0,12},{4,0},{8,4},{12,8},{16,20},{20,24},{24,28},{28,16},{1,13},{... | collective-permute-start | bytes 3145736 | tf_op jit(solution)/shard_map/ppermute | solution.py:420
  13.5 17.8 %collective-permute-start = (bf16[32,2048]{1,0:T(8,128)(2,1)S(1)}, bf16[32,2048]{1,0:T(8,128)(2,1)S(1)}, u32[]{:S(2)}, u32[]{:S(2)}) collective-permute-start(bf16[32,2048]{1,0:T(8,128)(2,1)S(1)} %get-tuple-element.34), channel_id=1, source_target_pairs={{0,4},{4,8},{8,12},{12,0},{1,5},{5,9},{9,13},{13,1},{2,6},{6,10},{... | collective-permute-start | bytes 393224 | tf_op jit(solution)/shard_map/ppermute | solution.py:412
  14.8 19.1 %collective-permute-start.1 = (bf16[32,2048]{1,0:T(8,128)(2,1)S(1)}, bf16[32,2048]{1,0:T(8,128)(2,1)S(1)}, u32[]{:S(2)}, u32[]{:S(2)}) collective-permute-start(bf16[32,2048]{1,0:T(8,128)(2,1)S(1)} %get-tuple-element.35), channel_id=1, source_target_pairs={{0,8},{4,12},{8,0},{12,4},{1,9},{5,13},{9,1},{13,5},{2,10},{6,14},... | collective-permute-start | bytes 393224 | tf_op jit(solution)/shard_map/ppermute | solution.py:412
  16.2 17.7 %collective-permute-start.2 = (bf16[32,2048]{1,0:T(8,128)(2,1)S(1)}, bf16[32,2048]{1,0:T(8,128)(2,1)S(1)}, u32[]{:S(2)}, u32[]{:S(2)}) collective-permute-start(bf16[32,2048]{1,0:T(8,128)(2,1)S(1)} %get-tuple-element.36), channel_id=1, source_target_pairs={{0,12},{4,0},{8,4},{12,8},{1,13},{5,1},{9,5},{13,9},{2,14},{6,2},{... | collective-permute-start | bytes 393224 | tf_op jit(solution)/shard_map/ppermute | solution.py:412
  33.9 1.0 copy-start
  34.9 2.2 %copy-start.1 = (bf16[1024,512]{1,0:T(8,128)(2,1)S(1)}, bf16[1024,512]{1,0:T(8,128)(2,1)}, u32[]{:S(2)}) copy-start(bf16[1024,512]{1,0:T(8,128)(2,1)} %copy-done) | copy-start | bytes 3145732
  35.0 88.2 %all-gather.7.cloned.1.call-start = ((), (), s32[]{:S(2)}) async-start(), calls=%async_computation.2 | async-start | bytes 4718592 | tf_op jit(solution)/shard_map/all_gather | solution.py:458
  37.0 27.7 %copy-start.13 = (f32[2048]{0:T(1024)S(1)}, f32[2048]{0:T(1024)}, u32[]{:S(2)}) copy-start(f32[2048]{0:T(1024)} %param.13) | copy-start | bytes 24580
  37.1 26.9 %collective-permute-start.6 = (bf16[2064,384]{1,0:T(8,128)(2,1)}, bf16[2064,384]{1,0:T(8,128)(2,1)S(1)}, u32[]{:S(2)}, u32[]{:S(2)}) collective-permute-start(bf16[2064,384]{1,0:T(8,128)(2,1)} %shard_map.101.wq0), channel_id=1, source_target_pairs={{0,12},{4,0},{8,4},{12,8},{16,20},{20,24},{24,28},{28,16},{1,13},{... | collective-permute-start | bytes 4755464 | tf_op jit(solution)/shard_map/ppermute | solution.py:433
  37.7 26.2 %collective-permute-start.8 = (bf16[512,512]{1,0:T(8,128)(2,1)S(1)}, bf16[512,512]{1,0:T(8,128)(2,1)S(1)}, u32[]{:S(2)}, u32[]{:S(2)}) collective-permute-start(bf16[512,512]{1,0:T(8,128)(2,1)S(1)} %shard_map.103), channel_id=1, source_target_pairs={{0,12},{4,0},{8,4},{12,8},{16,20},{20,24},{24,28},{28,16},{1,13},{... | collective-permute-start | bytes 1572872 | tf_op jit(solution)/shard_map/ppermute | solution.py:426
  38.2 26.5 %collective-permute-start.3 = (bf16[128,2048]{1,0:T(8,128)(2,1)S(1)}, bf16[128,2048]{1,0:T(8,128)(2,1)S(1)}, u32[]{:S(2)}, u32[]{:S(2)}) collective-permute-start(bf16[128,2048]{1,0:T(8,128)(2,1)S(1)} %constant_dynamic-update-slice_fusion.a0), channel_id=1, source_target_pairs={{0,1},{1,2},{2,3},{3,0},{4,5},{5,6},{6,7},{7,4},{8,9},{9,10},{10,1... | collective-permute-start | bytes 1572872 | tf_op jit(solution)/shard_map/ppermute | solution.py:422
  39.5 25.2 %collective-permute-start.4 = (bf16[128,2048]{1,0:T(8,128)(2,1)S(1)}, bf16[128,2048]{1,0:T(8,128)(2,1)}, u32[]{:S(2)}, u32[]{:S(2)}) collective-permute-start(bf16[128,2048]{1,0:T(8,128)(2,1)S(1)} %constant_dynamic-update-slice_fusion.a0), channel_id=1, source_target_pairs={{0,2},{1,3},{2,0},{3,1},{4,6},{5,7},{6,4},{7,5},{8,10},{9,11},{10,... | collective-permute-start | bytes 1572872 | tf_op jit(solution)/shard_map/ppermute | solution.py:422
  41.9 22.8 %collective-permute-start.5 = (bf16[128,2048]{1,0:T(8,128)(2,1)S(1)}, bf16[128,2048]{1,0:T(8,128)(2,1)}, u32[]{:S(2)}, u32[]{:S(2)}) collective-permute-start(bf16[128,2048]{1,0:T(8,128)(2,1)S(1)} %constant_dynamic-update-slice_fusion.a0), channel_id=1, source_target_pairs={{0,3},{1,0},{2,1},{3,2},{4,7},{5,4},{6,5},{7,6},{8,11},{9,8},{10,9... | collective-permute-start | bytes 1572872 | tf_op jit(solution)/shard_map/ppermute | solution.py:422
  64.0 2.4 %copy-start.17 = (bf16[512,512]{1,0:T(8,128)(2,1)}, bf16[512,512]{1,0:T(8,128)(2,1)S(1)}, u32[]{:S(2)}) copy-start(bf16[512,512]{1,0:T(8,128)(2,1)S(1)} %collective-permute-done.8) | copy-start | bytes 1572868
  64.6 3.1 %copy-start.10 = (s32[1,8]{1,0:T(1,128)S(1)}, s32[1,8]{1,0:T(1,128)}, u32[]{:S(2)}) copy-start(s32[1,8]{1,0:T(1,128)} %count_ref.7) | copy-start | bytes 100
  64.6 3.1 %copy-start.14 = (s32[1,16]{1,0:T(1,128)S(1)}, s32[1,16]{1,0:T(1,128)}, u32[]{:S(2)}) copy-start(s32[1,16]{1,0:T(1,128)} %member_ref.3) | copy-start | bytes 196
  64.6 12.7 %collective-permute-start.10 = (bf16[1040,384]{1,0:T(8,128)(2,1)S(1)}, bf16[1040,384]{1,0:T(8,128)(2,1)}, u32[]{:S(2)}, u32[]{:S(2)}) collective-permute-start(bf16[1040,384]{1,0:T(8,128)(2,1)S(1)} %shard_map.105), channel_id=1, source_target_pairs={{0,12},{4,0},{8,4},{12,8},{16,20},{20,24},{24,28},{28,16},{1,13},{... | collective-permute-start | bytes 2396168 | tf_op jit(solution)/shard_map/ppermute | solution.py:445
  66.4 1.3 copy-start.2
  67.7 6.5 %copy-start.15 = (bf16[512,2048]{1,0:T(8,128)(2,1)}, bf16[512,2048]{1,0:T(8,128)(2,1)S(1)}, u32[]{:S(2)}) copy-start(bf16[512,2048]{1,0:T(8,128)(2,1)S(1)} %get-tuple-element.42.xn) | copy-start | bytes 6291460
  74.2 16.4 %copy-start.6 = (bf16[512,256]{1,0:T(8,128)(2,1)}, bf16[512,256]{1,0:T(8,128)(2,1)S(1)}, u32[]{:S(2)}) copy-start(bf16[512,256]{1,0:T(8,128)(2,1)S(1)} %shard_map.106.o0) | copy-start | bytes 786436
  77.3 6.4 %collective-permute-start.9 = (bf16[2064,384]{1,0:T(8,128)(2,1)S(1)}, bf16[2064,384]{1,0:T(8,128)(2,1)S(1)}, u32[]{:S(2)}, u32[]{:S(2)}) collective-permute-start(bf16[2064,384]{1,0:T(8,128)(2,1)S(1)} %collective-permute-done.6.got_ref.wq1), channel_id=1, source_target_pairs={{0,16},{16,0},{1,17},{17,1},{2,18},{18,2},{3,19},{19,3},{4,20},{20... | collective-permute-start | bytes 4755464 | tf_op jit(solution)/shard_map/ppermute | solution.py:443
  78.7 4.9 %collective-permute-start.11 = (bf16[1040,384]{1,0:T(8,128)(2,1)}, bf16[1040,384]{1,0:T(8,128)(2,1)S(1)}, u32[]{:S(2)}, u32[]{:S(2)}) collective-permute-start(bf16[1040,384]{1,0:T(8,128)(2,1)} %collective-permute-done.10.wqa), channel_id=1, source_target_pairs={{0,16},{16,0},{1,17},{17,1},{2,18},{18,2},{3,19},{19,3},{4,20},{20... | collective-permute-start | bytes 2396168 | tf_op jit(solution)/shard_map/ppermute | solution.py:459
  78.8 15.2 %collective-permute-start.15 = (bf16[512,256]{1,0:T(8,128)(2,1)S(1)}, bf16[512,256]{1,0:T(8,128)(2,1)S(1)}, u32[]{:S(2)}, u32[]{:S(2)}) collective-permute-start(bf16[512,256]{1,0:T(8,128)(2,1)S(1)} %shard_map.106.o0), channel_id=1, source_target_pairs={{0,1},{1,2},{2,3},{3,0},{4,5},{5,6},{6,7},{7,4},{8,9},{9,10},{10,1... | collective-permute-start | bytes 786440 | tf_op jit(solution)/shard_map/ppermute | solution.py:474
  80.1 15.2 %collective-permute-start.16 = (bf16[512,256]{1,0:T(8,128)(2,1)S(1)}, bf16[512,256]{1,0:T(8,128)(2,1)S(1)}, u32[]{:S(2)}, u32[]{:S(2)}) collective-permute-start(bf16[512,256]{1,0:T(8,128)(2,1)S(1)} %shard_map.106.o0), channel_id=1, source_target_pairs={{0,2},{1,3},{2,0},{3,1},{4,6},{5,7},{6,4},{7,5},{8,10},{9,11},{10,... | collective-permute-start | bytes 786440 | tf_op jit(solution)/shard_map/ppermute | solution.py:474
  82.5 12.7 %collective-permute-start.17 = (bf16[512,256]{1,0:T(8,128)(2,1)S(1)}, bf16[512,256]{1,0:T(8,128)(2,1)S(1)}, u32[]{:S(2)}, u32[]{:S(2)}) collective-permute-start(bf16[512,256]{1,0:T(8,128)(2,1)S(1)} %shard_map.106.o0), channel_id=1, source_target_pairs={{0,3},{1,0},{2,1},{3,2},{4,7},{5,4},{6,5},{7,6},{8,11},{9,8},{10,9... | collective-permute-start | bytes 786440 | tf_op jit(solution)/shard_map/ppermute | solution.py:474
  83.7 1.6 copy-start.16
  90.6 14.3 %copy-start.12 = (bf16[512,256]{1,0:T(8,128)(2,1)}, bf16[512,256]{1,0:T(8,128)(2,1)S(1)}, u32[]{:S(2)}) copy-start(bf16[512,256]{1,0:T(8,128)(2,1)S(1)} %shard_map.107.f0) | copy-start | bytes 786436
  90.6 14.4 %collective-permute-start.12 = (bf16[512,256]{1,0:T(8,128)(2,1)S(1)}, bf16[512,256]{1,0:T(8,128)(2,1)S(1)}, u32[]{:S(2)}, u32[]{:S(2)}) collective-permute-start(bf16[512,256]{1,0:T(8,128)(2,1)S(1)} %shard_map.107.f0), channel_id=1, source_target_pairs={{0,1},{1,2},{2,3},{3,0},{4,5},{5,6},{6,7},{7,4},{8,9},{9,10},{10,1... | collective-permute-start | bytes 786440 | tf_op jit(solution)/shard_map/ppermute | solution.py:475
  91.6 14.3 %collective-permute-start.13 = (bf16[512,256]{1,0:T(8,128)(2,1)S(1)}, bf16[512,256]{1,0:T(8,128)(2,1)S(1)}, u32[]{:S(2)}, u32[]{:S(2)}) collective-permute-start(bf16[512,256]{1,0:T(8,128)(2,1)S(1)} %shard_map.107.f0), channel_id=1, source_target_pairs={{0,2},{1,3},{2,0},{3,1},{4,6},{5,7},{6,4},{7,5},{8,10},{9,11},{10,... | collective-permute-start | bytes 786440 | tf_op jit(solution)/shard_map/ppermute | solution.py:475
  94.1 1.2 copy-start.18
  94.1 11.8 %collective-permute-start.14 = (bf16[512,256]{1,0:T(8,128)(2,1)S(1)}, bf16[512,256]{1,0:T(8,128)(2,1)S(1)}, u32[]{:S(2)}, u32[]{:S(2)}) collective-permute-start(bf16[512,256]{1,0:T(8,128)(2,1)S(1)} %shard_map.107.f0), channel_id=1, source_target_pairs={{0,3},{1,0},{2,1},{3,2},{4,7},{5,4},{6,5},{7,6},{8,11},{9,8},{10,9... | collective-permute-start | bytes 786440 | tf_op jit(solution)/shard_map/ppermute | solution.py:475
  95.2 0.8 copy-start.20
  105.0 0.9 copy-start.21
  105.9 0.8 copy-start.23
  130.9 34.7 %copy-start.8 = (s32[4]{0:T(128)S(1)}, s32[4]{0:T(128)}, u32[]{:S(2)}) copy-start(s32[4]{0:T(128)} %copy-done.7) | copy-start | bytes 52
  166.8 9.7 %collective-permute-start.18 = (bf16[24,2048]{1,0:T(8,128)(2,1)S(1)}, bf16[24,2048]{1,0:T(8,128)(2,1)S(1)}, u32[]{:S(2)}, u32[]{:S(2)}) collective-permute-start(bf16[24,2048]{1,0:T(8,128)(2,1)S(1)} %get-tuple-element.54), channel_id=1, source_target_pairs={{0,16},{16,32},{32,48},{48,64},{64,80},{80,96},{96,112},{112,0},{1... | collective-permute-start | bytes 294920 | tf_op jit(solution)/shard_map/ppermute | solution.py:523
  170.3 7.0 %collective-permute-start.19 = (bf16[24,2048]{1,0:T(8,128)(2,1)S(1)}, bf16[24,2048]{1,0:T(8,128)(2,1)S(1)}, u32[]{:S(2)}, u32[]{:S(2)}) collective-permute-start(bf16[24,2048]{1,0:T(8,128)(2,1)S(1)} %get-tuple-element.55), channel_id=1, source_target_pairs={{0,32},{16,48},{32,64},{48,80},{64,96},{80,112},{96,0},{112,16},{1... | collective-permute-start | bytes 294920 | tf_op jit(solution)/shard_map/ppermute | solution.py:523
  172.1 6.4 %collective-permute-start.20 = (bf16[24,2048]{1,0:T(8,128)(2,1)S(1)}, bf16[24,2048]{1,0:T(8,128)(2,1)S(1)}, u32[]{:S(2)}, u32[]{:S(2)}) collective-permute-start(bf16[24,2048]{1,0:T(8,128)(2,1)S(1)} %get-tuple-element.56), channel_id=1, source_target_pairs={{0,48},{16,64},{32,80},{48,96},{64,112},{80,0},{96,16},{112,32},{1... | collective-permute-start | bytes 294920 | tf_op jit(solution)/shard_map/ppermute | solution.py:523
  174.2 8.4 %collective-permute-start.21 = (bf16[24,2048]{1,0:T(8,128)(2,1)S(1)}, bf16[24,2048]{1,0:T(8,128)(2,1)S(1)}, u32[]{:S(2)}, u32[]{:S(2)}) collective-permute-start(bf16[24,2048]{1,0:T(8,128)(2,1)S(1)} %get-tuple-element.57), channel_id=1, source_target_pairs={{0,64},{16,80},{32,96},{48,112},{64,0},{80,16},{96,32},{112,48},{1... | collective-permute-start | bytes 294920 | tf_op jit(solution)/shard_map/ppermute | solution.py:523
  174.2 9.0 %collective-permute-start.22 = (bf16[24,2048]{1,0:T(8,128)(2,1)S(1)}, bf16[24,2048]{1,0:T(8,128)(2,1)S(1)}, u32[]{:S(2)}, u32[]{:S(2)}) collective-permute-start(bf16[24,2048]{1,0:T(8,128)(2,1)S(1)} %get-tuple-element.58), channel_id=1, source_target_pairs={{0,80},{16,96},{32,112},{48,0},{64,16},{80,32},{96,48},{112,64},{1... | collective-permute-start | bytes 294920 | tf_op jit(solution)/shard_map/ppermute | solution.py:523
  176.5 6.7 %collective-permute-start.23 = (bf16[24,2048]{1,0:T(8,128)(2,1)S(1)}, bf16[24,2048]{1,0:T(8,128)(2,1)S(1)}, u32[]{:S(2)}, u32[]{:S(2)}) collective-permute-start(bf16[24,2048]{1,0:T(8,128)(2,1)S(1)} %get-tuple-element.59), channel_id=1, source_target_pairs={{0,96},{16,112},{32,0},{48,16},{64,32},{80,48},{96,64},{112,80},{1... | collective-permute-start | bytes 294920 | tf_op jit(solution)/shard_map/ppermute | solution.py:523
  177.3 6.4 %collective-permute-start.24 = (bf16[24,2048]{1,0:T(8,128)(2,1)S(1)}, bf16[24,2048]{1,0:T(8,128)(2,1)S(1)}, u32[]{:S(2)}, u32[]{:S(2)}) collective-permute-start(bf16[24,2048]{1,0:T(8,128)(2,1)S(1)} %get-tuple-element.60), channel_id=1, source_target_pairs={{0,112},{16,0},{32,16},{48,32},{64,48},{80,64},{96,80},{112,96},{1... | collective-permute-start | bytes 294920 | tf_op jit(solution)/shard_map/ppermute | solution.py:523
  (3 other events, 2.1 us)
Sparse Core Ops, SparseCore 0:
  35.1 52.4 all-gather.4
  89.3 32.3 all-gather.6
